TPU v7x, 256 devices: a whole 4x4x8 slice. The times are simulated.
256 devices in a mesh: batch: 2 (over y_hi), tm: 16 (over z, y_lo), height: 8 (over x, core).
Axes of the slice: x: 4, y: 4 (y_hi: 2, y_lo: 2; y = y_hi * 2 + y_lo), z: 8, core: 2. Of those that a mesh axis runs over, the one named last changes fastest.
Arguments:
- features: bfloat16 [2, 32, 64, 128, 128], P('batch', 'tm', 'height'), may hold values from -6 to 6
- w_spatial: bfloat16 [3, 3, 128, 128], replicated, may hold values from -0.1875 to 0.1875
- w_temporal: bfloat16 [3, 128, 128], replicated, may hold values from -0.3125 to 0.3125
- w_down: bfloat16 [3, 128, 128], replicated, may hold values from -0.3125 to 0.3125
- cotangent: bfloat16 [2, 16, 64, 128, 128], P('batch', 'tm', 'height'), may hold values from -40 to 40
Outputs:
- downsampled: bfloat16 [2, 16, 64, 128, 128], P('batch', 'tm', 'height')
- grad_features: bfloat16 [2, 32, 64, 128, 128], P('batch', 'tm', 'height')
- grad_spatial: float32 [3, 3, 128, 128], replicated
- grad_temporal: float32 [3, 128, 128], replicated
- grad_down: float32 [3, 128, 128], replicated
All inputs are finite; a program needn't handle non-finite values.
Results may differ from a plain program's by a relative error of at most 0.0052.
Values may be sent and summed in bfloat16 or wider, within the bound.
No kernel may reach another device: no remote copies, remote signals or barrier semaphores. Data moves between devices by JAX's collectives and lax.ppermute only.
A program may use at most 64 MiB of HBM per device.

v0:
```python
import jax
import jax.numpy as jnp
from jax import lax
from jax.sharding import PartitionSpec as P


def with_halo(block, sides, width):
    for axis, dim in sides:
        count = lax.axis_size(axis)
        forward = [(i, i + 1) for i in range(count - 1)]
        backward = [(target, source) for source, target in forward]
        low = lax.ppermute(
            lax.slice_in_dim(block, block.shape[dim] - width, None, axis=dim), axis, forward
        )
        high = lax.ppermute(lax.slice_in_dim(block, 0, width, axis=dim), axis, backward)
        block = jnp.concatenate([low, block, high], axis=dim)
    return block


def from_behind(shard, axis, by):
    count = lax.axis_size(axis)
    pairs = [(i, i + by) for i in range(count) if 0 <= i + by < count]
    return lax.ppermute(shard, axis, pairs)


def spatial(padded, kernel):
    rows = padded.shape[2] - 2
    cols = padded.shape[3]
    wide = jnp.pad(padded, ((0, 0), (0, 0), (0, 0), (1, 1), (0, 0)))
    total = jnp.zeros(padded.shape[:2] + (rows, cols, kernel.shape[3]), jnp.float32)
    for dy in range(3):
        for dx in range(3):
            total = total + jnp.einsum(
                "bfhwc,cd->bfhwd",
                wide[:, :, dy : dy + rows, dx : dx + cols],
                kernel[dy, dx],
                preferred_element_type=jnp.float32,
            )
    return total


def spatial_grad(padded, grad):
    rows = grad.shape[2]
    cols = grad.shape[3]
    wide = jnp.pad(padded, ((0, 0), (0, 0), (0, 0), (1, 1), (0, 0)))
    taps = []
    for dy in range(3):
        for dx in range(3):
            taps.append(
                jnp.einsum(
                    "bfhwc,bfhwd->cd",
                    wide[:, :, dy : dy + rows, dx : dx + cols],
                    grad,
                    preferred_element_type=jnp.float32,
                )
            )
    return jnp.stack(taps).reshape(3, 3, grad.shape[4], grad.shape[4])


def temporal(padded, kernel):
    frames = padded.shape[1] - 2
    total = jnp.zeros(
        padded.shape[:1] + (frames,) + padded.shape[2:4] + (kernel.shape[2],), jnp.float32
    )
    for k in range(3):
        total = total + jnp.einsum(
            "bfhwc,cd->bfhwd",
            padded[:, k : k + frames],
            kernel[k],
            preferred_element_type=jnp.float32,
        )
    return total


def per_device(features, w_spatial, w_temporal, w_down, cotangent):
    frames = features.shape[1]
    half = cotangent.shape[1]
    xpad = with_halo(features, (("height", 2),), 1)
    pre = spatial(xpad, w_spatial)
    act = jax.nn.silu(pre).astype(jnp.bfloat16)
    act_pad = with_halo(act, (("tm", 1),), 1)
    mixed = temporal(act_pad, w_temporal)
    resid = (features.astype(jnp.float32) + mixed).astype(jnp.bfloat16)
    before = from_behind(resid[:, -1:], "tm", 1)
    rpad = jnp.concatenate([before, resid], axis=1)
    down = jnp.zeros(cotangent.shape, jnp.float32)
    grad_down = []
    for k in range(3):
        picked = rpad[:, k : k + 2 * half : 2]
        down = down + jnp.einsum(
            "bfhwc,cd->bfhwd", picked, w_down[k], preferred_element_type=jnp.float32
        )
        grad_down.append(
            jnp.einsum("bfhwc,bfhwd->cd", picked, cotangent, preferred_element_type=jnp.float32)
        )
    grad_down = jnp.stack(grad_down)
    downsampled = down.astype(jnp.bfloat16)
    after = from_behind(cotangent, "tm", -1)
    gnext = jnp.concatenate([cotangent[:, 1:], after], axis=1)
    even = jnp.einsum("bfhwd,cd->bfhwc", cotangent, w_down[1], preferred_element_type=jnp.float32)
    odd = jnp.einsum("bfhwd,cd->bfhwc", cotangent, w_down[2], preferred_element_type=jnp.float32)
    odd = odd + jnp.einsum("bfhwd,cd->bfhwc", gnext, w_down[0], preferred_element_type=jnp.float32)
    g_resid = jnp.stack([even, odd], axis=2).reshape(features.shape)
    g_resid_b = g_resid.astype(jnp.bfloat16)
    gpad = with_halo(g_resid_b, (("tm", 1),), 1)
    flip_t = jnp.transpose(w_temporal[::-1], (0, 2, 1))
    g_act = temporal(gpad, flip_t)
    grad_temporal = jnp.stack(
        [
            jnp.einsum(
                "bfhwc,bfhwd->cd",
                act_pad[:, k : k + frames],
                g_resid_b,
                preferred_element_type=jnp.float32,
            )
            for k in range(3)
        ]
    )
    sig = jax.nn.sigmoid(pre)
    g_pre = (g_act * sig * (1.0 + pre * (1.0 - sig))).astype(jnp.bfloat16)
    grad_spatial = spatial_grad(xpad, g_pre)
    g_prepad = with_halo(g_pre, (("height", 2),), 1)
    flip_s = jnp.transpose(w_spatial[::-1, ::-1], (0, 1, 3, 2))
    grad_features = (g_resid + spatial(g_prepad, flip_s)).astype(jnp.bfloat16)
    grad_spatial, grad_temporal, grad_down = lax.psum(
        (grad_spatial, grad_temporal, grad_down), ("batch", "tm", "height")
    )
    return (downsampled, grad_features, grad_spatial, grad_temporal, grad_down)


def solution(mesh):
    placed = (
        P("batch", "tm", "height", None, None),
        P(),
        P(),
        P(),
        P("batch", "tm", "height", None, None),
    )
    return jax.shard_map(
        per_device,
        mesh=mesh,
        in_specs=placed,
        out_specs=(
            P("batch", "tm", "height", None, None),
            P("batch", "tm", "height", None, None),
            P(),
            P(),
            P(),
        ),
        check_vma=False,
    )
```

profile of v0, /device:TPU:1, one launch (start us, length us, event | category | flops | bytes accessed | tf_op | source)
XLA Modules:
  0.0 338.1 jit_solution(5406410502677556433)
XLA Ops:
  7.2 0.9 fusion.130
  8.2 4.5 %collective-permute-start = (bf16[1,2,1,128,128]{4,3,2,1,0:T(8,128)(2,1)S(1)}, bf16[1,2,1,128,128]{4,3,2,1,0:T(8,128)(2,1)S(1)}, u32[]{:S(2)}, u32[]{:S(2)}) collective-permute-start(bf16[1,2,1,128,128]{4,3,2,1,0:T(8,128)(2,1)S(1)} %get-tuple-element.14), channel_id=1, source_target_pairs={{0,1},{1,2},{2,3},{3,4},{4,5},{5,6},{6,7},{8,9},{9,10},{10,11},{11... | collective-permute-start | bytes 196616 | tf_op jit(solution)/shard_map/ppermute | solution.py:12
  12.7 2.1 collective-permute-start.1
  14.8 1.3 collective-permute-start.5
  16.1 1.2 fusion.60
  17.5 0.7 convert_bitcast_fusion.1
  19.2 0.3 fusion.51
  19.5 0.3 convolution_add_fusion.15
  19.8 0.3 convolution_add_fusion.14
  20.1 0.3 convolution_add_fusion.13
  20.4 0.3 convolution_add_fusion.12
  20.7 0.3 convolution_add_fusion.11
  21.3 0.5 multiply_convert_fusion
  21.8 1.3 collective-permute-start.3
  23.1 4.6 %collective-permute-start.2 = (bf16[1,1,8,128,128]{4,3,2,1,0:T(8,128)(2,1)S(1)}, bf16[1,1,8,128,128]{4,3,2,1,0:T(8,128)(2,1)S(1)}, u32[]{:S(2)}, u32[]{:S(2)}) collective-permute-start(bf16[1,1,8,128,128]{4,3,2,1,0:T(8,128)(2,1)S(1)} %get-tuple-element.12), channel_id=1, source_target_pairs={{0,8},{8,16},{16,24},{24,32},{32,40},{40,48},{48,56},{56,64},{64,7... | collective-permute-start | bytes 786440 | tf_op jit(solution)/shard_map/ppermute | solution.py:12
  27.7 0.3 fusion.77
  28.0 1.2 convolution_add_fusion.16
  29.3 0.8 copy-done.4
  30.2 0.3 fusion.75
  30.5 0.3 convolution_bitcast_fusion.1
  30.8 1.3 collective-permute-start.7
  32.1 4.9 %collective-permute-start.6 = (bf16[1,1,8,128,128]{4,3,2,1,0:T(8,128)(2,1)S(1)}, bf16[1,1,8,128,128]{4,3,2,1,0:T(8,128)(2,1)S(1)}, u32[]{:S(2)}, u32[]{:S(2)}) collective-permute-start(bf16[1,1,8,128,128]{4,3,2,1,0:T(8,128)(2,1)S(1)} %get-tuple-element.10), channel_id=1, source_target_pairs={{0,8},{8,16},{16,24},{24,32},{32,40},{40,48},{48,56},{56,64},{64,7... | collective-permute-start | bytes 786440 | tf_op jit(solution)/shard_map/ppermute | solution.py:12
  37.0 0.3 fusion.73
  37.3 6.7 %collective-permute-done.2 = bf16[1,1,8,128,128]{4,3,2,1,0:T(8,128)(2,1)S(1)} collective-permute-done((bf16[1,1,8,128,128]{4,3,2,1,0:T(8,128)(2,1)S(1)}, bf16[1,1,8,128,128]{4,3,2,1,0:T(8,128)(2,1)S(1)}, u32[]{:S(2)}, u32[]{:S(2)}) %collective-permute-start.2) | collective-permute-done | bytes 262176 | tf_op jit(solution)/shard_map/ppermute | solution.py:12
  44.0 0.3 fusion.11
  44.4 0.3 convolution_bitcast_fusion.12
  44.9 1.0 fusion.69
  45.9 4.1 %collective-permute-start.4 = (bf16[1,1,8,128,128]{4,3,2,1,0:T(8,128)(2,1)S(1)}, bf16[1,1,8,128,128]{4,3,2,1,0:T(8,128)(2,1)S(1)}, u32[]{:S(2)}, u32[]{:S(2)}) collective-permute-start(bf16[1,1,8,128,128]{4,3,2,1,0:T(8,128)(2,1)S(1)} %slice.271), channel_id=1, source_target_pairs={{0,8},{8,16},{16,24},{24,32},{32,40},{40,48},{48,56},{56,64},{64,7... | collective-permute-start | bytes 786440 | tf_op jit(solution)/shard_map/ppermute | solution.py:23
  50.0 0.4 convolution_bitcast_fusion
  50.4 0.3 convolution_bitcast_fusion.2
  50.7 0.3 convolution_bitcast_fusion.13
  51.0 0.7 pad_maximum_fusion.10
  51.7 0.3 fusion.38
  52.0 0.6 fusion.10
  52.6 0.3 fusion.25
  52.9 0.3 fusion.24
  53.3 0.3 fusion.23
  53.6 0.3 fusion.22
  54.0 0.4 fusion.21
  54.3 0.3 fusion.20
  54.7 0.3 fusion.19
  55.1 3.8 %collective-permute-start.8 = (bf16[1,2,1,128,128]{4,3,2,1,0:T(8,128)(2,1)S(1)}, bf16[1,2,1,128,128]{4,3,2,1,0:T(8,128)(2,1)S(1)}, u32[]{:S(2)}, u32[]{:S(2)}) collective-permute-start(bf16[1,2,1,128,128]{4,3,2,1,0:T(8,128)(2,1)S(1)} %get-tuple-element.8), channel_id=1, source_target_pairs={{0,1},{1,2},{2,3},{3,4},{4,5},{5,6},{6,7},{8,9},{9,10},{10,11},{11... | collective-permute-start | bytes 196616 | tf_op jit(solution)/shard_map/ppermute | solution.py:12
  58.8 2.1 collective-permute-start.9
  61.0 0.3 fusion.18
  61.3 0.3 fusion.17
  61.7 2.7 collective-permute-done.9
  64.6 0.3 fusion.36
  64.9 0.3 convolution_add_fusion.6
  65.2 0.3 convolution_add_fusion.5
  65.5 0.3 convolution_add_fusion.4
  65.8 0.3 convolution_add_fusion.3
  66.1 0.3 convolution_add_fusion.2
  66.4 1.3 convolution_add_fusion.1
  67.9 0.4 copy-done.5
  68.3 0.7 pad_maximum_fusion.11
  69.1 0.9 copy-done.6
  70.0 2.0 fusion.16
  71.9 0.3 fusion.29
  72.3 0.9 copy-done.2
  73.2 1.1 fusion.13
  74.3 253.6 %all-reduce.5.cloned.1.call-done = (f32[3,3,128,128]{3,2,1,0:T(8,128)}, f32[3,128,128]{2,1,0:T(8,128)}, f32[3,128,128]{2,1,0:T(8,128)}) async-done(((f32[3,3,128,128]{3,2,1,0:T(8,128)}, f32[3,128,128]{2,1,0:T(8,128)}, f32[3,128,128]{2,1,0:T(8,128)}), (f32[3,3,128,128]{3,2,1,0:T(8,128)}, f32[3,128,128]{2,1,0:T(8,128)}, f32[3,128,128]{2,1,0:T(8,128)})) %all-reduce.5.cloned.1.call-update) | async-done | bytes 983056 | tf_op jit(solution)/shard_map/psum | solution.py:125
  327.9 2.0 copy.91
  329.9 0.7 copy.92
  330.5 0.7 copy.93
  (51 shorter events, 2.4 us)
Async XLA Ops:
  7.2 10.1 %copy-start.1 = (bf16[1,1,8,128,128]{4,3,2,1,0:T(8,128)(2,1)S(1)}, bf16[1,1,8,128,128]{4,3,2,1,0:T(8,128)(2,1)}, u32[]{:S(2)}) copy-start(bf16[1,1,8,128,128]{4,3,2,1,0:T(8,128)(2,1)} %param.9) | copy-start | bytes 786436
  7.2 10.1 %copy-start.9 = (bf16[3,128,128]{2,1,0:T(8,128)(2,1)S(1)}, bf16[3,128,128]{2,1,0:T(8,128)(2,1)}, u32[]{:S(2)}) copy-start(bf16[3,128,128]{2,1,0:T(8,128)(2,1)} %param.8) | copy-start | bytes 294916
  7.2 320.7 %all-reduce.5.cloned.1.call-start = ((), (), s32[]{:S(2)}) async-start(), calls=%async_computation | async-start | bytes 1966080 | tf_op jit(solution)/shard_map/psum | solution.py:125
  8.2 10.5 %collective-permute-start = (bf16[1,2,1,128,128]{4,3,2,1,0:T(8,128)(2,1)S(1)}, bf16[1,2,1,128,128]{4,3,2,1,0:T(8,128)(2,1)S(1)}, u32[]{:S(2)}, u32[]{:S(2)}) collective-permute-start(bf16[1,2,1,128,128]{4,3,2,1,0:T(8,128)(2,1)S(1)} %get-tuple-element.14), channel_id=1, source_target_pairs={{0,1},{1,2},{2,3},{3,4},{4,5},{5,6},{6,7},{8,9},{9,10},{10,11},{11... | collective-permute-start | bytes 196616 | tf_op jit(solution)/shard_map/ppermute | solution.py:12
  12.7 5.6 %copy-start.8 = (bf16[3,128,128]{2,1,0:T(8,128)(2,1)S(1)}, bf16[3,128,128]{2,1,0:T(8,128)(2,1)}, u32[]{:S(2)}) copy-start(bf16[3,128,128]{2,1,0:T(8,128)(2,1)} %param.7) | copy-start | bytes 294916
  12.7 6.0 %collective-permute-start.1 = (bf16[1,2,1,128,128]{4,3,2,1,0:T(8,128)(2,1)S(1)}, bf16[1,2,1,128,128]{4,3,2,1,0:T(8,128)(2,1)S(1)}, u32[]{:S(2)}, u32[]{:S(2)}) collective-permute-start(bf16[1,2,1,128,128]{4,3,2,1,0:T(8,128)(2,1)S(1)} %get-tuple-element.15), channel_id=1, source_target_pairs={{1,0},{2,1},{3,2},{4,3},{5,4},{6,5},{7,6},{9,8},{10,9},{11,10},{12... | collective-permute-start | bytes 196616 | tf_op jit(solution)/shard_map/ppermute | solution.py:15
  14.8 13.2 %collective-permute-start.5 = (bf16[1,1,8,128,128]{4,3,2,1,0:T(8,128)(2,1)}, bf16[1,1,8,128,128]{4,3,2,1,0:T(8,128)(2,1)}, u32[]{:S(2)}, u32[]{:S(2)}) collective-permute-start(bf16[1,1,8,128,128]{4,3,2,1,0:T(8,128)(2,1)} %param.9), channel_id=1, source_target_pairs={{8,0},{16,8},{24,16},{32,24},{40,32},{48,40},{56,48},{64,56},{72,6... | collective-permute-start | bytes 786440 | tf_op jit(solution)/shard_map/ppermute | solution.py:23
  17.3 1.1 copy-start.3
  17.5 1.2 copy-start
  18.7 2.5 copy-start.12
  21.8 15.2 %collective-permute-start.3 = (bf16[1,1,8,128,128]{4,3,2,1,0:T(8,128)(2,1)S(1)}, bf16[1,1,8,128,128]{4,3,2,1,0:T(8,128)(2,1)S(1)}, u32[]{:S(2)}, u32[]{:S(2)}) collective-permute-start(bf16[1,1,8,128,128]{4,3,2,1,0:T(8,128)(2,1)S(1)} %get-tuple-element.13), channel_id=1, source_target_pairs={{8,0},{16,8},{24,16},{32,24},{40,32},{48,40},{56,48},{64,56},{72,6... | collective-permute-start | bytes 786440 | tf_op jit(solution)/shard_map/ppermute | solution.py:15
  23.1 20.9 %collective-permute-start.2 = (bf16[1,1,8,128,128]{4,3,2,1,0:T(8,128)(2,1)S(1)}, bf16[1,1,8,128,128]{4,3,2,1,0:T(8,128)(2,1)S(1)}, u32[]{:S(2)}, u32[]{:S(2)}) collective-permute-start(bf16[1,1,8,128,128]{4,3,2,1,0:T(8,128)(2,1)S(1)} %get-tuple-element.12), channel_id=1, source_target_pairs={{0,8},{8,16},{16,24},{24,32},{32,40},{40,48},{48,56},{56,64},{64,7... | collective-permute-start | bytes 786440 | tf_op jit(solution)/shard_map/ppermute | solution.py:12
  29.2 1.0 copy-start.4
  30.8 20.9 %collective-permute-start.7 = (bf16[1,1,8,128,128]{4,3,2,1,0:T(8,128)(2,1)S(1)}, bf16[1,1,8,128,128]{4,3,2,1,0:T(8,128)(2,1)S(1)}, u32[]{:S(2)}, u32[]{:S(2)}) collective-permute-start(bf16[1,1,8,128,128]{4,3,2,1,0:T(8,128)(2,1)S(1)} %get-tuple-element.11), channel_id=1, source_target_pairs={{8,0},{16,8},{24,16},{32,24},{40,32},{48,40},{56,48},{64,56},{72,6... | collective-permute-start | bytes 786440 | tf_op jit(solution)/shard_map/ppermute | solution.py:15
  32.1 19.9 %collective-permute-start.6 = (bf16[1,1,8,128,128]{4,3,2,1,0:T(8,128)(2,1)S(1)}, bf16[1,1,8,128,128]{4,3,2,1,0:T(8,128)(2,1)S(1)}, u32[]{:S(2)}, u32[]{:S(2)}) collective-permute-start(bf16[1,1,8,128,128]{4,3,2,1,0:T(8,128)(2,1)S(1)} %get-tuple-element.10), channel_id=1, source_target_pairs={{0,8},{8,16},{16,24},{24,32},{32,40},{40,48},{48,56},{56,64},{64,7... | collective-permute-start | bytes 786440 | tf_op jit(solution)/shard_map/ppermute | solution.py:12
  45.9 21.7 %collective-permute-start.4 = (bf16[1,1,8,128,128]{4,3,2,1,0:T(8,128)(2,1)S(1)}, bf16[1,1,8,128,128]{4,3,2,1,0:T(8,128)(2,1)S(1)}, u32[]{:S(2)}, u32[]{:S(2)}) collective-permute-start(bf16[1,1,8,128,128]{4,3,2,1,0:T(8,128)(2,1)S(1)} %slice.271), channel_id=1, source_target_pairs={{0,8},{8,16},{16,24},{24,32},{32,40},{40,48},{48,56},{56,64},{64,7... | collective-permute-start | bytes 786440 | tf_op jit(solution)/shard_map/ppermute | solution.py:23
  54.7 6.3 %copy-start.13 = (bf16[1,2,1,128,128]{4,3,2,1,0:T(8,128)(2,1)S(1)}, bf16[1,2,1,128,128]{4,3,2,1,0:T(8,128)(2,1)}, u32[]{:S(2)}) copy-start(bf16[1,2,1,128,128]{4,3,2,1,0:T(8,128)(2,1)} %copy-done.12) | copy-start | bytes 196612
  55.1 6.6 %collective-permute-start.8 = (bf16[1,2,1,128,128]{4,3,2,1,0:T(8,128)(2,1)S(1)}, bf16[1,2,1,128,128]{4,3,2,1,0:T(8,128)(2,1)S(1)}, u32[]{:S(2)}, u32[]{:S(2)}) collective-permute-start(bf16[1,2,1,128,128]{4,3,2,1,0:T(8,128)(2,1)S(1)} %get-tuple-element.8), channel_id=1, source_target_pairs={{0,1},{1,2},{2,3},{3,4},{4,5},{5,6},{6,7},{8,9},{9,10},{10,11},{11... | collective-permute-start | bytes 196616 | tf_op jit(solution)/shard_map/ppermute | solution.py:12
  58.8 5.6 %collective-permute-start.9 = (bf16[1,2,1,128,128]{4,3,2,1,0:T(8,128)(2,1)S(1)}, bf16[1,2,1,128,128]{4,3,2,1,0:T(8,128)(2,1)S(1)}, u32[]{:S(2)}, u32[]{:S(2)}) collective-permute-start(bf16[1,2,1,128,128]{4,3,2,1,0:T(8,128)(2,1)S(1)} %get-tuple-element.9), channel_id=1, source_target_pairs={{1,0},{2,1},{3,2},{4,3},{5,4},{6,5},{7,6},{9,8},{10,9},{11,10},{12... | collective-permute-start | bytes 196616 | tf_op jit(solution)/shard_map/ppermute | solution.py:15
  61.7 3.3 copy-start.7
  67.6 0.7 copy-start.5
  69.0 0.9 copy-start.6
  71.9 1.2 copy-start.2
  327.9 2.0 copy-start.11
  327.9 2.7 copy-start.10
Sparse Core Ops, SparseCore 0:
  69.2 258.6 all-reduce.4
where the time goes:
time: 340 us; the launch traced here: 338 us
  waiting for transfers between devices  263 us (77%)
  starting transfers between devices  30 us (9%)
  matrix products  19.9 us (6%)
  between operations  14.6 us (4%)
  local copies, waits for them, and re-layouts  7.92 us (2%)
    psum x1, waiting for transfers between devices, per_device(): lax.psum((grad_spatial, grad_temporal, grad_down), ('batch', 'tm', 'heigh...  254 us
    ppermute x4, starting transfers between devices, with_halo(): lax.ppermute(lax.slice_in_dim(block, block.shape[dim] - width, None, axis...  17.8 us
    dot_general x18, matrix products, spatial(): jnp.einsum('bfhwc,cd->bfhwd', wide[:, :, dy:dy + rows, dx:dx + cols], ker...  7.14 us
    unnamed x33, local copies, waits for them, and re-layouts  6.83 us
  transfers between devices with their start and end apart: 11, of which 3 were waited for; matrix products, arithmetic and copies ran while one was open for 7% of the time, Pallas kernels for 0%

commit v1 on v0

v1 whole, which is shorter than its diff:
```python
import jax
import jax.numpy as jnp
from jax import lax
from jax.experimental import pallas as pl
from jax.experimental.pallas import tpu as pltpu
from jax.sharding import Mesh, PartitionSpec as P

F32, BF16 = jnp.float32, jnp.bfloat16
C = 128
PLANE = ("yh", "yl", "x")


def mm(a, b):
    return lax.dot_general(a, b, (((1,), (0,)), ((), ())), preferred_element_type=F32)


def mm_nt(a, b):
    return lax.dot_general(a, b, (((1,), (1,)), ((), ())), preferred_element_type=F32)


def mm_tn(a, b):
    return lax.dot_general(a, b, (((0,), (0,)), ((), ())), preferred_element_type=F32)


def columns(x):
    wide = x.astype(F32)
    count = wide.shape[0]
    col = lax.broadcasted_iota(jnp.int32, wide.shape, 0) % 128
    before = jnp.where(col == 0, 0.0, pltpu.roll(wide, 1, 0)).astype(BF16)
    after = jnp.where(col == 127, 0.0, pltpu.roll(wide, count - 1, 0)).astype(BF16)
    return before, x, after


def row_pairs(cat):
    depth = cat.shape[1]
    rows = cat.reshape(5, 2, 128, depth)
    even, odd = rows[:, 0], rows[:, 1]
    parts = [even[0:4], odd[0:4], even[1:5], odd[1:5]]
    return jnp.concatenate([p.reshape(512, depth) for p in parts], axis=1)


def forward_kernel(x_ref, lo_ref, hi_ref, w_ref, slope_ref, act_ref, xt_ref, at_ref, wide_ref):
    wide_ref[...] = jnp.zeros_like(wide_ref)
    for out in range(2):
        for dy in range(3):
            for dx in range(3):
                start = ((dy + out) * 3 + dx) * C
                wide_ref[start : start + C, out * C : (out + 1) * C] = w_ref[dy, dx]
    for f in range(2):
        x = jnp.concatenate([lo_ref[f], x_ref[f], hi_ref[f]], axis=0).reshape(1280, C)
        xt_ref[f] = x.T
        pre = mm(row_pairs(jnp.concatenate(columns(x), axis=1)), wide_ref[...])
        sig = 1.0 / (1.0 + jnp.exp(-pre))
        act = (pre * sig).astype(BF16)
        slope = sig * (1.0 + pre * (1.0 - sig))
        for out in range(2):
            part = slice(out * C, (out + 1) * C)
            act_ref[f, :, out] = act[:, part].reshape(4, 128, C)
            slope_ref[f, :, out] = slope[:, part].reshape(4, 128, C)
        at_ref[f] = act_ref[f].reshape(1024, C).T


def grads_kernel(
    place_ref, slope_ref, xt_ref, at_ref, cot_ref, prev_ref, next_ref, wt_ref, wd_ref,
    gpre_ref, send_ref, keep_ref, mats_ref,
):
    first = place_ref[0] == 0
    core = place_ref[1]
    cot, before, after = (r[...].reshape(1024, C) for r in (cot_ref, prev_ref, next_ref))
    zero = jnp.zeros((C, C), BF16)
    w_pair = jnp.concatenate(
        [
            jnp.concatenate([wd_ref[2], wd_ref[0]], axis=1),
            jnp.concatenate([zero, wd_ref[1]], axis=1),
        ],
        axis=0,
    )
    low = mm_nt(jnp.concatenate([before, cot], axis=1), w_pair).astype(BF16)
    high = mm_nt(jnp.concatenate([cot, after], axis=1), w_pair).astype(BF16)
    g_m1 = jnp.where(first, jnp.zeros_like(low[:, :C]), low[:, :C])
    g_0, g_1, g_2 = low[:, C:], high[:, :C], high[:, C:]
    w_time = jnp.concatenate(
        [
            jnp.concatenate([wt_ref[2], wt_ref[1], wt_ref[0], zero], axis=1),
            jnp.concatenate([zero, wt_ref[2], wt_ref[1], wt_ref[0]], axis=1),
        ],
        axis=0,
    )
    g_act = mm_nt(jnp.concatenate([g_m1, g_0, g_1, g_2], axis=1), w_time)
    spatial = None
    for f in range(2):
        gp = (g_act[:, f * C : (f + 1) * C] * slope_ref[f].reshape(1024, C)).astype(BF16)
        gpre_ref[f] = gp.reshape(8, 128, C)
        behind, here, ahead = columns(gp)
        shifted = jnp.concatenate([ahead, here, behind], axis=1)
        xt = jnp.concatenate([xt_ref[f, :, dy * 128 : dy * 128 + 1024] for dy in range(3)], axis=0)
        term = mm(xt, shifted)
        spatial = term if spatial is None else spatial + term
    for dy in range(3):
        for dx in range(3):
            mats_ref[dy * 3 + dx] = spatial[dy * C : (dy + 1) * C, dx * C : (dx + 1) * C].reshape(2, 64, C)
    a0, a1 = at_ref[0], at_ref[1]
    x0, x1 = xt_ref[0, :, 128:1152], xt_ref[1, :, 128:1152]
    time = mm(a0, jnp.concatenate([g_1, g_0, g_m1], axis=1))
    time = time + mm(a1, jnp.concatenate([g_2, g_1, g_0], axis=1))
    for k in range(3):
        mats_ref[9 + k] = time[:, k * C : (k + 1) * C].reshape(2, 64, C)
    both = mm(
        jnp.concatenate([a0, a1, x0, x1], axis=0), jnp.concatenate([cot, after], axis=1)
    )
    tail = mm(a0, before)
    m_0, m_1 = both[0:128, :C], both[128:256, :C]
    m_m2, m_m1 = both[0:128, C:], both[128:256, C:]
    skip = jnp.where(first, jnp.zeros_like(m_0), m_0)
    kinds = (
        (both[384:512, C:], (m_m2, m_m1, skip)),
        (both[256:384, :C], (m_m1, m_0, m_1)),
        (both[384:512, :C], (m_0, m_1, tail)),
    )
    for k, (base, terms) in enumerate(kinds):
        total = base
        for tap, m in enumerate(terms):
            top = m.astype(BF16)
            rest = (m - top.astype(F32)).astype(BF16)
            total = total + mm_tn(wt_ref[tap], top) + mm_tn(wt_ref[tap], rest)
        mats_ref[12 + k] = total.reshape(2, 64, C)
    send_ref[...] = mats_ref[:, 1 - core].astype(BF16)
    keep_ref[...] = mats_ref[:, core]


def resid_kernel(x_ref, act_ref, prev_ref, next_ref, wt_ref, resid_ref):
    zero = jnp.zeros((C, C), BF16)
    w_time = jnp.concatenate(
        [
            jnp.concatenate([wt_ref[0], wt_ref[1], wt_ref[2], zero], axis=0),
            jnp.concatenate([zero, wt_ref[0], wt_ref[1], wt_ref[2]], axis=0),
        ],
        axis=1,
    )
    parts = [prev_ref[...], act_ref[0], act_ref[1], next_ref[...]]
    mixed = mm(jnp.concatenate([p.reshape(1024, C) for p in parts], axis=1), w_time)
    for f in range(2):
        total = x_ref[f].astype(F32).reshape(1024, C) + mixed[:, f * C : (f + 1) * C]
        resid_ref[f] = total.astype(BF16).reshape(8, 128, C)


def down_kernel(resid_ref, before_ref, wd_ref, out_ref):
    parts = [before_ref[...], resid_ref[0], resid_ref[1]]
    rows = jnp.concatenate([p.reshape(1024, C) for p in parts], axis=1)
    weights = jnp.concatenate([wd_ref[0], wd_ref[1], wd_ref[2]], axis=0)
    out_ref[...] = mm(rows, weights).astype(BF16).reshape(8, 128, C)


def features_kernel(gpre_ref, lo_ref, hi_ref, cot_ref, next_ref, w_ref, wd_ref, out_ref, wide_ref):
    wide_ref[...] = jnp.zeros_like(wide_ref)
    for out in range(2):
        for dy in range(3):
            for dx in range(3):
                start = ((dy + out) * 3 + dx) * C
                wide_ref[out * C : (out + 1) * C, start : start + C] = w_ref[2 - dy, 2 - dx]
    zero = jnp.zeros((C, C), BF16)
    w_pair = jnp.concatenate(
        [
            jnp.concatenate([wd_ref[1], zero], axis=1),
            jnp.concatenate([wd_ref[2], wd_ref[0]], axis=1),
        ],
        axis=0,
    )
    cot, after = (r[...].reshape(1024, C) for r in (cot_ref, next_ref))
    resid = mm_nt(jnp.concatenate([cot, after], axis=1), w_pair)
    for f in range(2):
        g = jnp.concatenate([lo_ref[f], gpre_ref[f], hi_ref[f]], axis=0).reshape(1280, C)
        conv = mm_nt(row_pairs(jnp.concatenate(columns(g), axis=1)), wide_ref[...])
        base = resid[:, f * C : (f + 1) * C].reshape(4, 2, 128, C)
        for out in range(2):
            part = conv[:, out * C : (out + 1) * C].reshape(4, 128, C)
            out_ref[f, :, out] = (base[:, out] + part).astype(BF16)


VMEM = pl.BlockSpec(memory_space=pltpu.VMEM)
SMEM = pl.BlockSpec(memory_space=pltpu.SMEM)


def call(kernel, outs, args, taps, scratch=(), scalars=0):
    return pl.pallas_call(
        kernel,
        out_shape=[jax.ShapeDtypeStruct(s, d) for s, d in outs],
        in_specs=[SMEM] * scalars + [VMEM] * (len(args) - scalars),
        out_specs=[VMEM] * len(outs),
        scratch_shapes=list(scratch),
        compiler_params=pltpu.CompilerParams(vmem_limit_bytes=40 * 1024 * 1024),
        cost_estimate=pl.CostEstimate(
            flops=int(taps * 2048 * C * C * 2), bytes_accessed=4_000_000, transcendentals=0
        ),
    )(*args)


def shift(x, axis, by):
    count = lax.axis_size(axis)
    return lax.ppermute(x, axis, [(i, i + by) for i in range(count) if 0 <= i + by < count])


def swap(x, axis, mask):
    return lax.ppermute(x, axis, [(i, i ^ mask) for i in range(lax.axis_size(axis))])


def sum_all(send, keep, core):
    half = keep + swap(send, "core", 1).astype(F32)
    half = jnp.concatenate([half.astype(BF16), jnp.zeros((1, 64, C), BF16)])
    got = lax.all_to_all(half, PLANE, 0, 0, tiled=True)
    total = jnp.sum(got.astype(F32), axis=0)
    for mask in (1, 2, 4):
        total = total + swap(total, "z", mask)
    out = jnp.broadcast_to(total.astype(BF16), (16, 64, C))
    out = lax.all_to_all(out, PLANE, 0, 0, tiled=True)[:15]
    other = swap(out, "core", 1)
    low, high = jnp.where(core == 0, out, other), jnp.where(core == 0, other, out)
    return jnp.concatenate([low, high], axis=1).astype(F32)


def per_device(features, w_spatial, w_temporal, w_down, cotangent):
    time, rows = ("z", "yl"), ("x", "core")
    x, cot = features[0], cotangent[0, 0]
    core = lax.axis_index("core")
    place = jnp.stack([lax.axis_index(time), core]).astype(jnp.int32)
    lo, hi = shift(x[:, 7:], rows, 1), shift(x[:, :1], rows, -1)
    cot_prev, cot_next = shift(cot, time, 1), shift(cot, time, -1)
    slope, act, xt, at = call(
        forward_kernel,
        [((2, 4, 2, 128, C), F32), ((2, 4, 2, 128, C), BF16), ((2, C, 1280), BF16), ((2, C, 1024), BF16)],
        (x, lo, hi, w_spatial), 9,
        scratch=[pltpu.VMEM((12 * C, 2 * C), BF16)],
    )
    gpre, send, keep = call(
        grads_kernel,
        [((2, 8, 128, C), BF16), ((15, 64, C), BF16), ((15, 64, C), F32)],
        (place, slope, xt, at, cot, cot_prev, cot_next, w_temporal, w_down), 21,
        scratch=[pltpu.VMEM((15, 2, 64, C), F32)], scalars=1,
    )
    grads = sum_all(send, keep, core)
    act = act.reshape(2, 8, 128, C)
    act_prev, act_next = shift(act[1], time, 1), shift(act[0], time, -1)
    g_lo, g_hi = shift(gpre[:, 7:], rows, 1), shift(gpre[:, :1], rows, -1)
    (resid,) = call(
        resid_kernel, [((2, 8, 128, C), BF16)], (x, act, act_prev, act_next, w_temporal), 3
    )
    before = shift(resid[1], time, 1)
    (grad_features,) = call(
        features_kernel, [((2, 4, 2, 128, C), BF16)],
        (gpre, g_lo, g_hi, cot, cot_next, w_spatial, w_down), 11,
        scratch=[pltpu.VMEM((2 * C, 12 * C), BF16)],
    )
    (down,) = call(down_kernel, [((8, 128, C), BF16)], (resid, before, w_down), 1.5)
    return (
        down[None, None],
        grad_features.reshape(1, 2, 8, 128, C),
        grads[:9].reshape(3, 3, C, C),
        grads[9:12],
        grads[12:],
    )


def solution(mesh):
    fine = Mesh(mesh.devices.reshape(2, 8, 2, 4, 2), ("yh", "z", "yl", "x", "core"))
    block = P("yh", ("z", "yl"), ("x", "core"), None, None)
    return jax.shard_map(
        per_device,
        mesh=fine,
        in_specs=(block, P(), P(), P(), block),
        out_specs=(block, block, P(), P(), P()),
        check_vma=False,
    )
```

time: 340 us -> 94.3 us (0.28)
  waiting for transfers between devices: 263 us -> 14.8 us
  matrix products: 19.9 us -> 0 us
  starting transfers between devices: 30 us -> 46.9 us
  blocking collectives: 0 us -> 15.8 us
  between operations: 14.6 us -> 0.95 us
  Pallas kernels: 0 us -> 8.37 us
    psum x1 -> x0, waiting for transfers between devices: 254 us -> none  [per_device(): lax.psum((grad_spatial, grad_temporal, grad_down), ('batch', 'tm', 'heigh...]
    dot_general x45 -> x0, matrix products: 19.9 us -> none  [the longest x18 7.14 us: spatial(): jnp.einsum('bfhwc,cd->bfhwd', wide[:, :, dy:dy + rows, dx:dx + cols], ker...]
    all_to_all x0 -> x1, blocking collectives: none -> 15.8 us  [sum_all(): got = lax.all_to_all(half, PLANE, 0, 0, tiled=True)]
    ppermute x10 -> x14, starting transfers between devices: 30 us -> 42.7 us  [the longest x9 21.7 us: shift(): lax.ppermute(x, axis, [(i, i + by) for i in range(count) if 0 <= i + by <...]
    pallas_call x0 -> x5, Pallas kernels: none -> 8.37 us  [call(): pl.pallas_call(kernel, out_shape=[jax.ShapeDtypeStruct(s, d) for s, d in...]
    unnamed x33 -> x16, local copies, waits for them, and re-layouts: 6.83 us -> 1.08 us
    all_to_all x0 -> x1, starting transfers between devices: none -> 4.19 us  [sum_all(): out = lax.all_to_all(out, PLANE, 0, 0, tiled=True)[:15]]
    all_to_all x0 -> x1, waiting for transfers between devices: none -> 3.77 us  [sum_all(): out = lax.all_to_all(out, PLANE, 0, 0, tiled=True)[:15]]
  transfers between devices with their start and end apart: 11 -> 15, of which waited for: 3 -> 6; matrix products, arithmetic and copies ran while one was open for 7% -> 3% of each run, Pallas kernels for 0% -> 5%
where the time goes in v1:
time: 94.3 us; the launch traced here: 93.5 us
  starting transfers between devices  46.9 us (50%)
  blocking collectives  15.8 us (17%)
  waiting for transfers between devices  14.8 us (16%)
  Pallas kernels  8.37 us (9%)
  local copies, waits for them, and re-layouts  4.63 us (5%)
  other arithmetic  2.04 us (2%)
  between operations  0.95 us (1%)
    ppermute x9, starting transfers between devices, shift(): lax.ppermute(x, axis, [(i, i + by) for i in range(count) if 0 <= i + by <...  21.7 us
    ppermute x5, starting transfers between devices, swap(): lax.ppermute(x, axis, [(i, i ^ mask) for i in range(lax.axis_size(axis))])  21 us
    all_to_all x1, blocking collectives, sum_all(): got = lax.all_to_all(half, PLANE, 0, 0, tiled=True)  15.8 us
    pallas_call x5, Pallas kernels, call(): pl.pallas_call(kernel, out_shape=[jax.ShapeDtypeStruct(s, d) for s, d in...  8.37 us
    ppermute x9, waiting for transfers between devices, shift(): lax.ppermute(x, axis, [(i, i + by) for i in range(count) if 0 <= i + by <...  6.93 us
    all_to_all x1, starting transfers between devices, sum_all(): out = lax.all_to_all(out, PLANE, 0, 0, tiled=True)[:15]  4.19 us
    ppermute x5, waiting for transfers between devices, swap(): lax.ppermute(x, axis, [(i, i ^ mask) for i in range(lax.axis_size(axis))])  4.11 us
    all_to_all x1, waiting for transfers between devices, sum_all(): out = lax.all_to_all(out, PLANE, 0, 0, tiled=True)[:15]  3.77 us
  transfers between devices with their start and end apart: 15, of which 6 were waited for; matrix products, arithmetic and copies ran while one was open for 3% of the time, Pallas kernels for 5%

profile of v1, /device:TPU:1, one launch (start us, length us, event | category | flops | bytes accessed | tf_op | source)
XLA Modules:
  0.0 93.5 jit_solution(3690811221764126388)
XLA Ops:
  0.6 0.0 copy-start.4
  0.6 4.2 %collective-permute-start.5 = (bf16[8,128,128]{2,1,0:T(8,128)(2,1)}, bf16[8,128,128]{2,1,0:T(8,128)(2,1)S(1)}, u32[]{:S(2)}, u32[]{:S(2)}) collective-permute-start(bf16[8,128,128]{2,1,0:T(8,128)(2,1)} %bitcast.16), channel_id=1, source_target_pairs={{0,8},{8,16},{16,24},{24,32},{32,40},{40,48},{48,56},{56,64},{64,7... | collective-permute-start | bytes 786440 | tf_op jit(solution)/shard_map/ppermute | solution.py:200
  4.8 1.3 %collective-permute-start.6 = (bf16[8,128,128]{2,1,0:T(8,128)(2,1)}, bf16[8,128,128]{2,1,0:T(8,128)(2,1)S(1)}, u32[]{:S(2)}, u32[]{:S(2)}) collective-permute-start(bf16[8,128,128]{2,1,0:T(8,128)(2,1)} %bitcast.17), channel_id=1, source_target_pairs={{8,0},{16,8},{24,16},{32,24},{40,32},{48,40},{56,48},{64,56},{72,6... | collective-permute-start | bytes 786440 | tf_op jit(solution)/shard_map/ppermute | solution.py:200
  6.1 0.9 fusion.2
  7.0 4.0 %collective-permute-start = (bf16[2,1,128,128]{3,2,1,0:T(8,128)(2,1)S(1)}, bf16[2,1,128,128]{3,2,1,0:T(8,128)(2,1)S(1)}, u32[]{:S(2)}, u32[]{:S(2)}) collective-permute-start(bf16[2,1,128,128]{3,2,1,0:T(8,128)(2,1)S(1)} %get-tuple-element.24), channel_id=1, source_target_pairs={{0,1},{1,2},{2,3},{3,4},{4,5},{5,6},{6,7},{8,9},{9,10},{10,11},{11... | collective-permute-start | bytes 196616 | tf_op jit(solution)/shard_map/ppermute | solution.py:200
  11.0 1.9 %collective-permute-start.1 = (bf16[2,1,128,128]{3,2,1,0:T(8,128)(2,1)S(1)}, bf16[2,1,128,128]{3,2,1,0:T(8,128)(2,1)S(1)}, u32[]{:S(2)}, u32[]{:S(2)}) collective-permute-start(bf16[2,1,128,128]{3,2,1,0:T(8,128)(2,1)S(1)} %get-tuple-element.23), channel_id=1, source_target_pairs={{1,0},{2,1},{3,2},{4,3},{5,4},{6,5},{7,6},{9,8},{10,9},{11,10},{12... | collective-permute-start | bytes 196616 | tf_op jit(solution)/shard_map/ppermute | solution.py:200
  12.9 0.1 pad_add_fusion.place_ref
  13.0 0.0 collective-permute-done.lo_ref
  13.0 3.6 %collective-permute-done.1.hi_ref = bf16[2,1,128,128]{3,2,1,0:T(8,128)(2,1)S(1)} collective-permute-done((bf16[2,1,128,128]{3,2,1,0:T(8,128)(2,1)S(1)}, bf16[2,1,128,128]{3,2,1,0:T(8,128)(2,1)S(1)}, u32[]{:S(2)}, u32[]{:S(2)}) %collective-permute-start.1) | collective-permute-done | bytes 65568 | tf_op jit(solution)/shard_map/ppermute | solution.py:200
  16.6 0.0 copy-done.4
  16.6 0.0 copy-start
  16.6 1.0 %copy-done = bf16[1,2,8,128,128]{4,3,2,1,0:T(8,128)(2,1)S(1)} copy-done((bf16[1,2,8,128,128]{4,3,2,1,0:T(8,128)(2,1)S(1)}, bf16[1,2,8,128,128]{4,3,2,1,0:T(8,128)(2,1)}, u32[]{:S(2)}) %copy-start) | copy-done | bytes 524312
  17.6 0.0 copy-start.2
  17.6 0.0 copy-start.3
  17.6 0.0 copy-start.5
  17.6 1.5 %shard_map.92 = (f32[2,4,2,128,128]{4,3,2,1,0:T(8,128)S(1)}, bf16[2,4,2,128,128]{4,3,2,1,0:T(8,128)(2,1)S(1)}, bf16[2,128,1280]{2,1,0:T(8,128)(2,1)S(1)}, bf16[2,128,1024]{2,1,0:T(8,128)(2,1)S(1)}) custom-call(bf16[2,8,128,128]{3,2,1,0:T(8,128)(2,1)S(1)} %bitcast.14, bf16[2,1,128,128]{3,2,1,0:T(8,128)(2,1)S(1)} %collective-permute-done.lo_ref, ...), custom_call_target="tpu_custom_call" | custom-call | flops 603979776 | bytes 4000000 | tf_op jit(solution)/shard_map/pallas_call | solution.py:185
  19.1 0.0 collective-permute-done.5.prev_ref
  19.1 0.0 collective-permute-done.6.next_ref
  19.1 0.0 copy-start.6
  19.2 0.0 copy-done.2
  19.2 0.0 copy-done.3
  19.2 0.0 copy-done.5
  19.2 3.4 %shard_map.95 = (bf16[2,8,128,128]{3,2,1,0:T(8,128)(2,1)S(1)}, bf16[15,64,128]{2,1,0:T(8,128)(2,1)S(1)}, f32[15,64,128]{2,1,0:T(8,128)S(1)}) custom-call(s32[2]{0:T(128)S(1)} %pad_add_fusion.place_ref, f32[2,4,2,128,128]{4,3,2,1,0:T(8,128)S(1)} %get-tuple-element.13.slope_ref, bf16[2,128,1280]{2,1,0:T(8,128)(2,1)S(1)} %get-tuple-element.14.xt_ref, ...), custom_call_target="tpu_custom_call" | custom-call | flops 1409286144 | bytes 4000000 | tf_op jit(solution)/shard_map/pallas_call | solution.py:185
  22.6 0.0 copy-done.6
  22.6 0.1 collective-permute-start.9
  22.7 1.5 %collective-permute-done.9 = bf16[15,64,128]{2,1,0:T(8,128)(2,1)S(1)} collective-permute-done((bf16[15,64,128]{2,1,0:T(8,128)(2,1)S(1)}, bf16[15,64,128]{2,1,0:T(8,128)(2,1)S(1)}, u32[]{:S(2)}, u32[]{:S(2)}) %collective-permute-start.9) | collective-permute-done | bytes 245792 | tf_op jit(solution)/shard_map/ppermute | solution.py:204
  24.2 0.1 add_convert_fusion
  24.3 15.8 %all_to_all.10 = bf16[16,64,128]{2,1,0:T(8,128)(2,1)S(1)} all-to-all(bf16[16,64,128]{2,1,0:T(8,128)(2,1)S(1)} %concatenate.6), channel_id=1, replica_groups=mesh['yh'=2,'z'=8,'yl'=2,'x'=4,'core'=2] {'yh','yl','x'}, dimensions={0} | all-to-all | bytes 524288 | tf_op jit(solution)/shard_map/all_to_all | solution.py:210
  40.2 2.8 %collective-permute-start.10 = (f32[64,128]{1,0:T(8,128)S(1)}, f32[64,128]{1,0:T(8,128)S(1)}, u32[]{:S(2)}, u32[]{:S(2)}) collective-permute-start(f32[64,128]{1,0:T(8,128)S(1)} %convert_reduce_fusion), channel_id=1, source_target_pairs={{0,16},{16,0},{32,48},{48,32},{64,80},{80,64},{96,112},{112,96},{1... | collective-permute-start | bytes 98312 | tf_op jit(solution)/shard_map/ppermute | solution.py:204
  42.9 1.3 %collective-permute-done.10 = f32[64,128]{1,0:T(8,128)S(1)} collective-permute-done((f32[64,128]{1,0:T(8,128)S(1)}, f32[64,128]{1,0:T(8,128)S(1)}, u32[]{:S(2)}, u32[]{:S(2)}) %collective-permute-start.10) | collective-permute-done | bytes 32800 | tf_op jit(solution)/shard_map/ppermute | solution.py:204
  44.2 3.2 %collective-permute-start.11 = (f32[64,128]{1,0:T(8,128)S(1)}, f32[64,128]{1,0:T(8,128)S(1)}, u32[]{:S(2)}, u32[]{:S(2)}) collective-permute-start(f32[64,128]{1,0:T(8,128)S(1)} %add.19), channel_id=1, source_target_pairs={{0,32},{16,48},{32,0},{48,16},{64,96},{80,112},{96,64},{112,80},{1... | collective-permute-start | bytes 98312 | tf_op jit(solution)/shard_map/ppermute | solution.py:204
  47.5 0.0 copy-start.1
  47.5 1.4 %collective-permute-start.2 = (bf16[8,128,128]{2,1,0:T(8,128)(2,1)S(1)}, bf16[8,128,128]{2,1,0:T(8,128)(2,1)S(1)}, u32[]{:S(2)}, u32[]{:S(2)}) collective-permute-start(bf16[8,128,128]{2,1,0:T(8,128)(2,1)S(1)} %bitcast.22), channel_id=1, source_target_pairs={{0,8},{8,16},{16,24},{24,32},{32,40},{40,48},{48,56},{56,64},{64,7... | collective-permute-start | bytes 786440 | tf_op jit(solution)/shard_map/ppermute | solution.py:200
  49.0 1.3 %collective-permute-start.3 = (bf16[8,128,128]{2,1,0:T(8,128)(2,1)S(1)}, bf16[8,128,128]{2,1,0:T(8,128)(2,1)S(1)}, u32[]{:S(2)}, u32[]{:S(2)}) collective-permute-start(bf16[8,128,128]{2,1,0:T(8,128)(2,1)S(1)} %bitcast.21), channel_id=1, source_target_pairs={{8,0},{16,8},{24,16},{32,24},{40,32},{48,40},{56,48},{64,56},{72,6... | collective-permute-start | bytes 786440 | tf_op jit(solution)/shard_map/ppermute | solution.py:200
  50.3 0.0 collective-permute-done.11
  50.3 9.6 %collective-permute-start.12 = (f32[64,128]{1,0:T(8,128)S(1)}, f32[64,128]{1,0:T(8,128)S(1)}, u32[]{:S(2)}, u32[]{:S(2)}) collective-permute-start(f32[64,128]{1,0:T(8,128)S(1)} %add.20), channel_id=1, source_target_pairs={{0,64},{16,80},{32,96},{48,112},{64,0},{80,16},{96,32},{112,48},{1... | collective-permute-start | bytes 98312 | tf_op jit(solution)/shard_map/ppermute | solution.py:204
  59.9 1.3 %collective-permute-done.12 = f32[64,128]{1,0:T(8,128)S(1)} collective-permute-done((f32[64,128]{1,0:T(8,128)S(1)}, f32[64,128]{1,0:T(8,128)S(1)}, u32[]{:S(2)}, u32[]{:S(2)}) %collective-permute-start.12) | collective-permute-done | bytes 32800 | tf_op jit(solution)/shard_map/ppermute | solution.py:204
  61.2 0.8 broadcast_in_dim.8
  62.0 4.2 %all-to-all-start.1 = ((bf16[16,64,128]{2,1,0:T(8,128)(2,1)}), bf16[16,64,128]{2,1,0:T(8,128)(2,1)}, u32[]{:S(2)}, u32[]{:S(2)}) async-start(bf16[16,64,128]{2,1,0:T(8,128)(2,1)} %broadcast_in_dim.8), calls=%async_computation.1 | async-start | bytes 524288 | tf_op jit(solution)/shard_map/all_to_all | solution.py:215
  66.2 0.0 collective-permute-done.2.prev_ref
  66.2 0.0 collective-permute-done.3.next_ref
  66.2 0.0 copy-done.1
  66.2 0.4 shard_map.93.resid_ref
  66.7 0.0 copy-start.7
  66.7 3.3 %collective-permute-start.4 = (bf16[8,128,128]{2,1,0:T(8,128)(2,1)S(1)}, bf16[8,128,128]{2,1,0:T(8,128)(2,1)S(1)}, u32[]{:S(2)}, u32[]{:S(2)}) collective-permute-start(bf16[8,128,128]{2,1,0:T(8,128)(2,1)S(1)} %slice_bitcast_fusion), channel_id=1, source_target_pairs={{0,8},{8,16},{16,24},{24,32},{32,40},{40,48},{48,56},{56,64},{64,7... | collective-permute-start | bytes 786440 | tf_op jit(solution)/shard_map/ppermute | solution.py:200
  70.0 3.8 %all-to-all-done.1 = bf16[16,64,128]{2,1,0:T(8,128)(2,1)} async-done(((bf16[16,64,128]{2,1,0:T(8,128)(2,1)}), bf16[16,64,128]{2,1,0:T(8,128)(2,1)}, u32[]{:S(2)}, u32[]{:S(2)}) %all-to-all-start.1) | async-done | bytes 262176 | tf_op jit(solution)/shard_map/all_to_all | solution.py:215
  73.7 1.0 %slice.49 = bf16[15,64,128]{2,1,0:T(8,128)(2,1)S(1)} slice(bf16[16,64,128]{2,1,0:T(8,128)(2,1)} %all-to-all-done.1), slice={[0:15], [0:64], [0:128]} | slice | bytes 491520 | tf_op jit(solution)/shard_map/slice | solution.py:215
  74.7 5.3 %collective-permute-start.13 = (bf16[15,64,128]{2,1,0:T(8,128)(2,1)S(1)}, bf16[15,64,128]{2,1,0:T(8,128)(2,1)S(1)}, u32[]{:S(2)}, u32[]{:S(2)}) collective-permute-start(bf16[15,64,128]{2,1,0:T(8,128)(2,1)S(1)} %slice.49), channel_id=1, source_target_pairs={{0,1},{1,0},{2,3},{3,2},{4,5},{5,4},{6,7},{7,6},{8,9},{9,8},{10,11... | collective-permute-start | bytes 737288 | tf_op jit(solution)/shard_map/ppermute | solution.py:204
  80.1 2.1 %collective-permute-start.7 = (bf16[2,1,128,128]{3,2,1,0:T(8,128)(2,1)S(1)}, bf16[2,1,128,128]{3,2,1,0:T(8,128)(2,1)S(1)}, u32[]{:S(2)}, u32[]{:S(2)}) collective-permute-start(bf16[2,1,128,128]{3,2,1,0:T(8,128)(2,1)S(1)} %get-tuple-element.20), channel_id=1, source_target_pairs={{0,1},{1,2},{2,3},{3,4},{4,5},{5,6},{6,7},{8,9},{9,10},{10,11},{11... | collective-permute-start | bytes 196616 | tf_op jit(solution)/shard_map/ppermute | solution.py:200
  82.2 2.2 %collective-permute-start.8 = (bf16[2,1,128,128]{3,2,1,0:T(8,128)(2,1)S(1)}, bf16[2,1,128,128]{3,2,1,0:T(8,128)(2,1)S(1)}, u32[]{:S(2)}, u32[]{:S(2)}) collective-permute-start(bf16[2,1,128,128]{3,2,1,0:T(8,128)(2,1)S(1)} %get-tuple-element.19), channel_id=1, source_target_pairs={{1,0},{2,1},{3,2},{4,3},{5,4},{6,5},{7,6},{9,8},{10,9},{11,10},{12... | collective-permute-start | bytes 196616 | tf_op jit(solution)/shard_map/ppermute | solution.py:200
  84.4 0.0 collective-permute-done.7.lo_ref
  84.4 3.3 %collective-permute-done.8.hi_ref = bf16[2,1,128,128]{3,2,1,0:T(8,128)(2,1)S(1)} collective-permute-done((bf16[2,1,128,128]{3,2,1,0:T(8,128)(2,1)S(1)}, bf16[2,1,128,128]{3,2,1,0:T(8,128)(2,1)S(1)}, u32[]{:S(2)}, u32[]{:S(2)}) %collective-permute-start.8) | collective-permute-done | bytes 65568 | tf_op jit(solution)/shard_map/ppermute | solution.py:200
  87.7 0.0 copy-done.7
  87.8 2.0 %shard_map.96 = bf16[2,4,2,128,128]{4,3,2,1,0:T(8,128)(2,1)} custom-call(bf16[2,8,128,128]{3,2,1,0:T(8,128)(2,1)S(1)} %get-tuple-element.16.gpre_ref, bf16[2,1,128,128]{3,2,1,0:T(8,128)(2,1)S(1)} %collective-permute-done.7.lo_ref, bf16[2,1,128,128]{3,2,1,0:T(8,128)(2,1)S(1)} %collective-permute-done.8.hi_ref, bf16[8,128,128]{2,1,0:T(8,128)(2,1)S(1)} %bitcast.19, ...), custom_call_target="tpu_custom_call" | custom-call | flops 738197504 | bytes 4000000 | tf_op jit(solution)/shard_map/pallas_call | solution.py:185
  89.7 0.0 collective-permute-done.4.before_ref
  89.7 1.1 %shard_map.94 = bf16[8,128,128]{2,1,0:T(8,128)(2,1)} custom-call(bf16[2,8,128,128]{3,2,1,0:T(8,128)(2,1)S(1)} %shard_map.93.resid_ref, bf16[8,128,128]{2,1,0:T(8,128)(2,1)S(1)} %collective-permute-done.4.before_ref, bf16[3,128,128]{2,1,0:T(8,128)(2,1)S(1)} %copy-done.3), custom_call_target="tpu_custom_call" | custom-call | flops 100663296 | bytes 4000000 | tf_op jit(solution)/shard_map/pallas_call | solution.py:185
  90.8 0.0 collective-permute-done.13
  90.8 1.0 %broadcast_select_fusion.1 = (bf16[15,64,128]{2,1,0:T(8,128)(2,1)S(1)}, bf16[15,64,128]{2,1,0:T(8,128)(2,1)S(1)}) fusion(bf16[15,64,128]{2,1,0:T(8,128)(2,1)S(1)} %collective-permute-done.13, pred[]{:T(512)S(6)} %eq.4, bf16[16,64,128]{2,1,0:T(8,128)(2,1)} %all-to-all-done.1), kind=kLoop, calls=%fused_computation.5 | loop fusion | flops 245760 | bytes 983041 | tf_op jit(solution)/shard_map/jit(_where)/select_n | solution.py:217
  91.8 0.1 maximum_convert_fusion
  91.9 0.8 maximum_convert_fusion.1
  92.7 0.9 slice.50
  (8 shorter events, 0.1 us)
Async XLA Ops:
  0.6 15.9 %copy-start.4 = (bf16[3,3,128,128]{3,2,1,0:T(8,128)(2,1)S(1)}, bf16[3,3,128,128]{3,2,1,0:T(8,128)(2,1)}, u32[]{:S(2)}) copy-start(bf16[3,3,128,128]{3,2,1,0:T(8,128)(2,1)} %w_ref.3) | copy-start | bytes 884740
  0.6 18.5 %collective-permute-start.5 = (bf16[8,128,128]{2,1,0:T(8,128)(2,1)}, bf16[8,128,128]{2,1,0:T(8,128)(2,1)S(1)}, u32[]{:S(2)}, u32[]{:S(2)}) collective-permute-start(bf16[8,128,128]{2,1,0:T(8,128)(2,1)} %bitcast.16), channel_id=1, source_target_pairs={{0,8},{8,16},{16,24},{24,32},{32,40},{40,48},{48,56},{56,64},{64,7... | collective-permute-start | bytes 786440 | tf_op jit(solution)/shard_map/ppermute | solution.py:200
  4.8 14.3 %collective-permute-start.6 = (bf16[8,128,128]{2,1,0:T(8,128)(2,1)}, bf16[8,128,128]{2,1,0:T(8,128)(2,1)S(1)}, u32[]{:S(2)}, u32[]{:S(2)}) collective-permute-start(bf16[8,128,128]{2,1,0:T(8,128)(2,1)} %bitcast.17), channel_id=1, source_target_pairs={{8,0},{16,8},{24,16},{32,24},{40,32},{48,40},{56,48},{64,56},{72,6... | collective-permute-start | bytes 786440 | tf_op jit(solution)/shard_map/ppermute | solution.py:200
  7.0 6.0 %collective-permute-start = (bf16[2,1,128,128]{3,2,1,0:T(8,128)(2,1)S(1)}, bf16[2,1,128,128]{3,2,1,0:T(8,128)(2,1)S(1)}, u32[]{:S(2)}, u32[]{:S(2)}) collective-permute-start(bf16[2,1,128,128]{3,2,1,0:T(8,128)(2,1)S(1)} %get-tuple-element.24), channel_id=1, source_target_pairs={{0,1},{1,2},{2,3},{3,4},{4,5},{5,6},{6,7},{8,9},{9,10},{10,11},{11... | collective-permute-start | bytes 196616 | tf_op jit(solution)/shard_map/ppermute | solution.py:200
  11.0 5.6 %collective-permute-start.1 = (bf16[2,1,128,128]{3,2,1,0:T(8,128)(2,1)S(1)}, bf16[2,1,128,128]{3,2,1,0:T(8,128)(2,1)S(1)}, u32[]{:S(2)}, u32[]{:S(2)}) collective-permute-start(bf16[2,1,128,128]{3,2,1,0:T(8,128)(2,1)S(1)} %get-tuple-element.23), channel_id=1, source_target_pairs={{1,0},{2,1},{3,2},{4,3},{5,4},{6,5},{7,6},{9,8},{10,9},{11,10},{12... | collective-permute-start | bytes 196616 | tf_op jit(solution)/shard_map/ppermute | solution.py:200
  16.6 1.0 %copy-start = (bf16[1,2,8,128,128]{4,3,2,1,0:T(8,128)(2,1)S(1)}, bf16[1,2,8,128,128]{4,3,2,1,0:T(8,128)(2,1)}, u32[]{:S(2)}) copy-start(bf16[1,2,8,128,128]{4,3,2,1,0:T(8,128)(2,1)} %param.5) | copy-start | bytes 1572868
  17.6 1.5 %copy-start.2 = (bf16[3,128,128]{2,1,0:T(8,128)(2,1)S(1)}, bf16[3,128,128]{2,1,0:T(8,128)(2,1)}, u32[]{:S(2)}) copy-start(bf16[3,128,128]{2,1,0:T(8,128)(2,1)} %wt_ref.3) | copy-start | bytes 294916
  17.6 1.6 %copy-start.3 = (bf16[3,128,128]{2,1,0:T(8,128)(2,1)S(1)}, bf16[3,128,128]{2,1,0:T(8,128)(2,1)}, u32[]{:S(2)}) copy-start(bf16[3,128,128]{2,1,0:T(8,128)(2,1)} %wd_ref.5) | copy-start | bytes 294916
  17.6 1.6 %copy-start.5 = (bf16[1,1,8,128,128]{4,3,2,1,0:T(8,128)(2,1)S(1)}, bf16[1,1,8,128,128]{4,3,2,1,0:T(8,128)(2,1)}, u32[]{:S(2)}) copy-start(bf16[1,1,8,128,128]{4,3,2,1,0:T(8,128)(2,1)} %param.9) | copy-start | bytes 786436
  19.1 3.4 %copy-start.6 = (bf16[8,128,128]{2,1,0:T(8,128)(2,1)}, bf16[8,128,128]{2,1,0:T(8,128)(2,1)S(1)}, u32[]{:S(2)}) copy-start(bf16[8,128,128]{2,1,0:T(8,128)(2,1)S(1)} %collective-permute-done.6.next_ref) | copy-start | bytes 786436
  22.6 1.6 %collective-permute-start.9 = (bf16[15,64,128]{2,1,0:T(8,128)(2,1)S(1)}, bf16[15,64,128]{2,1,0:T(8,128)(2,1)S(1)}, u32[]{:S(2)}, u32[]{:S(2)}) collective-permute-start(bf16[15,64,128]{2,1,0:T(8,128)(2,1)S(1)} %get-tuple-element.18), channel_id=1, source_target_pairs={{0,1},{1,0},{2,3},{3,2},{4,5},{5,4},{6,7},{7,6},{8,9},{9,8},{10,11... | collective-permute-start | bytes 737288 | tf_op jit(solution)/shard_map/ppermute | solution.py:204
  40.2 4.1 %collective-permute-start.10 = (f32[64,128]{1,0:T(8,128)S(1)}, f32[64,128]{1,0:T(8,128)S(1)}, u32[]{:S(2)}, u32[]{:S(2)}) collective-permute-start(f32[64,128]{1,0:T(8,128)S(1)} %convert_reduce_fusion), channel_id=1, source_target_pairs={{0,16},{16,0},{32,48},{48,32},{64,80},{80,64},{96,112},{112,96},{1... | collective-permute-start | bytes 98312 | tf_op jit(solution)/shard_map/ppermute | solution.py:204
  44.2 6.0 %collective-permute-start.11 = (f32[64,128]{1,0:T(8,128)S(1)}, f32[64,128]{1,0:T(8,128)S(1)}, u32[]{:S(2)}, u32[]{:S(2)}) collective-permute-start(f32[64,128]{1,0:T(8,128)S(1)} %add.19), channel_id=1, source_target_pairs={{0,32},{16,48},{32,0},{48,16},{64,96},{80,112},{96,64},{112,80},{1... | collective-permute-start | bytes 98312 | tf_op jit(solution)/shard_map/ppermute | solution.py:204
  47.5 18.7 %copy-start.1 = (bf16[1,2,8,128,128]{4,3,2,1,0:T(8,128)(2,1)S(1)}, bf16[1,2,8,128,128]{4,3,2,1,0:T(8,128)(2,1)}, u32[]{:S(2)}) copy-start(bf16[1,2,8,128,128]{4,3,2,1,0:T(8,128)(2,1)} %param.5) | copy-start | bytes 1572868
  47.5 18.7 %collective-permute-start.2 = (bf16[8,128,128]{2,1,0:T(8,128)(2,1)S(1)}, bf16[8,128,128]{2,1,0:T(8,128)(2,1)S(1)}, u32[]{:S(2)}, u32[]{:S(2)}) collective-permute-start(bf16[8,128,128]{2,1,0:T(8,128)(2,1)S(1)} %bitcast.22), channel_id=1, source_target_pairs={{0,8},{8,16},{16,24},{24,32},{32,40},{40,48},{48,56},{56,64},{64,7... | collective-permute-start | bytes 786440 | tf_op jit(solution)/shard_map/ppermute | solution.py:200
  49.0 17.2 %collective-permute-start.3 = (bf16[8,128,128]{2,1,0:T(8,128)(2,1)S(1)}, bf16[8,128,128]{2,1,0:T(8,128)(2,1)S(1)}, u32[]{:S(2)}, u32[]{:S(2)}) collective-permute-start(bf16[8,128,128]{2,1,0:T(8,128)(2,1)S(1)} %bitcast.21), channel_id=1, source_target_pairs={{8,0},{16,8},{24,16},{32,24},{40,32},{48,40},{56,48},{64,56},{72,6... | collective-permute-start | bytes 786440 | tf_op jit(solution)/shard_map/ppermute | solution.py:200
  50.3 10.9 %collective-permute-start.12 = (f32[64,128]{1,0:T(8,128)S(1)}, f32[64,128]{1,0:T(8,128)S(1)}, u32[]{:S(2)}, u32[]{:S(2)}) collective-permute-start(f32[64,128]{1,0:T(8,128)S(1)} %add.20), channel_id=1, source_target_pairs={{0,64},{16,80},{32,96},{48,112},{64,0},{80,16},{96,32},{112,48},{1... | collective-permute-start | bytes 98312 | tf_op jit(solution)/shard_map/ppermute | solution.py:204
  62.0 11.7 %all-to-all-start.1 = ((bf16[16,64,128]{2,1,0:T(8,128)(2,1)}), bf16[16,64,128]{2,1,0:T(8,128)(2,1)}, u32[]{:S(2)}, u32[]{:S(2)}) async-start(bf16[16,64,128]{2,1,0:T(8,128)(2,1)} %broadcast_in_dim.8), calls=%async_computation.1 | async-start | bytes 524288 | tf_op jit(solution)/shard_map/all_to_all | solution.py:215
  66.7 21.1 %copy-start.7 = (bf16[8,128,128]{2,1,0:T(8,128)(2,1)S(1)}, bf16[8,128,128]{2,1,0:T(8,128)(2,1)}, u32[]{:S(2)}) copy-start(bf16[8,128,128]{2,1,0:T(8,128)(2,1)} %copy-done.6) | copy-start | bytes 786436
  66.7 23.0 %collective-permute-start.4 = (bf16[8,128,128]{2,1,0:T(8,128)(2,1)S(1)}, bf16[8,128,128]{2,1,0:T(8,128)(2,1)S(1)}, u32[]{:S(2)}, u32[]{:S(2)}) collective-permute-start(bf16[8,128,128]{2,1,0:T(8,128)(2,1)S(1)} %slice_bitcast_fusion), channel_id=1, source_target_pairs={{0,8},{8,16},{16,24},{24,32},{32,40},{40,48},{48,56},{56,64},{64,7... | collective-permute-start | bytes 786440 | tf_op jit(solution)/shard_map/ppermute | solution.py:200
  74.7 16.1 %collective-permute-start.13 = (bf16[15,64,128]{2,1,0:T(8,128)(2,1)S(1)}, bf16[15,64,128]{2,1,0:T(8,128)(2,1)S(1)}, u32[]{:S(2)}, u32[]{:S(2)}) collective-permute-start(bf16[15,64,128]{2,1,0:T(8,128)(2,1)S(1)} %slice.49), channel_id=1, source_target_pairs={{0,1},{1,0},{2,3},{3,2},{4,5},{5,4},{6,7},{7,6},{8,9},{9,8},{10,11... | collective-permute-start | bytes 737288 | tf_op jit(solution)/shard_map/ppermute | solution.py:204
  80.1 4.3 %collective-permute-start.7 = (bf16[2,1,128,128]{3,2,1,0:T(8,128)(2,1)S(1)}, bf16[2,1,128,128]{3,2,1,0:T(8,128)(2,1)S(1)}, u32[]{:S(2)}, u32[]{:S(2)}) collective-permute-start(bf16[2,1,128,128]{3,2,1,0:T(8,128)(2,1)S(1)} %get-tuple-element.20), channel_id=1, source_target_pairs={{0,1},{1,2},{2,3},{3,4},{4,5},{5,6},{6,7},{8,9},{9,10},{10,11},{11... | collective-permute-start | bytes 196616 | tf_op jit(solution)/shard_map/ppermute | solution.py:200
  82.2 5.6 %collective-permute-start.8 = (bf16[2,1,128,128]{3,2,1,0:T(8,128)(2,1)S(1)}, bf16[2,1,128,128]{3,2,1,0:T(8,128)(2,1)S(1)}, u32[]{:S(2)}, u32[]{:S(2)}) collective-permute-start(bf16[2,1,128,128]{3,2,1,0:T(8,128)(2,1)S(1)} %get-tuple-element.19), channel_id=1, source_target_pairs={{1,0},{2,1},{3,2},{4,3},{5,4},{6,5},{7,6},{9,8},{10,9},{11,10},{12... | collective-permute-start | bytes 196616 | tf_op jit(solution)/shard_map/ppermute | solution.py:200

commit v2 on v1

--- a/solution.py
+++ b/solution.py
@@ -39,7 +39,14 @@
     return jnp.concatenate([p.reshape(512, depth) for p in parts], axis=1)
 
 
-def forward_kernel(x_ref, lo_ref, hi_ref, w_ref, slope_ref, act_ref, xt_ref, at_ref, wide_ref):
+def sides(place_ref, at, near, far):
+    odd = place_ref[at] % 2 == 1
+    return jnp.where(odd, near, far), jnp.where(odd, far, near)
+
+
+def forward_kernel(
+    place_ref, x_ref, near_ref, far_ref, w_ref, slope_ref, act_ref, xt_ref, at_ref, wide_ref
+):
     wide_ref[...] = jnp.zeros_like(wide_ref)
     for out in range(2):
         for dy in range(3):
@@ -47,7 +54,8 @@
                 start = ((dy + out) * 3 + dx) * C
                 wide_ref[start : start + C, out * C : (out + 1) * C] = w_ref[dy, dx]
     for f in range(2):
-        x = jnp.concatenate([lo_ref[f], x_ref[f], hi_ref[f]], axis=0).reshape(1280, C)
+        lo, hi = sides(place_ref, 1, near_ref[f], far_ref[f])
+        x = jnp.concatenate([lo[None], x_ref[f], hi[None]], axis=0).reshape(1280, C)
         xt_ref[f] = x.T
         pre = mm(row_pairs(jnp.concatenate(columns(x), axis=1)), wide_ref[...])
         sig = 1.0 / (1.0 + jnp.exp(-pre))
@@ -61,12 +69,13 @@
 
 
 def grads_kernel(
-    place_ref, slope_ref, xt_ref, at_ref, cot_ref, prev_ref, next_ref, wt_ref, wd_ref,
+    place_ref, slope_ref, xt_ref, at_ref, cot_ref, near_ref, far_ref, wt_ref, wd_ref,
     gpre_ref, send_ref, keep_ref, mats_ref,
 ):
     first = place_ref[0] == 0
     core = place_ref[1]
-    cot, before, after = (r[...].reshape(1024, C) for r in (cot_ref, prev_ref, next_ref))
+    cot, near, far = (r[...].reshape(1024, C) for r in (cot_ref, near_ref, far_ref))
+    before, after = sides(place_ref, 0, near, far)
     zero = jnp.zeros((C, C), BF16)
     w_pair = jnp.concatenate(
         [
@@ -128,7 +137,7 @@
     keep_ref[...] = mats_ref[:, core]
 
 
-def resid_kernel(x_ref, act_ref, prev_ref, next_ref, wt_ref, resid_ref):
+def resid_kernel(place_ref, x_ref, act_ref, near_ref, far_ref, wt_ref, resid_ref):
     zero = jnp.zeros((C, C), BF16)
     w_time = jnp.concatenate(
         [
@@ -137,8 +146,9 @@
         ],
         axis=1,
     )
-    parts = [prev_ref[...], act_ref[0], act_ref[1], next_ref[...]]
-    mixed = mm(jnp.concatenate([p.reshape(1024, C) for p in parts], axis=1), w_time)
+    parts = [r.reshape(1024, C) for r in (near_ref[...], far_ref[...], act_ref[0], act_ref[1])]
+    before, after = sides(place_ref, 0, parts[0], parts[1])
+    mixed = mm(jnp.concatenate([before, parts[2], parts[3], after], axis=1), w_time)
     for f in range(2):
         total = x_ref[f].astype(F32).reshape(1024, C) + mixed[:, f * C : (f + 1) * C]
         resid_ref[f] = total.astype(BF16).reshape(8, 128, C)
@@ -151,7 +161,10 @@
     out_ref[...] = mm(rows, weights).astype(BF16).reshape(8, 128, C)
 
 
-def features_kernel(gpre_ref, lo_ref, hi_ref, cot_ref, next_ref, w_ref, wd_ref, out_ref, wide_ref):
+def features_kernel(
+    place_ref, gpre_ref, g_near_ref, g_far_ref, cot_ref, near_ref, far_ref, w_ref, wd_ref,
+    out_ref, wide_ref,
+):
     wide_ref[...] = jnp.zeros_like(wide_ref)
     for out in range(2):
         for dy in range(3):
@@ -166,10 +179,12 @@
         ],
         axis=0,
     )
-    cot, after = (r[...].reshape(1024, C) for r in (cot_ref, next_ref))
+    cot, near, far = (r[...].reshape(1024, C) for r in (cot_ref, near_ref, far_ref))
+    after = sides(place_ref, 0, near, far)[1]
     resid = mm_nt(jnp.concatenate([cot, after], axis=1), w_pair)
     for f in range(2):
-        g = jnp.concatenate([lo_ref[f], gpre_ref[f], hi_ref[f]], axis=0).reshape(1280, C)
+        lo, hi = sides(place_ref, 1, g_near_ref[f], g_far_ref[f])
+        g = jnp.concatenate([lo[None], gpre_ref[f], hi[None]], axis=0).reshape(1280, C)
         conv = mm_nt(row_pairs(jnp.concatenate(columns(g), axis=1)), wide_ref[...])
         base = resid[:, f * C : (f + 1) * C].reshape(4, 2, 128, C)
         for out in range(2):
@@ -195,6 +210,16 @@
     )(*args)
 
 
+def gather_kernel(place_ref, mine_ref, other_ref, spatial_ref, time_ref, down_ref):
+    mine = place_ref[1] == 0
+    low = jnp.where(mine, mine_ref[...], other_ref[...]).astype(F32)
+    high = jnp.where(mine, other_ref[...], mine_ref[...]).astype(F32)
+    for first, ref in ((0, spatial_ref), (9, time_ref), (12, down_ref)):
+        count = ref.shape[0]
+        ref[:, :64] = low[first : first + count]
+        ref[:, 64:] = high[first : first + count]
+
+
 def shift(x, axis, by):
     count = lax.axis_size(axis)
     return lax.ppermute(x, axis, [(i, i + by) for i in range(count) if 0 <= i + by < count])
@@ -204,18 +229,15 @@
     return lax.ppermute(x, axis, [(i, i ^ mask) for i in range(lax.axis_size(axis))])
 
 
-def sum_all(send, keep, core):
-    half = keep + swap(send, "core", 1).astype(F32)
-    half = jnp.concatenate([half.astype(BF16), jnp.zeros((1, 64, C), BF16)])
-    got = lax.all_to_all(half, PLANE, 0, 0, tiled=True)
-    total = jnp.sum(got.astype(F32), axis=0)
-    for mask in (1, 2, 4):
-        total = total + swap(total, "z", mask)
-    out = jnp.broadcast_to(total.astype(BF16), (16, 64, C))
-    out = lax.all_to_all(out, PLANE, 0, 0, tiled=True)[:15]
-    other = swap(out, "core", 1)
-    low, high = jnp.where(core == 0, out, other), jnp.where(core == 0, other, out)
-    return jnp.concatenate([low, high], axis=1).astype(F32)
+def swap_far(x, axis):
+    count = lax.axis_size(axis)
+    pairs = [(i, i + 1) for i in range(1, count - 1, 2)]
+    return lax.ppermute(x, axis, pairs + [(b, a) for a, b in pairs])
+
+
+def neighbours(low, high, axis):
+    odd = lax.axis_index(axis) % 2 == 1
+    return swap(jnp.where(odd, low, high), axis, 1), swap_far(jnp.where(odd, high, low), axis)
 
 
 def per_device(features, w_spatial, w_temporal, w_down, cotangent):
@@ -223,40 +245,57 @@
     x, cot = features[0], cotangent[0, 0]
     core = lax.axis_index("core")
     place = jnp.stack([lax.axis_index(time), core]).astype(jnp.int32)
-    lo, hi = shift(x[:, 7:], rows, 1), shift(x[:, :1], rows, -1)
-    cot_prev, cot_next = shift(cot, time, 1), shift(cot, time, -1)
+    cot_near, cot_far = swap(cot, time, 1), swap_far(cot, time)
+    x_near, x_far = neighbours(x[:, 0], x[:, 7], rows)
     slope, act, xt, at = call(
         forward_kernel,
         [((2, 4, 2, 128, C), F32), ((2, 4, 2, 128, C), BF16), ((2, C, 1280), BF16), ((2, C, 1024), BF16)],
-        (x, lo, hi, w_spatial), 9,
-        scratch=[pltpu.VMEM((12 * C, 2 * C), BF16)],
-    )
+        (place, x, x_near, x_far, w_spatial), 9,
+        scratch=[pltpu.VMEM((12 * C, 2 * C), BF16)], scalars=1,
+    )
+    act = act.reshape(2, 8, 128, C)
+    act_near, act_far = neighbours(act[0], act[1], time)
     gpre, send, keep = call(
         grads_kernel,
         [((2, 8, 128, C), BF16), ((15, 64, C), BF16), ((15, 64, C), F32)],
-        (place, slope, xt, at, cot, cot_prev, cot_next, w_temporal, w_down), 21,
+        (place, slope, xt, at, cot, cot_near, cot_far, w_temporal, w_down), 21,
         scratch=[pltpu.VMEM((15, 2, 64, C), F32)], scalars=1,
     )
-    grads = sum_all(send, keep, core)
-    act = act.reshape(2, 8, 128, C)
-    act_prev, act_next = shift(act[1], time, 1), shift(act[0], time, -1)
-    g_lo, g_hi = shift(gpre[:, 7:], rows, 1), shift(gpre[:, :1], rows, -1)
+    half = keep + swap(send, "core", 1).astype(F32)
+    half = jnp.concatenate([half.astype(BF16), jnp.zeros((1, 64, C), BF16)])
+    got = lax.all_to_all(half, PLANE, 0, 0, tiled=True)
+    got, act_near, act_far, gpre = lax.optimization_barrier((got, act_near, act_far, gpre))
+    total = jnp.sum(got.astype(F32), axis=0)
+    total = total + swap(total, "z", 1)
     (resid,) = call(
-        resid_kernel, [((2, 8, 128, C), BF16)], (x, act, act_prev, act_next, w_temporal), 3
-    )
+        resid_kernel, [((2, 8, 128, C), BF16)],
+        (place, x, act, act_near, act_far, w_temporal), 3, scalars=1,
+    )
+    total, resid = lax.optimization_barrier((total, resid))
     before = shift(resid[1], time, 1)
+    g_near, g_far = neighbours(gpre[:, 0], gpre[:, 7], rows)
+    total = total + swap(total, "z", 2)
+    total, g_near, g_far = lax.optimization_barrier((total, g_near, g_far))
     (grad_features,) = call(
         features_kernel, [((2, 4, 2, 128, C), BF16)],
-        (gpre, g_lo, g_hi, cot, cot_next, w_spatial, w_down), 11,
-        scratch=[pltpu.VMEM((2 * C, 12 * C), BF16)],
-    )
+        (place, gpre, g_near, g_far, cot, cot_near, cot_far, w_spatial, w_down), 11,
+        scratch=[pltpu.VMEM((2 * C, 12 * C), BF16)], scalars=1,
+    )
+    total = total + swap(total, "z", 4)
     (down,) = call(down_kernel, [((8, 128, C), BF16)], (resid, before, w_down), 1.5)
+    total, grad_features, down = lax.optimization_barrier((total, grad_features, down))
+    out = jnp.broadcast_to(total.astype(BF16), (16, 64, C))
+    out = lax.all_to_all(out, PLANE, 0, 0, tiled=True)
+    grads = call(
+        gather_kernel, [((n, C, C), F32) for n in (9, 3, 3)], (place, out, swap(out, "core", 1)), 0,
+        scalars=1,
+    )
     return (
         down[None, None],
         grad_features.reshape(1, 2, 8, 128, C),
-        grads[:9].reshape(3, 3, C, C),
-        grads[9:12],
-        grads[12:],
+        grads[0].reshape(3, 3, C, C),
+        grads[1],
+        grads[2],
     )
 
 

time: 94.3 us -> 88.8 us (0.942)
  Pallas kernels: 8.37 us -> 12.2 us
  blocking collectives: 15.8 us -> 12.5 us
  local copies, waits for them, and re-layouts: 4.63 us -> 1.97 us
  starting transfers between devices: 46.9 us -> 44.7 us
    ppermute x9 -> x1, starting transfers between devices: 21.7 us -> 1.44 us  [shift(): lax.ppermute(x, axis, [(i, i + by) for i in range(count) if 0 <= i + by <...]
    ppermute x0 -> x4, starting transfers between devices: none -> 10.7 us  [swap_far(): return lax.ppermute(x, axis, pairs + [(b, a) for a, b in pairs])]
    ppermute x9 -> x1, waiting for transfers between devices: 6.93 us -> 0.01 us  [shift(): lax.ppermute(x, axis, [(i, i + by) for i in range(count) if 0 <= i + by <...]
    all_to_all x1, starting transfers between devices: 4.19 us -> 9.33 us  [per_device(): got = lax.all_to_all(half, PLANE, 0, 0, tiled=True)]
    all_to_all x1, waiting for transfers between devices: 3.77 us -> 7.85 us  [per_device(): got = lax.all_to_all(half, PLANE, 0, 0, tiled=True)]
    pallas_call x5 -> x6, Pallas kernels: 8.37 us -> 12.2 us  [call(): pl.pallas_call(kernel, out_shape=[jax.ShapeDtypeStruct(s, d) for s, d in...]
    all_to_all x1, blocking collectives: 15.8 us -> 12.5 us  [per_device(): out = lax.all_to_all(out, PLANE, 0, 0, tiled=True)]
    slice x5 -> x0, local copies, waits for them, and re-layouts: 2.75 us -> none  [the longest x1 0.96 us: sum_all(): out = lax.all_to_all(out, PLANE, 0, 0, tiled=True)[:15]]
  transfers between devices with their start and end apart: 15 -> 15, of which waited for: 6 -> 6; matrix products, arithmetic and copies ran while one was open for 3% -> 4% of each run, Pallas kernels for 5% -> 6%
where the time goes in v2:
time: 88.8 us; the launch traced here: 88.4 us
  starting transfers between devices  44.7 us (50%)
  waiting for transfers between devices  14.2 us (16%)
  blocking collectives  12.5 us (14%)
  Pallas kernels  12.2 us (14%)
  other arithmetic  2.01 us (2%)
  local copies, waits for them, and re-layouts  1.97 us (2%)
    ppermute x9, starting transfers between devices, swap(): lax.ppermute(x, axis, [(i, i ^ mask) for i in range(lax.axis_size(axis))])  23.2 us
    all_to_all x1, blocking collectives, per_device(): out = lax.all_to_all(out, PLANE, 0, 0, tiled=True)  12.5 us
    pallas_call x6, Pallas kernels, call(): pl.pallas_call(kernel, out_shape=[jax.ShapeDtypeStruct(s, d) for s, d in...  12.2 us
    ppermute x4, starting transfers between devices, swap_far(): return lax.ppermute(x, axis, pairs + [(b, a) for a, b in pairs])  10.7 us
    all_to_all x1, starting transfers between devices, per_device(): got = lax.all_to_all(half, PLANE, 0, 0, tiled=True)  9.33 us
    all_to_all x1, waiting for transfers between devices, per_device(): got = lax.all_to_all(half, PLANE, 0, 0, tiled=True)  7.85 us
    ppermute x9, waiting for transfers between devices, swap(): lax.ppermute(x, axis, [(i, i ^ mask) for i in range(lax.axis_size(axis))])  4.54 us
  transfers between devices with their start and end apart: 15, of which 6 were waited for; matrix products, arithmetic and copies ran while one was open for 4% of the time, Pallas kernels for 6%

profile of v2, /device:TPU:1, one launch (start us, length us, event | category | flops | bytes accessed | tf_op | source)
XLA Modules:
  0.0 88.4 jit_solution(9717550584469296736)
XLA Ops:
  0.6 0.7 collective-permute-start.3
  1.3 5.0 %collective-permute-start.2 = (bf16[8,128,128]{2,1,0:T(8,128)(2,1)}, bf16[8,128,128]{2,1,0:T(8,128)(2,1)S(1)}, u32[]{:S(2)}, u32[]{:S(2)}) collective-permute-start(bf16[8,128,128]{2,1,0:T(8,128)(2,1)} %bitcast.27), channel_id=1, source_target_pairs={{0,8},{8,0},{16,24},{24,16},{32,40},{40,32},{48,56},{56,48},{64,72... | collective-permute-start | bytes 786440 | tf_op jit(solution)/shard_map/ppermute | solution.py:229
  6.3 0.0 copy-start
  6.3 0.0 copy-start.3
  6.3 1.2 %copy.19 = bf16[1,2,8,128,128]{4,3,1,2,0:T(8,128)(2,1)S(1)} copy(bf16[1,2,8,128,128]{4,3,2,1,0:T(8,128)(2,1)} %param.5) | data formatting | bytes 1048576 | tf_op args[0]
  7.5 4.2 %collective-permute-start.1 = (bf16[2,128,128]{2,1,0:T(8,128)(2,1)S(1)}, bf16[2,128,128]{2,1,0:T(8,128)(2,1)S(1)}, u32[]{:S(2)}, u32[]{:S(2)}) collective-permute-start(bf16[2,128,128]{2,1,0:T(8,128)(2,1)S(1)} %get-tuple-element.53), channel_id=1, source_target_pairs={{1,2},{3,4},{5,6},{2,1},{4,3},{6,5},{9,10},{11,12},{13,14},{10,9},... | collective-permute-start | bytes 196616 | tf_op jit(solution)/shard_map/ppermute | solution.py:235
  11.7 0.1 collective-permute-start
  11.8 0.1 pad_add_fusion.place_ref
  11.9 1.8 %collective-permute-done.1.far_ref = bf16[2,128,128]{2,1,0:T(8,128)(2,1)S(1)} collective-permute-done((bf16[2,128,128]{2,1,0:T(8,128)(2,1)S(1)}, bf16[2,128,128]{2,1,0:T(8,128)(2,1)S(1)}, u32[]{:S(2)}, u32[]{:S(2)}) %collective-permute-start.1) | collective-permute-done | bytes 65568 | tf_op jit(solution)/shard_map/ppermute | solution.py:235
  13.7 0.0 collective-permute-done.near_ref
  13.7 0.0 copy-done
  13.7 0.0 copy-done.3
  13.7 0.0 copy-start.1
  13.7 0.0 copy-start.2
  13.7 0.0 copy-start.4
  13.7 2.0 %shard_map.92 = (f32[2,4,2,128,128]{4,3,2,1,0:T(8,128)S(1)}, bf16[2,4,2,128,128]{4,3,2,1,0:T(8,128)(2,1)S(1)}, bf16[2,128,1280]{2,1,0:T(8,128)(2,1)S(1)}, bf16[2,128,1024]{2,1,0:T(8,128)(2,1)S(1)}) custom-call(s32[2]{0:T(128)S(1)} %pad_add_fusion.place_ref, bf16[2,8,128,128]{3,2,1,0:T(8,128)(2,1)S(1)} %bitcast.23, ...), custom_call_target="tpu_custom_call" | custom-call | flops 603979776 | bytes 4000000 | tf_op jit(solution)/shard_map/pallas_call | solution.py:200
  15.8 0.0 collective-permute-done.3.far_ref
  15.8 0.0 copy-start.5
  15.8 1.7 %collective-permute-done.2.near_ref = bf16[8,128,128]{2,1,0:T(8,128)(2,1)S(1)} collective-permute-done((bf16[8,128,128]{2,1,0:T(8,128)(2,1)}, bf16[8,128,128]{2,1,0:T(8,128)(2,1)S(1)}, u32[]{:S(2)}, u32[]{:S(2)}) %collective-permute-start.2) | collective-permute-done | bytes 262176 | tf_op jit(solution)/shard_map/ppermute | solution.py:229
  17.5 0.0 copy-start.7
  17.5 0.0 copy-done.1
  17.5 0.0 copy-done.2
  17.5 0.0 copy-done.4
  17.5 4.1 %shard_map.93 = (bf16[2,8,128,128]{3,2,1,0:T(8,128)(2,1)S(1)}, bf16[15,64,128]{2,1,0:T(8,128)(2,1)}, f32[15,64,128]{2,1,0:T(8,128)S(1)}) custom-call(s32[2]{0:T(128)S(1)} %pad_add_fusion.place_ref, f32[2,4,2,128,128]{4,3,2,1,0:T(8,128)S(1)} %get-tuple-element.27.slope_ref, bf16[2,128,1280]{2,1,0:T(8,128)(2,1)S(1)} %get-tuple-element.28.xt_ref, ...), custom_call_target="tpu_custom_call" | custom-call | flops 1409286144 | bytes 4000000 | tf_op jit(solution)/shard_map/pallas_call | solution.py:200
  21.6 0.0 copy-done.5
  21.6 0.0 copy-done.7
  21.6 0.5 collective-permute-start.4
  22.1 0.8 broadcast_select_fusion
  22.9 2.1 %collective-permute-start.5 = (bf16[8,128,128]{2,1,0:T(8,128)(2,1)}, bf16[8,128,128]{2,1,0:T(8,128)(2,1)S(1)}, u32[]{:S(2)}, u32[]{:S(2)}) collective-permute-start(bf16[8,128,128]{2,1,0:T(8,128)(2,1)} %bitcast.7), channel_id=1, source_target_pairs={{0,8},{8,0},{16,24},{24,16},{32,40},{40,32},{48,56},{56,48},{64,72... | collective-permute-start | bytes 786440 | tf_op jit(solution)/shard_map/ppermute | solution.py:229
  25.0 0.7 collective-permute-start.6
  25.7 0.0 collective-permute-done.4
  25.7 1.0 %add_convert_fusion = bf16[15,64,128]{2,1,0:T(8,128)(2,1)S(1)} fusion(f32[15,64,128]{2,1,0:T(8,128)S(1)} %get-tuple-element.30, bf16[15,64,128]{2,1,0:T(8,128)(2,1)} %collective-permute-done.4), kind=kLoop, calls=%fused_computation.2 | loop fusion | flops 368640 | bytes 983040 | tf_op jit(solution)/shard_map/convert_element_type | solution.py:265
  26.7 0.7 concatenate.3
  27.4 9.3 %all-to-all-start = ((bf16[16,64,128]{2,1,0:T(8,128)(2,1)}), bf16[16,64,128]{2,1,0:T(8,128)(2,1)S(1)}, u32[]{:S(2)}, u32[]{:S(2)}) async-start(bf16[16,64,128]{2,1,0:T(8,128)(2,1)} %concatenate.3), calls=%async_computation | async-start | bytes 524288 | tf_op jit(solution)/shard_map/all_to_all | solution.py:266
  36.8 0.0 collective-permute-done.5.near_ref
  36.8 0.0 collective-permute-done.6.far_ref
  36.8 7.9 %all-to-all-done = bf16[16,64,128]{2,1,0:T(8,128)(2,1)S(1)} async-done(((bf16[16,64,128]{2,1,0:T(8,128)(2,1)}), bf16[16,64,128]{2,1,0:T(8,128)(2,1)S(1)}, u32[]{:S(2)}, u32[]{:S(2)}) %all-to-all-start) | async-done | bytes 262176 | tf_op jit(solution)/shard_map/all_to_all | solution.py:266
  44.7 1.7 %collective-permute-start.7 = (f32[64,128]{1,0:T(8,128)S(1)}, f32[64,128]{1,0:T(8,128)S(1)}, u32[]{:S(2)}, u32[]{:S(2)}) collective-permute-start(f32[64,128]{1,0:T(8,128)S(1)} %convert_reduce_fusion), channel_id=1, source_target_pairs={{0,16},{16,0},{32,48},{48,32},{64,80},{80,64},{96,112},{112,96},{1... | collective-permute-start | bytes 98312 | tf_op jit(solution)/shard_map/ppermute | solution.py:229
  46.4 1.0 %shard_map.94.resid_ref = bf16[2,8,128,128]{3,2,1,0:T(8,128)(2,1)S(1)} custom-call(s32[2]{0:T(128)S(1)} %pad_add_fusion.place_ref, bf16[2,8,128,128]{3,2,1,0:T(8,128)(2,1)S(1)} %bitcast.24, bf16[2,8,128,128]{3,2,1,0:T(8,128)(2,1)S(1)} %bitcast.25, bf16[8,128,128]{2,1,0:T(8,128)(2,1)S(1)} %collective-permute-done.5.near_ref, ...), custom_call_target="tpu_custom_call" | custom-call | flops 201326592 | bytes 4000000 | tf_op jit(solution)/shard_map/pallas_call | solution.py:200
  47.4 0.3 collective-permute-done.7
  47.7 0.0 copy-start.8
  47.8 0.0 copy-start.6
  47.8 1.4 %collective-permute-start.12 = (bf16[8,128,128]{2,1,0:T(8,128)(2,1)S(1)}, bf16[8,128,128]{2,1,0:T(8,128)(2,1)S(1)}, u32[]{:S(2)}, u32[]{:S(2)}) collective-permute-start(bf16[8,128,128]{2,1,0:T(8,128)(2,1)S(1)} %slice_bitcast_fusion), channel_id=1, source_target_pairs={{0,8},{8,16},{16,24},{24,32},{32,40},{40,48},{48,56},{56,64},{64,7... | collective-permute-start | bytes 786440 | tf_op jit(solution)/shard_map/ppermute | solution.py:225
  49.3 5.2 %collective-permute-start.10 = (bf16[2,128,128]{2,1,0:T(8,128)(2,1)S(1)}, bf16[2,128,128]{2,1,0:T(8,128)(2,1)S(1)}, u32[]{:S(2)}, u32[]{:S(2)}) collective-permute-start(bf16[2,128,128]{2,1,0:T(8,128)(2,1)S(1)} %get-tuple-element.49), channel_id=1, source_target_pairs={{1,2},{3,4},{5,6},{2,1},{4,3},{6,5},{9,10},{11,12},{13,14},{10,9},... | collective-permute-start | bytes 196616 | tf_op jit(solution)/shard_map/ppermute | solution.py:235
  54.4 0.1 collective-permute-start.9
  54.5 4.6 %collective-permute-start.8 = (f32[64,128]{1,0:T(8,128)S(1)}, f32[64,128]{1,0:T(8,128)S(1)}, u32[]{:S(2)}, u32[]{:S(2)}) collective-permute-start(f32[64,128]{1,0:T(8,128)S(1)} %add.35), channel_id=1, source_target_pairs={{0,32},{16,48},{32,0},{48,16},{64,96},{80,112},{96,64},{112,80},{1... | collective-permute-start | bytes 98312 | tf_op jit(solution)/shard_map/ppermute | solution.py:229
  59.1 1.3 %collective-permute-done.8 = f32[64,128]{1,0:T(8,128)S(1)} collective-permute-done((f32[64,128]{1,0:T(8,128)S(1)}, f32[64,128]{1,0:T(8,128)S(1)}, u32[]{:S(2)}, u32[]{:S(2)}) %collective-permute-start.8) | collective-permute-done | bytes 32800 | tf_op jit(solution)/shard_map/ppermute | solution.py:229
  60.4 0.0 collective-permute-done.10.g_far_ref
  60.4 0.0 collective-permute-done.9.g_near_ref
  60.4 4.6 %collective-permute-start.11 = (f32[64,128]{1,0:T(8,128)S(1)}, f32[64,128]{1,0:T(8,128)S(1)}, u32[]{:S(2)}, u32[]{:S(2)}) collective-permute-start(f32[64,128]{1,0:T(8,128)S(1)} %add.36), channel_id=1, source_target_pairs={{0,64},{16,80},{32,96},{48,112},{64,0},{80,16},{96,32},{112,48},{1... | collective-permute-start | bytes 98312 | tf_op jit(solution)/shard_map/ppermute | solution.py:229
  65.0 0.0 copy-done.8
  65.0 0.0 copy-done.6
  65.0 2.5 %shard_map.95 = bf16[2,4,2,128,128]{4,3,2,1,0:T(8,128)(2,1)} custom-call(s32[2]{0:T(128)S(1)} %pad_add_fusion.place_ref, bf16[2,8,128,128]{3,2,1,0:T(8,128)(2,1)S(1)} %get-tuple-element.38.gpre_ref, bf16[2,128,128]{2,1,0:T(8,128)(2,1)S(1)} %collective-permute-done.9.g_near_ref, bf16[2,128,128]{2,1,0:T(8,128)(2,1)S(1)} %collective-permute-done.10.g_far_ref, ...), custom_call_target="tpu_custom_call" | custom-call | flops 738197504 | bytes 4000000 | tf_op jit(solution)/shard_map/pallas_call | solution.py:200
  67.5 0.0 collective-permute-done.11
  67.5 0.0 collective-permute-done.12.before_ref
  67.5 1.1 %shard_map.96 = bf16[8,128,128]{2,1,0:T(8,128)(2,1)} custom-call(bf16[2,8,128,128]{3,2,1,0:T(8,128)(2,1)S(1)} %shard_map.94.resid_ref, bf16[8,128,128]{2,1,0:T(8,128)(2,1)S(1)} %collective-permute-done.12.before_ref, bf16[3,128,128]{2,1,0:T(8,128)(2,1)S(1)} %copy-done.2), custom_call_target="tpu_custom_call" | custom-call | flops 100663296 | bytes 4000000 | tf_op jit(solution)/shard_map/pallas_call | solution.py:200
  68.7 12.5 %all_to_all.10.mine_ref = bf16[16,64,128]{2,1,0:T(8,128)(2,1)S(1)} all-to-all(bf16[16,64,128]{2,1,0:T(8,128)(2,1)S(1)} %broadcast_in_dim.8), channel_id=1, replica_groups=mesh['yh'=2,'z'=8,'yl'=2,'x'=4,'core'=2] {'yh','yl','x'}, dimensions={0} | all-to-all | bytes 524288 | tf_op jit(solution)/shard_map/all_to_all | solution.py:288
  81.2 4.6 %collective-permute-start.13 = (bf16[16,64,128]{2,1,0:T(8,128)(2,1)S(1)}, bf16[16,64,128]{2,1,0:T(8,128)(2,1)S(1)}, u32[]{:S(2)}, u32[]{:S(2)}) collective-permute-start(bf16[16,64,128]{2,1,0:T(8,128)(2,1)S(1)} %all_to_all.10.mine_ref), channel_id=1, source_target_pairs={{0,1},{1,0},{2,3},{3,2},{4,5},{5,4},{6,7},{7,6},{8,9},{9,8},{10,11... | collective-permute-start | bytes 786440 | tf_op jit(solution)/shard_map/ppermute | solution.py:229
  85.8 1.2 %collective-permute-done.13.other_ref = bf16[16,64,128]{2,1,0:T(8,128)(2,1)S(1)} collective-permute-done((bf16[16,64,128]{2,1,0:T(8,128)(2,1)S(1)}, bf16[16,64,128]{2,1,0:T(8,128)(2,1)S(1)}, u32[]{:S(2)}, u32[]{:S(2)}) %collective-permute-start.13) | collective-permute-done | bytes 262176 | tf_op jit(solution)/shard_map/ppermute | solution.py:229
  86.9 1.5 %shard_map.97 = (f32[9,128,128]{2,1,0:T(8,128)}, f32[3,128,128]{2,1,0:T(8,128)}, f32[3,128,128]{2,1,0:T(8,128)}) custom-call(s32[2]{0:T(128)S(1)} %pad_add_fusion.place_ref, bf16[16,64,128]{2,1,0:T(8,128)(2,1)S(1)} %all_to_all.10.mine_ref, bf16[16,64,128]{2,1,0:T(8,128)(2,1)S(1)} %collective-permute-done.13.other_ref), custom_call_target="tpu_custom_call" | custom-call | bytes 4000000 | tf_op jit(solution)/shard_map/pallas_call | solution.py:200
  (8 shorter events, 0.2 us)
Async XLA Ops:
  0.6 15.1 %collective-permute-start.3 = (bf16[8,128,128]{2,1,0:T(8,128)(2,1)}, bf16[8,128,128]{2,1,0:T(8,128)(2,1)S(1)}, u32[]{:S(2)}, u32[]{:S(2)}) collective-permute-start(bf16[8,128,128]{2,1,0:T(8,128)(2,1)} %bitcast.26), channel_id=1, source_target_pairs={{8,16},{24,32},{40,48},{56,64},{72,80},{88,96},{104,112},{16,8},{3... | collective-permute-start | bytes 786440 | tf_op jit(solution)/shard_map/ppermute | solution.py:235
  1.3 16.2 %collective-permute-start.2 = (bf16[8,128,128]{2,1,0:T(8,128)(2,1)}, bf16[8,128,128]{2,1,0:T(8,128)(2,1)S(1)}, u32[]{:S(2)}, u32[]{:S(2)}) collective-permute-start(bf16[8,128,128]{2,1,0:T(8,128)(2,1)} %bitcast.27), channel_id=1, source_target_pairs={{0,8},{8,0},{16,24},{24,16},{32,40},{40,32},{48,56},{56,48},{64,72... | collective-permute-start | bytes 786440 | tf_op jit(solution)/shard_map/ppermute | solution.py:229
  6.3 7.4 %copy-start = (bf16[1,2,8,128,128]{4,3,2,1,0:T(8,128)(2,1)S(1)}, bf16[1,2,8,128,128]{4,3,2,1,0:T(8,128)(2,1)}, u32[]{:S(2)}) copy-start(bf16[1,2,8,128,128]{4,3,2,1,0:T(8,128)(2,1)} %param.5) | copy-start | bytes 1572868
  6.3 7.4 %copy-start.3 = (bf16[3,3,128,128]{3,2,1,0:T(8,128)(2,1)S(1)}, bf16[3,3,128,128]{3,2,1,0:T(8,128)(2,1)}, u32[]{:S(2)}) copy-start(bf16[3,3,128,128]{3,2,1,0:T(8,128)(2,1)} %w_ref.3) | copy-start | bytes 884740
  7.5 6.2 %collective-permute-start.1 = (bf16[2,128,128]{2,1,0:T(8,128)(2,1)S(1)}, bf16[2,128,128]{2,1,0:T(8,128)(2,1)S(1)}, u32[]{:S(2)}, u32[]{:S(2)}) collective-permute-start(bf16[2,128,128]{2,1,0:T(8,128)(2,1)S(1)} %get-tuple-element.53), channel_id=1, source_target_pairs={{1,2},{3,4},{5,6},{2,1},{4,3},{6,5},{9,10},{11,12},{13,14},{10,9},... | collective-permute-start | bytes 196616 | tf_op jit(solution)/shard_map/ppermute | solution.py:235
  11.7 1.9 %collective-permute-start = (bf16[2,128,128]{2,1,0:T(8,128)(2,1)S(1)}, bf16[2,128,128]{2,1,0:T(8,128)(2,1)S(1)}, u32[]{:S(2)}, u32[]{:S(2)}) collective-permute-start(bf16[2,128,128]{2,1,0:T(8,128)(2,1)S(1)} %get-tuple-element.54), channel_id=1, source_target_pairs={{0,1},{1,0},{2,3},{3,2},{4,5},{5,4},{6,7},{7,6},{8,9},{9,8},{10,11... | collective-permute-start | bytes 196616 | tf_op jit(solution)/shard_map/ppermute | solution.py:229
  13.7 3.9 %copy-start.1 = (bf16[3,128,128]{2,1,0:T(8,128)(2,1)S(1)}, bf16[3,128,128]{2,1,0:T(8,128)(2,1)}, u32[]{:S(2)}) copy-start(bf16[3,128,128]{2,1,0:T(8,128)(2,1)} %wt_ref.3) | copy-start | bytes 294916
  13.7 3.8 %copy-start.2 = (bf16[3,128,128]{2,1,0:T(8,128)(2,1)S(1)}, bf16[3,128,128]{2,1,0:T(8,128)(2,1)}, u32[]{:S(2)}) copy-start(bf16[3,128,128]{2,1,0:T(8,128)(2,1)} %wd_ref.5) | copy-start | bytes 294916
  13.7 3.8 %copy-start.4 = (bf16[1,1,8,128,128]{4,3,2,1,0:T(8,128)(2,1)S(1)}, bf16[1,1,8,128,128]{4,3,2,1,0:T(8,128)(2,1)}, u32[]{:S(2)}) copy-start(bf16[1,1,8,128,128]{4,3,2,1,0:T(8,128)(2,1)} %param.9) | copy-start | bytes 786436
  15.8 5.8 %copy-start.5 = (bf16[8,128,128]{2,1,0:T(8,128)(2,1)}, bf16[8,128,128]{2,1,0:T(8,128)(2,1)S(1)}, u32[]{:S(2)}) copy-start(bf16[8,128,128]{2,1,0:T(8,128)(2,1)S(1)} %collective-permute-done.3.far_ref) | copy-start | bytes 786436
  17.5 4.1 %copy-start.7 = (bf16[8,128,128]{2,1,0:T(8,128)(2,1)}, bf16[8,128,128]{2,1,0:T(8,128)(2,1)S(1)}, u32[]{:S(2)}) copy-start(bf16[8,128,128]{2,1,0:T(8,128)(2,1)S(1)} %collective-permute-done.2.near_ref) | copy-start | bytes 786436
  21.6 4.1 %collective-permute-start.4 = (bf16[15,64,128]{2,1,0:T(8,128)(2,1)}, bf16[15,64,128]{2,1,0:T(8,128)(2,1)}, u32[]{:S(2)}, u32[]{:S(2)}) collective-permute-start(bf16[15,64,128]{2,1,0:T(8,128)(2,1)} %get-tuple-element.31), channel_id=1, source_target_pairs={{0,1},{1,0},{2,3},{3,2},{4,5},{5,4},{6,7},{7,6},{8,9},{9,8},{10,11... | collective-permute-start | bytes 737288 | tf_op jit(solution)/shard_map/ppermute | solution.py:229
  22.9 13.8 %collective-permute-start.5 = (bf16[8,128,128]{2,1,0:T(8,128)(2,1)}, bf16[8,128,128]{2,1,0:T(8,128)(2,1)S(1)}, u32[]{:S(2)}, u32[]{:S(2)}) collective-permute-start(bf16[8,128,128]{2,1,0:T(8,128)(2,1)} %bitcast.7), channel_id=1, source_target_pairs={{0,8},{8,0},{16,24},{24,16},{32,40},{40,32},{48,56},{56,48},{64,72... | collective-permute-start | bytes 786440 | tf_op jit(solution)/shard_map/ppermute | solution.py:229
  25.0 11.8 %collective-permute-start.6 = (bf16[8,128,128]{2,1,0:T(8,128)(2,1)}, bf16[8,128,128]{2,1,0:T(8,128)(2,1)S(1)}, u32[]{:S(2)}, u32[]{:S(2)}) collective-permute-start(bf16[8,128,128]{2,1,0:T(8,128)(2,1)} %bitcast.8), channel_id=1, source_target_pairs={{8,16},{24,32},{40,48},{56,64},{72,80},{88,96},{104,112},{16,8},{3... | collective-permute-start | bytes 786440 | tf_op jit(solution)/shard_map/ppermute | solution.py:235
  27.4 17.2 %all-to-all-start = ((bf16[16,64,128]{2,1,0:T(8,128)(2,1)}), bf16[16,64,128]{2,1,0:T(8,128)(2,1)S(1)}, u32[]{:S(2)}, u32[]{:S(2)}) async-start(bf16[16,64,128]{2,1,0:T(8,128)(2,1)} %concatenate.3), calls=%async_computation | async-start | bytes 524288 | tf_op jit(solution)/shard_map/all_to_all | solution.py:266
  44.7 3.0 %collective-permute-start.7 = (f32[64,128]{1,0:T(8,128)S(1)}, f32[64,128]{1,0:T(8,128)S(1)}, u32[]{:S(2)}, u32[]{:S(2)}) collective-permute-start(f32[64,128]{1,0:T(8,128)S(1)} %convert_reduce_fusion), channel_id=1, source_target_pairs={{0,16},{16,0},{32,48},{48,32},{64,80},{80,64},{96,112},{112,96},{1... | collective-permute-start | bytes 98312 | tf_op jit(solution)/shard_map/ppermute | solution.py:229
  47.7 17.2 %copy-start.8 = (bf16[8,128,128]{2,1,0:T(8,128)(2,1)S(1)}, bf16[8,128,128]{2,1,0:T(8,128)(2,1)}, u32[]{:S(2)}) copy-start(bf16[8,128,128]{2,1,0:T(8,128)(2,1)} %copy-done.7) | copy-start | bytes 786436
  47.8 17.2 %copy-start.6 = (bf16[8,128,128]{2,1,0:T(8,128)(2,1)S(1)}, bf16[8,128,128]{2,1,0:T(8,128)(2,1)}, u32[]{:S(2)}) copy-start(bf16[8,128,128]{2,1,0:T(8,128)(2,1)} %copy-done.5) | copy-start | bytes 786436
  47.8 19.8 %collective-permute-start.12 = (bf16[8,128,128]{2,1,0:T(8,128)(2,1)S(1)}, bf16[8,128,128]{2,1,0:T(8,128)(2,1)S(1)}, u32[]{:S(2)}, u32[]{:S(2)}) collective-permute-start(bf16[8,128,128]{2,1,0:T(8,128)(2,1)S(1)} %slice_bitcast_fusion), channel_id=1, source_target_pairs={{0,8},{8,16},{16,24},{24,32},{32,40},{40,48},{48,56},{56,64},{64,7... | collective-permute-start | bytes 786440 | tf_op jit(solution)/shard_map/ppermute | solution.py:225
  49.3 11.1 %collective-permute-start.10 = (bf16[2,128,128]{2,1,0:T(8,128)(2,1)S(1)}, bf16[2,128,128]{2,1,0:T(8,128)(2,1)S(1)}, u32[]{:S(2)}, u32[]{:S(2)}) collective-permute-start(bf16[2,128,128]{2,1,0:T(8,128)(2,1)S(1)} %get-tuple-element.49), channel_id=1, source_target_pairs={{1,2},{3,4},{5,6},{2,1},{4,3},{6,5},{9,10},{11,12},{13,14},{10,9},... | collective-permute-start | bytes 196616 | tf_op jit(solution)/shard_map/ppermute | solution.py:235
  54.4 6.0 %collective-permute-start.9 = (bf16[2,128,128]{2,1,0:T(8,128)(2,1)S(1)}, bf16[2,128,128]{2,1,0:T(8,128)(2,1)S(1)}, u32[]{:S(2)}, u32[]{:S(2)}) collective-permute-start(bf16[2,128,128]{2,1,0:T(8,128)(2,1)S(1)} %get-tuple-element.50), channel_id=1, source_target_pairs={{0,1},{1,0},{2,3},{3,2},{4,5},{5,4},{6,7},{7,6},{8,9},{9,8},{10,11... | collective-permute-start | bytes 196616 | tf_op jit(solution)/shard_map/ppermute | solution.py:229
  54.5 5.9 %collective-permute-start.8 = (f32[64,128]{1,0:T(8,128)S(1)}, f32[64,128]{1,0:T(8,128)S(1)}, u32[]{:S(2)}, u32[]{:S(2)}) collective-permute-start(f32[64,128]{1,0:T(8,128)S(1)} %add.35), channel_id=1, source_target_pairs={{0,32},{16,48},{32,0},{48,16},{64,96},{80,112},{96,64},{112,80},{1... | collective-permute-start | bytes 98312 | tf_op jit(solution)/shard_map/ppermute | solution.py:229
  60.4 7.1 %collective-permute-start.11 = (f32[64,128]{1,0:T(8,128)S(1)}, f32[64,128]{1,0:T(8,128)S(1)}, u32[]{:S(2)}, u32[]{:S(2)}) collective-permute-start(f32[64,128]{1,0:T(8,128)S(1)} %add.36), channel_id=1, source_target_pairs={{0,64},{16,80},{32,96},{48,112},{64,0},{80,16},{96,32},{112,48},{1... | collective-permute-start | bytes 98312 | tf_op jit(solution)/shard_map/ppermute | solution.py:229
  81.2 5.7 %collective-permute-start.13 = (bf16[16,64,128]{2,1,0:T(8,128)(2,1)S(1)}, bf16[16,64,128]{2,1,0:T(8,128)(2,1)S(1)}, u32[]{:S(2)}, u32[]{:S(2)}) collective-permute-start(bf16[16,64,128]{2,1,0:T(8,128)(2,1)S(1)} %all_to_all.10.mine_ref), channel_id=1, source_target_pairs={{0,1},{1,0},{2,3},{3,2},{4,5},{5,4},{6,7},{7,6},{8,9},{9,8},{10,11... | collective-permute-start | bytes 786440 | tf_op jit(solution)/shard_map/ppermute | solution.py:229

commit v3 on v2

v3 whole, which is shorter than its diff:
```python
import jax
import jax.numpy as jnp
from jax import lax
from jax.experimental import pallas as pl
from jax.experimental.pallas import tpu as pltpu
from jax.sharding import Mesh, PartitionSpec as P

F32, BF16 = jnp.float32, jnp.bfloat16
C = 128
PLANE = ("yh", "yl", "x")


def mm(a, b):
    return lax.dot_general(a, b, (((1,), (0,)), ((), ())), preferred_element_type=F32)


def mm_nt(a, b):
    return lax.dot_general(a, b, (((1,), (1,)), ((), ())), preferred_element_type=F32)


def mm_tn(a, b):
    return lax.dot_general(a, b, (((0,), (0,)), ((), ())), preferred_element_type=F32)


def columns(x):
    wide = x.astype(F32)
    count = wide.shape[0]
    col = lax.broadcasted_iota(jnp.int32, wide.shape, 0) % 128
    before = jnp.where(col == 0, 0.0, pltpu.roll(wide, 1, 0)).astype(BF16)
    after = jnp.where(col == 127, 0.0, pltpu.roll(wide, count - 1, 0)).astype(BF16)
    return before, x, after


def row_pairs(cat):
    depth = cat.shape[1]
    rows = cat.reshape(5, 2, 128, depth)
    even, odd = rows[:, 0], rows[:, 1]
    parts = [even[0:4], odd[0:4], even[1:5], odd[1:5]]
    return jnp.concatenate([p.reshape(512, depth) for p in parts], axis=1)


def frame_index():
    return lax.axis_index("z") * 2 + lax.axis_index("yl")


def sort_sides(odd, near_ref, far_ref, before_ref, after_ref):
    @pl.when(odd)
    def _():
        before_ref[...] = near_ref[...]
        after_ref[...] = far_ref[...]

    @pl.when(jnp.logical_not(odd))
    def _():
        before_ref[...] = far_ref[...]
        after_ref[...] = near_ref[...]


def pick_kernel(low_ref, high_ref, near_ref, far_ref):
    sort_sides(lax.axis_index("core") == 1, low_ref, high_ref, near_ref, far_ref)


def forward_kernel(
    x_ref, near_ref, far_ref, w_ref, wt_ref, wd_ref,
    slope_ref, act_ref, xt_ref, at_ref, to_near_ref, to_far_ref, wide_ref, rows_ref,
):
    wide_ref[...] = jnp.zeros_like(wide_ref)
    for out in range(2):
        for dy in range(3):
            for dx in range(3):
                start = ((dy + out) * 3 + dx) * C
                wide_ref[start : start + C, out * C : (out + 1) * C] = w_ref[dy, dx]
    sort_sides(lax.axis_index("core") == 1, near_ref, far_ref, rows_ref.at[:, 0], rows_ref.at[:, 9])
    rows_ref[:, 1:9] = x_ref[...]
    for f in range(2):
        x = rows_ref[f].reshape(1280, C)
        xt_ref[f] = x.T
        pre = mm(row_pairs(jnp.concatenate(columns(x), axis=1)), wide_ref[...])
        sig = 1.0 / (1.0 + jnp.exp(-pre))
        act = (pre * sig).astype(BF16)
        slope = sig * (1.0 + pre * (1.0 - sig))
        for out in range(2):
            part = slice(out * C, (out + 1) * C)
            act_ref[f, :, out] = act[:, part].reshape(4, 128, C)
            slope_ref[f, :, out] = slope[:, part].reshape(4, 128, C)
        at_ref[f] = act_ref[f].reshape(1024, C).T
    zero = jnp.zeros((C, C), BF16)
    a0, a1 = act_ref[0].reshape(1024, C), act_ref[1].reshape(1024, C)
    w_time = jnp.concatenate(
        [
            jnp.concatenate([wt_ref[0], zero], axis=1),
            jnp.concatenate([wt_ref[1], wt_ref[0]], axis=1),
        ],
        axis=0,
    )
    mixed = mm(jnp.concatenate([a0, a1], axis=1), w_time)
    last = (x_ref[1].reshape(1024, C).astype(F32) + mixed[:, :C]).astype(BF16)
    both = jnp.concatenate([last, mixed[:, C:].astype(BF16)], axis=1)
    ahead = mm(both, jnp.concatenate([wd_ref[0], wd_ref[1]], axis=0)).astype(BF16)
    odd = lax.axis_index("yl") == 1

    @pl.when(odd)
    def _():
        to_near_ref[...] = a0.reshape(8, 128, C)
        to_far_ref[...] = ahead.reshape(8, 128, C)

    @pl.when(jnp.logical_not(odd))
    def _():
        to_near_ref[...] = ahead.reshape(8, 128, C)
        to_far_ref[...] = a0.reshape(8, 128, C)


def grads_kernel(
    slope_ref, xt_ref, at_ref, cot_ref, near_ref, far_ref, wt_ref, wd_ref,
    gpre_ref, to_near_ref, to_far_ref, send_ref, keep_ref, mats_ref, before_ref, after_ref,
):
    first = frame_index() == 0
    core = lax.axis_index("core")
    sort_sides(lax.axis_index("yl") == 1, near_ref, far_ref, before_ref, after_ref)
    cot, before, after = (r[...].reshape(1024, C) for r in (cot_ref, before_ref, after_ref))
    zero = jnp.zeros((C, C), BF16)
    w_pair = jnp.concatenate(
        [
            jnp.concatenate([wd_ref[2], wd_ref[0]], axis=1),
            jnp.concatenate([zero, wd_ref[1]], axis=1),
        ],
        axis=0,
    )
    low = mm_nt(jnp.concatenate([before, cot], axis=1), w_pair).astype(BF16)
    high = mm_nt(jnp.concatenate([cot, after], axis=1), w_pair).astype(BF16)
    g_m1 = jnp.where(first, jnp.zeros_like(low[:, :C]), low[:, :C])
    g_0, g_1, g_2 = low[:, C:], high[:, :C], high[:, C:]
    w_time = jnp.concatenate(
        [
            jnp.concatenate([wt_ref[2], wt_ref[1], wt_ref[0], zero], axis=1),
            jnp.concatenate([zero, wt_ref[2], wt_ref[1], wt_ref[0]], axis=1),
        ],
        axis=0,
    )
    g_act = mm_nt(jnp.concatenate([g_m1, g_0, g_1, g_2], axis=1), w_time)
    spatial = None
    for f in range(2):
        gp = (g_act[:, f * C : (f + 1) * C] * slope_ref[f].reshape(1024, C)).astype(BF16)
        gpre_ref[f] = gp.reshape(8, 128, C)
        behind, here, ahead = columns(gp)
        shifted = jnp.concatenate([ahead, here, behind], axis=1)
        xt = jnp.concatenate([xt_ref[f, :, dy * 128 : dy * 128 + 1024] for dy in range(3)], axis=0)
        term = mm(xt, shifted)
        spatial = term if spatial is None else spatial + term
    row = 7 * (1 - core)
    for f in range(2):
        to_near_ref[f] = gpre_ref[f, row]
        to_far_ref[f] = gpre_ref[f, 7 - row]
    for dy in range(3):
        for dx in range(3):
            mats_ref[dy * 3 + dx] = spatial[dy * C : (dy + 1) * C, dx * C : (dx + 1) * C].reshape(2, 64, C)
    a0, a1 = at_ref[0], at_ref[1]
    x0, x1 = xt_ref[0, :, 128:1152], xt_ref[1, :, 128:1152]
    time = mm(a0, jnp.concatenate([g_1, g_0, g_m1], axis=1))
    time = time + mm(a1, jnp.concatenate([g_2, g_1, g_0], axis=1))
    for k in range(3):
        mats_ref[9 + k] = time[:, k * C : (k + 1) * C].reshape(2, 64, C)
    both = mm(
        jnp.concatenate([a0, a1, x0, x1], axis=0), jnp.concatenate([cot, after], axis=1)
    )
    tail = mm(a0, before)
    m_0, m_1 = both[0:128, :C], both[128:256, :C]
    m_m2, m_m1 = both[0:128, C:], both[128:256, C:]
    skip = jnp.where(first, jnp.zeros_like(m_0), m_0)
    kinds = (
        (both[384:512, C:], (m_m2, m_m1, skip)),
        (both[256:384, :C], (m_m1, m_0, m_1)),
        (both[384:512, :C], (m_0, m_1, tail)),
    )
    for k, (base, terms) in enumerate(kinds):
        total = base
        for tap, m in enumerate(terms):
            top = m.astype(BF16)
            rest = (m - top.astype(F32)).astype(BF16)
            total = total + mm_tn(wt_ref[tap], top) + mm_tn(wt_ref[tap], rest)
        mats_ref[12 + k] = total.reshape(2, 64, C)
    send_ref[...] = mats_ref[:, 1 - core].astype(BF16)
    keep_ref[...] = mats_ref[:, core]


def merge_kernel(keep_ref, got_ref, out_ref):
    out_ref[:15] = (keep_ref[...] + got_ref[...].astype(F32)).astype(BF16)
    out_ref[15] = jnp.zeros((64, C), BF16)


def down_kernel(x_ref, act_ref, near_ref, far_ref, wt_ref, wd_ref, out_ref, ahead_ref, after_ref):
    sort_sides(lax.axis_index("yl") == 1, near_ref, far_ref, ahead_ref, after_ref)
    zero = jnp.zeros((C, C), BF16)
    first = jnp.where(frame_index() == 0, zero, wt_ref[2])
    w_time = jnp.concatenate(
        [
            jnp.concatenate([first, wt_ref[1], wt_ref[0]], axis=1),
            jnp.concatenate([zero, wt_ref[2], wt_ref[1]], axis=1),
            jnp.concatenate([zero, zero, wt_ref[2]], axis=1),
        ],
        axis=0,
    )
    parts = [act_ref[0], act_ref[1], after_ref[...]]
    mixed = mm(jnp.concatenate([p.reshape(1024, C) for p in parts], axis=1), w_time)
    resid = [mixed[:, :C].astype(BF16)]
    for f in range(2):
        total = x_ref[f].astype(F32).reshape(1024, C) + mixed[:, (f + 1) * C : (f + 2) * C]
        resid.append(total.astype(BF16))
    weights = jnp.concatenate([wd_ref[0], wd_ref[1], wd_ref[2]], axis=0)
    down = mm(jnp.concatenate(resid, axis=1), weights)
    down = down + ahead_ref[...].reshape(1024, C).astype(F32)
    out_ref[...] = down.astype(BF16).reshape(8, 128, C)


def features_kernel(
    gpre_ref, g_near_ref, g_far_ref, cot_ref, near_ref, far_ref, w_ref, wd_ref,
    out_ref, wide_ref, rows_ref, before_ref, after_ref,
):
    wide_ref[...] = jnp.zeros_like(wide_ref)
    for out in range(2):
        for dy in range(3):
            for dx in range(3):
                start = ((dy + out) * 3 + dx) * C
                wide_ref[out * C : (out + 1) * C, start : start + C] = w_ref[2 - dy, 2 - dx]
    zero = jnp.zeros((C, C), BF16)
    w_pair = jnp.concatenate(
        [
            jnp.concatenate([wd_ref[1], zero], axis=1),
            jnp.concatenate([wd_ref[2], wd_ref[0]], axis=1),
        ],
        axis=0,
    )
    sort_sides(lax.axis_index("yl") == 1, near_ref, far_ref, before_ref, after_ref)
    sort_sides(lax.axis_index("core") == 1, g_near_ref, g_far_ref, rows_ref.at[:, 0], rows_ref.at[:, 9])
    rows_ref[:, 1:9] = gpre_ref[...]
    cot, after = (r[...].reshape(1024, C) for r in (cot_ref, after_ref))
    resid = mm_nt(jnp.concatenate([cot, after], axis=1), w_pair)
    for f in range(2):
        g = rows_ref[f].reshape(1280, C)
        conv = mm_nt(row_pairs(jnp.concatenate(columns(g), axis=1)), wide_ref[...])
        base = resid[:, f * C : (f + 1) * C].reshape(4, 2, 128, C)
        for out in range(2):
            part = conv[:, out * C : (out + 1) * C].reshape(4, 128, C)
            out_ref[f, :, out] = (base[:, out] + part).astype(BF16)


VMEM = pl.BlockSpec(memory_space=pltpu.VMEM)


def call(kernel, outs, args, taps, scratch=()):
    return pl.pallas_call(
        kernel,
        out_shape=[jax.ShapeDtypeStruct(s, d) for s, d in outs],
        in_specs=[VMEM] * len(args),
        out_specs=[VMEM] * len(outs),
        scratch_shapes=list(scratch),
        compiler_params=pltpu.CompilerParams(vmem_limit_bytes=24 * 1024 * 1024),
        cost_estimate=pl.CostEstimate(
            flops=int(taps * 2048 * C * C * 2), bytes_accessed=4_000_000, transcendentals=0
        ),
    )(*args)


def gather_kernel(mine_ref, other_ref, spatial_ref, time_ref, down_ref):
    mine = lax.axis_index("core") == 0
    low = jnp.where(mine, mine_ref[...], other_ref[...]).astype(F32)
    high = jnp.where(mine, other_ref[...], mine_ref[...]).astype(F32)
    for first, ref in ((0, spatial_ref), (9, time_ref), (12, down_ref)):
        count = ref.shape[0]
        ref[:, :64] = low[first : first + count]
        ref[:, 64:] = high[first : first + count]


def swap(x, axis, mask):
    return lax.ppermute(x, axis, [(i, i ^ mask) for i in range(lax.axis_size(axis))])


def swap_far(x, axis):
    count = lax.axis_size(axis)
    pairs = [(i, i + 1) for i in range(1, count - 1, 2)]
    return lax.ppermute(x, axis, pairs + [(b, a) for a, b in pairs])


def per_device(features, w_spatial, w_temporal, w_down, cotangent):
    time, rows = ("z", "yl"), ("x", "core")
    x, cot = features[0], cotangent[0, 0]
    frame, edge = ((8, 128, C), BF16), ((2, 128, C), BF16)
    frame_scratch, rows_scratch = pltpu.VMEM(*frame), pltpu.VMEM((2, 10, 128, C), BF16)
    cot_near, cot_far = swap(cot, time, 1), swap_far(cot, time)
    low, high = lax.optimization_barrier((x[:, 0], x[:, 7]))
    to_near, to_far = call(pick_kernel, [edge, edge], (low, high), 0)
    x_near, x_far = swap(to_near, rows, 1), swap_far(to_far, rows)
    slope, act, xt, at, to_near, to_far = call(
        forward_kernel,
        [((2, 4, 2, 128, C), F32), ((2, 4, 2, 128, C), BF16), ((2, C, 1280), BF16), ((2, C, 1024), BF16), frame, frame],
        (x, x_near, x_far, w_spatial, w_temporal, w_down), 11,
        scratch=[pltpu.VMEM((12 * C, 2 * C), BF16), rows_scratch],
    )
    t_near, t_far = swap(to_near, time, 1), swap_far(to_far, time)
    gpre, to_near, to_far, send, keep = call(
        grads_kernel,
        [((2, 8, 128, C), BF16), edge, edge, ((15, 64, C), BF16), ((15, 64, C), F32)],
        (slope, xt, at, cot, cot_near, cot_far, w_temporal, w_down), 21,
        scratch=[pltpu.VMEM((15, 2, 64, C), F32), frame_scratch, frame_scratch],
    )
    (half,) = call(merge_kernel, [((16, 64, C), BF16)], (keep, swap(send, "core", 1)), 0)
    got = lax.all_to_all(half, PLANE, 0, 0, tiled=True)
    got, to_near, to_far = lax.optimization_barrier((got, to_near, to_far))
    total = jnp.sum(got.astype(F32), axis=0)
    g_near, g_far = swap(to_near, rows, 1), swap_far(to_far, rows)
    total = total + swap(total, "z", 1)
    total = total + swap(total, "z", 2)
    total, t_near, t_far, g_near, g_far = lax.optimization_barrier((total, t_near, t_far, g_near, g_far))
    (down,) = call(
        down_kernel, [frame], (x, act.reshape(2, 8, 128, C), t_near, t_far, w_temporal, w_down), 5,
        scratch=[frame_scratch, frame_scratch],
    )
    total = total + swap(total, "z", 4)
    total, down = lax.optimization_barrier((total, down))
    out = jnp.broadcast_to(total.astype(BF16), (16, 64, C))
    out = lax.all_to_all(out, PLANE, 0, 0, tiled=True)
    (grad_features,) = call(
        features_kernel, [((2, 4, 2, 128, C), BF16)],
        (gpre, g_near, g_far, cot, cot_near, cot_far, w_spatial, w_down), 11,
        scratch=[pltpu.VMEM((2 * C, 12 * C), BF16), rows_scratch, frame_scratch, frame_scratch],
    )
    out, grad_features = lax.optimization_barrier((out, grad_features))
    grads = call(
        gather_kernel, [((n, C, C), F32) for n in (9, 3, 3)], (out, swap(out, "core", 1)), 0,
    )
    return (
        down[None, None],
        grad_features.reshape(1, 2, 8, 128, C),
        grads[0].reshape(3, 3, C, C),
        grads[1],
        grads[2],
    )


def solution(mesh):
    fine = Mesh(mesh.devices.reshape(2, 8, 2, 4, 2), ("yh", "z", "yl", "x", "core"))
    block = P("yh", ("z", "yl"), ("x", "core"), None, None)
    return jax.shard_map(
        per_device,
        mesh=fine,
        in_specs=(block, P(), P(), P(), block),
        out_specs=(block, block, P(), P(), P()),
        check_vma=False,
    )
```

time: 88.8 us -> 76.6 us (0.86)
  blocking collectives: 12.5 us -> 0 us
  waiting for transfers between devices: 14.2 us -> 19.9 us
  starting transfers between devices: 44.7 us -> 41.4 us
  other arithmetic: 2.01 us -> 0.06 us
  Pallas kernels: 12.2 us -> 10.3 us
  local copies, waits for them, and re-layouts: 1.97 us -> 3.71 us
    all_to_all x1 -> x0, blocking collectives: 12.5 us -> none  [per_device(): out = lax.all_to_all(out, PLANE, 0, 0, tiled=True)]
    all_to_all x0 -> x1, waiting for transfers between devices: none -> 5.48 us  [per_device(): out = lax.all_to_all(out, PLANE, 0, 0, tiled=True)]
    all_to_all x0 -> x1, starting transfers between devices: none -> 4.43 us  [per_device(): out = lax.all_to_all(out, PLANE, 0, 0, tiled=True)]
    ppermute x4, starting transfers between devices: 10.7 us -> 6.43 us  [swap_far(): return lax.ppermute(x, axis, pairs + [(b, a) for a, b in pairs])]
    all_to_all x1, starting transfers between devices: 9.33 us -> 7.06 us  [per_device(): got = lax.all_to_all(half, PLANE, 0, 0, tiled=True)]
    pallas_call x6 -> x7, Pallas kernels: 12.2 us -> 10.3 us  [call(): pl.pallas_call(kernel, out_shape=[jax.ShapeDtypeStruct(s, d) for s, d in...]
    all_to_all x1, waiting for transfers between devices: 7.85 us -> 6.07 us  [per_device(): got = lax.all_to_all(half, PLANE, 0, 0, tiled=True)]
    ppermute x1 -> x0, starting transfers between devices: 1.44 us -> none  [shift(): lax.ppermute(x, axis, [(i, i + by) for i in range(count) if 0 <= i + by <...]
  transfers between devices with their start and end apart: 15 -> 15, of which waited for: 6 -> 7; matrix products, arithmetic and copies ran while one was open for 4% -> 1% of each run, Pallas kernels for 6% -> 7%
where the time goes in v3:
time: 76.6 us; the launch traced here: 76.1 us
  starting transfers between devices  41.4 us (54%)
  waiting for transfers between devices  19.9 us (26%)
  Pallas kernels  10.3 us (13%)
  local copies, waits for them, and re-layouts  3.71 us (5%)
  between operations  0.83 us (1%)
    ppermute x9, starting transfers between devices, swap(): lax.ppermute(x, axis, [(i, i ^ mask) for i in range(lax.axis_size(axis))])  23.4 us
    pallas_call x7, Pallas kernels, call(): pl.pallas_call(kernel, out_shape=[jax.ShapeDtypeStruct(s, d) for s, d in...  10.3 us
    all_to_all x1, starting transfers between devices, per_device(): got = lax.all_to_all(half, PLANE, 0, 0, tiled=True)  7.06 us
    ppermute x4, starting transfers between devices, swap_far(): return lax.ppermute(x, axis, pairs + [(b, a) for a, b in pairs])  6.43 us
    all_to_all x1, waiting for transfers between devices, per_device(): got = lax.all_to_all(half, PLANE, 0, 0, tiled=True)  6.07 us
    ppermute x9, waiting for transfers between devices, swap(): lax.ppermute(x, axis, [(i, i ^ mask) for i in range(lax.axis_size(axis))])  5.76 us
    all_to_all x1, waiting for transfers between devices, per_device(): out = lax.all_to_all(out, PLANE, 0, 0, tiled=True)  5.48 us
    all_to_all x1, starting transfers between devices, per_device(): out = lax.all_to_all(out, PLANE, 0, 0, tiled=True)  4.43 us
  transfers between devices with their start and end apart: 15, of which 7 were waited for; matrix products, arithmetic and copies ran while one was open for 1% of the time, Pallas kernels for 7%

profile of v3, /device:TPU:1, one launch (start us, length us, event | category | flops | bytes accessed | tf_op | source)
XLA Modules:
  0.0 76.1 jit_solution(7816854692066928755)
XLA Ops:
  0.6 0.7 collective-permute-start.3
  1.3 5.0 %collective-permute-start.2 = (bf16[8,128,128]{2,1,0:T(8,128)(2,1)}, bf16[8,128,128]{2,1,0:T(8,128)(2,1)S(1)}, u32[]{:S(2)}, u32[]{:S(2)}) collective-permute-start(bf16[8,128,128]{2,1,0:T(8,128)(2,1)} %bitcast.15), channel_id=1, source_target_pairs={{0,8},{8,0},{16,24},{24,16},{32,40},{40,32},{48,56},{56,48},{64,72... | collective-permute-start | bytes 786440 | tf_op jit(solution)/shard_map/ppermute | solution.py:274
  6.3 0.0 copy-start.3
  6.3 0.9 %slice_bitcast_fusion = (bf16[2,128,128]{2,1,0:T(8,128)(2,1)S(1)}, bf16[2,128,128]{2,1,0:T(8,128)(2,1)S(1)}) fusion(bf16[2,8,128,128]{3,2,1,0:T(8,128)(2,1)} %bitcast.10), kind=kLoop, calls=%fused_computation.1 | loop fusion | bytes 262144 | tf_op jit(solution)/shard_map/squeeze | solution.py:289
  7.2 0.0 copy-start.2
  7.2 1.3 %collective-permute-start = (bf16[2,128,128]{2,1,0:T(8,128)(2,1)S(1)}, bf16[2,128,128]{2,1,0:T(8,128)(2,1)S(1)}, u32[]{:S(2)}, u32[]{:S(2)}) collective-permute-start(bf16[2,128,128]{2,1,0:T(8,128)(2,1)S(1)} %get-tuple-element.37), channel_id=1, source_target_pairs={{0,1},{1,0},{2,3},{3,2},{4,5},{5,4},{6,7},{7,6},{8,9},{9,8},{10,11... | collective-permute-start | bytes 196616 | tf_op jit(solution)/shard_map/ppermute | solution.py:274
  8.6 3.0 %collective-permute-start.1 = (bf16[2,128,128]{2,1,0:T(8,128)(2,1)S(1)}, bf16[2,128,128]{2,1,0:T(8,128)(2,1)S(1)}, u32[]{:S(2)}, u32[]{:S(2)}) collective-permute-start(bf16[2,128,128]{2,1,0:T(8,128)(2,1)S(1)} %get-tuple-element.38), channel_id=1, source_target_pairs={{1,2},{3,4},{5,6},{2,1},{4,3},{6,5},{9,10},{11,12},{13,14},{10,9},... | collective-permute-start | bytes 196616 | tf_op jit(solution)/shard_map/ppermute | solution.py:280
  11.6 0.0 collective-permute-done.near_ref
  11.6 2.5 %collective-permute-done.1.far_ref = bf16[2,128,128]{2,1,0:T(8,128)(2,1)S(1)} collective-permute-done((bf16[2,128,128]{2,1,0:T(8,128)(2,1)S(1)}, bf16[2,128,128]{2,1,0:T(8,128)(2,1)S(1)}, u32[]{:S(2)}, u32[]{:S(2)}) %collective-permute-start.1) | collective-permute-done | bytes 65568 | tf_op jit(solution)/shard_map/ppermute | solution.py:280
  14.1 0.0 copy-done.3
  14.1 0.0 copy-done.2
  14.2 0.0 copy-start
  14.2 1.0 %copy-done = bf16[1,2,8,128,128]{4,3,2,1,0:T(8,128)(2,1)S(1)} copy-done((bf16[1,2,8,128,128]{4,3,2,1,0:T(8,128)(2,1)S(1)}, bf16[1,2,8,128,128]{4,3,2,1,0:T(8,128)(2,1)}, u32[]{:S(2)}) %copy-start) | copy-done | bytes 524312
  15.2 0.0 copy-start.4
  15.2 1.0 %copy-done.4 = bf16[3,3,128,128]{3,2,1,0:T(8,128)(2,1)S(1)} copy-done((bf16[3,3,128,128]{3,2,1,0:T(8,128)(2,1)S(1)}, bf16[3,3,128,128]{3,2,1,0:T(8,128)(2,1)}, u32[]{:S(2)}) %copy-start.4) | copy-done | bytes 294936
  16.2 0.0 copy-start.6
  16.2 1.9 %shard_map.93 = (f32[2,4,2,128,128]{4,3,2,1,0:T(8,128)S(1)}, bf16[2,4,2,128,128]{4,3,2,1,0:T(8,128)(2,1)S(1)}, bf16[2,128,1280]{2,1,0:T(8,128)(2,1)S(1)}, bf16[2...) custom-call(bf16[2,8,128,128]{3,2,1,0:T(8,128)(2,1)S(1)} %bitcast.11, ...), custom_call_target="tpu_custom_call" | custom-call | flops 738197504 | bytes 4000000 | tf_op jit(solution)/shard_map/pallas_call | solution.py:250
  18.0 0.0 collective-permute-done.3.far_ref
  18.0 0.0 collective-permute-done.2.near_ref
  18.1 0.0 copy-done.6
  18.1 3.0 %shard_map.94 = (bf16[2,8,128,128]{3,2,1,0:T(8,128)(2,1)S(1)}, bf16[2,128,128]{2,1,0:T(8,128)(2,1)S(1)}, bf16[2,128,128]{2,1,0:T(8,128)(2,1)S(1)}, bf16[15,64,128]{2,1,0:T(8,128)(2,1)S(1)}, f32[15,64,128]{2,1,0:T(8,128)S(1)}) custom-call(f32[2,4,2,128,128]{4,3,2,1,0:T(8,128)S(1)} %get-tuple-element.39.slope_ref, ...), custom_call_target="tpu_custom_call" | custom-call | flops 1409286144 | bytes 4000000 | tf_op jit(solution)/shard_map/pallas_call | solution.py:250
  21.1 0.0 copy-start.7
  21.1 0.1 collective-permute-start.4
  21.2 1.5 %collective-permute-done.4.got_ref = bf16[15,64,128]{2,1,0:T(8,128)(2,1)S(1)} collective-permute-done((bf16[15,64,128]{2,1,0:T(8,128)(2,1)S(1)}, bf16[15,64,128]{2,1,0:T(8,128)(2,1)S(1)}, u32[]{:S(2)}, u32[]{:S(2)}) %collective-permute-start.4) | collective-permute-done | bytes 245792 | tf_op jit(solution)/shard_map/ppermute | solution.py:274
  22.7 0.7 shard_map.95
  23.4 0.0 copy-start.1
  23.4 0.0 copy-done.7
  23.4 7.1 %all-to-all-start = ((bf16[16,64,128]{2,1,0:T(8,128)(2,1)}), bf16[16,64,128]{2,1,0:T(8,128)(2,1)S(1)}, u32[]{:S(2)}, u32[]{:S(2)}) async-start(bf16[16,64,128]{2,1,0:T(8,128)(2,1)} %shard_map.95), calls=%async_computation | async-start | bytes 524288 | tf_op jit(solution)/shard_map/all_to_all | solution.py:306
  30.5 1.4 %collective-permute-start.7 = (bf16[8,128,128]{2,1,0:T(8,128)(2,1)S(1)}, bf16[8,128,128]{2,1,0:T(8,128)(2,1)S(1)}, u32[]{:S(2)}, u32[]{:S(2)}) collective-permute-start(bf16[8,128,128]{2,1,0:T(8,128)(2,1)S(1)} %get-tuple-element.47), channel_id=1, source_target_pairs={{0,8},{8,0},{16,24},{24,16},{32,40},{40,32},{48,56},{56,48},{64,72... | collective-permute-start | bytes 786440 | tf_op jit(solution)/shard_map/ppermute | solution.py:274
  31.9 0.7 collective-permute-start.8
  32.5 6.1 %all-to-all-done = bf16[16,64,128]{2,1,0:T(8,128)(2,1)S(1)} async-done(((bf16[16,64,128]{2,1,0:T(8,128)(2,1)}), bf16[16,64,128]{2,1,0:T(8,128)(2,1)S(1)}, u32[]{:S(2)}, u32[]{:S(2)}) %all-to-all-start) | async-done | bytes 262176 | tf_op jit(solution)/shard_map/all_to_all | solution.py:306
  38.7 1.9 %collective-permute-start.5 = (f32[64,128]{1,0:T(8,128)S(1)}, f32[64,128]{1,0:T(8,128)S(1)}, u32[]{:S(2)}, u32[]{:S(2)}) collective-permute-start(f32[64,128]{1,0:T(8,128)S(1)} %convert_reduce_fusion), channel_id=1, source_target_pairs={{0,16},{16,0},{32,48},{48,32},{64,80},{80,64},{96,112},{112,96},{1... | collective-permute-start | bytes 98312 | tf_op jit(solution)/shard_map/ppermute | solution.py:274
  40.6 1.8 %collective-permute-start.9 = (bf16[2,128,128]{2,1,0:T(8,128)(2,1)S(1)}, bf16[2,128,128]{2,1,0:T(8,128)(2,1)S(1)}, u32[]{:S(2)}, u32[]{:S(2)}) collective-permute-start(bf16[2,128,128]{2,1,0:T(8,128)(2,1)S(1)} %get-tuple-element.49), channel_id=1, source_target_pairs={{0,1},{1,0},{2,3},{3,2},{4,5},{5,4},{6,7},{7,6},{8,9},{9,8},{10,11... | collective-permute-start | bytes 196616 | tf_op jit(solution)/shard_map/ppermute | solution.py:274
  42.4 2.1 %collective-permute-start.10 = (bf16[2,128,128]{2,1,0:T(8,128)(2,1)S(1)}, bf16[2,128,128]{2,1,0:T(8,128)(2,1)S(1)}, u32[]{:S(2)}, u32[]{:S(2)}) collective-permute-start(bf16[2,128,128]{2,1,0:T(8,128)(2,1)S(1)} %get-tuple-element.50), channel_id=1, source_target_pairs={{1,2},{3,4},{5,6},{2,1},{4,3},{6,5},{9,10},{11,12},{13,14},{10,9},... | collective-permute-start | bytes 196616 | tf_op jit(solution)/shard_map/ppermute | solution.py:280
  44.4 0.0 collective-permute-done.5
  44.5 4.2 %collective-permute-start.6 = (f32[64,128]{1,0:T(8,128)S(1)}, f32[64,128]{1,0:T(8,128)S(1)}, u32[]{:S(2)}, u32[]{:S(2)}) collective-permute-start(f32[64,128]{1,0:T(8,128)S(1)} %add.9), channel_id=1, source_target_pairs={{0,32},{16,48},{32,0},{48,16},{64,96},{80,112},{96,64},{112,80},{1... | collective-permute-start | bytes 98312 | tf_op jit(solution)/shard_map/ppermute | solution.py:274
  48.7 1.8 %collective-permute-done.6 = f32[64,128]{1,0:T(8,128)S(1)} collective-permute-done((f32[64,128]{1,0:T(8,128)S(1)}, f32[64,128]{1,0:T(8,128)S(1)}, u32[]{:S(2)}, u32[]{:S(2)}) %collective-permute-start.6) | collective-permute-done | bytes 32800 | tf_op jit(solution)/shard_map/ppermute | solution.py:274
  50.5 0.0 collective-permute-done.7.near_ref
  50.5 0.0 collective-permute-done.8.far_ref
  50.5 0.0 collective-permute-done.9.g_near_ref
  50.5 0.0 collective-permute-done.10.g_far_ref
  50.5 3.9 %collective-permute-start.11 = (f32[64,128]{1,0:T(8,128)S(1)}, f32[64,128]{1,0:T(8,128)S(1)}, u32[]{:S(2)}, u32[]{:S(2)}) collective-permute-start(f32[64,128]{1,0:T(8,128)S(1)} %add.10), channel_id=1, source_target_pairs={{0,64},{16,80},{32,96},{48,112},{64,0},{80,16},{96,32},{112,48},{1... | collective-permute-start | bytes 98312 | tf_op jit(solution)/shard_map/ppermute | solution.py:274
  54.4 0.0 copy-done.1
  54.4 1.6 %shard_map.96 = bf16[8,128,128]{2,1,0:T(8,128)(2,1)} custom-call(bf16[2,8,128,128]{3,2,1,0:T(8,128)(2,1)S(1)} %bitcast.12, bf16[2,8,128,128]{3,2,1,0:T(8,128)(2,1)S(1)} %bitcast.13, bf16[8,128,128]{2,1,0:T(8,128)(2,1)S(1)} %collective-permute-done.7.near_ref, bf16[8,128,128]{2,1,0:T(8,128)(2,1)S(1)} %collective-permute-done.8.far_ref, ...), custom_call_target="tpu_custom_call" | custom-call | flops 335544320 | bytes 4000000 | tf_op jit(solution)/shard_map/pallas_call | solution.py:250
  55.9 0.0 copy-start.8
  55.9 1.3 %collective-permute-done.11 = f32[64,128]{1,0:T(8,128)S(1)} collective-permute-done((f32[64,128]{1,0:T(8,128)S(1)}, f32[64,128]{1,0:T(8,128)S(1)}, u32[]{:S(2)}, u32[]{:S(2)}) %collective-permute-start.11) | collective-permute-done | bytes 32800 | tf_op jit(solution)/shard_map/ppermute | solution.py:274
  57.3 0.8 broadcast_in_dim.7
  58.0 0.0 copy-start.5
  58.0 4.4 %all-to-all-start.1 = ((bf16[16,64,128]{2,1,0:T(8,128)(2,1)}), bf16[16,64,128]{2,1,0:T(8,128)(2,1)S(1)}, u32[]{:S(2)}, u32[]{:S(2)}) async-start(bf16[16,64,128]{2,1,0:T(8,128)(2,1)} %broadcast_in_dim.7), calls=%async_computation.1 | async-start | bytes 524288 | tf_op jit(solution)/shard_map/all_to_all | solution.py:320
  62.5 0.0 copy-done.8
  62.5 0.0 copy-done.5
  62.5 2.1 %shard_map.97 = bf16[2,4,2,128,128]{4,3,2,1,0:T(8,128)(2,1)} custom-call(bf16[2,8,128,128]{3,2,1,0:T(8,128)(2,1)S(1)} %copy-done.8, bf16[2,128,128]{2,1,0:T(8,128)(2,1)S(1)} %collective-permute-done.9.g_near_ref, bf16[2,128,128]{2,1,0:T(8,128)(2,1)S(1)} %collective-permute-done.10.g_far_ref, bf16[8,128,128]{2,1,0:T(8,128)(2,1)S(1)} %bitcast.17, ...), custom_call_target="tpu_custom_call" | custom-call | flops 738197504 | bytes 4000000 | tf_op jit(solution)/shard_map/pallas_call | solution.py:250
  64.6 5.5 %all-to-all-done.1.mine_ref = bf16[16,64,128]{2,1,0:T(8,128)(2,1)S(1)} async-done(((bf16[16,64,128]{2,1,0:T(8,128)(2,1)}), bf16[16,64,128]{2,1,0:T(8,128)(2,1)S(1)}, u32[]{:S(2)}, u32[]{:S(2)}) %all-to-all-start.1) | async-done | bytes 262176 | tf_op jit(solution)/shard_map/all_to_all | solution.py:320
  70.1 3.9 %collective-permute-start.12 = (bf16[16,64,128]{2,1,0:T(8,128)(2,1)S(1)}, bf16[16,64,128]{2,1,0:T(8,128)(2,1)S(1)}, u32[]{:S(2)}, u32[]{:S(2)}) collective-permute-start(bf16[16,64,128]{2,1,0:T(8,128)(2,1)S(1)} %all-to-all-done.1.mine_ref), channel_id=1, source_target_pairs={{0,1},{1,0},{2,3},{3,2},{4,5},{5,4},{6,7},{7,6},{8,9},{9,8},{10,11... | collective-permute-start | bytes 786440 | tf_op jit(solution)/shard_map/ppermute | solution.py:274
  74.0 1.2 %collective-permute-done.12.other_ref = bf16[16,64,128]{2,1,0:T(8,128)(2,1)S(1)} collective-permute-done((bf16[16,64,128]{2,1,0:T(8,128)(2,1)S(1)}, bf16[16,64,128]{2,1,0:T(8,128)(2,1)S(1)}, u32[]{:S(2)}, u32[]{:S(2)}) %collective-permute-start.12) | collective-permute-done | bytes 262176 | tf_op jit(solution)/shard_map/ppermute | solution.py:274
  75.1 1.0 %shard_map.98 = (f32[9,128,128]{2,1,0:T(8,128)}, f32[3,128,128]{2,1,0:T(8,128)}, f32[3,128,128]{2,1,0:T(8,128)}) custom-call(bf16[16,64,128]{2,1,0:T(8,128)(2,1)S(1)} %all-to-all-done.1.mine_ref, bf16[16,64,128]{2,1,0:T(8,128)(2,1)S(1)} %collective-permute-done.12.other_ref), custom_call_target="tpu_custom_call" | custom-call | bytes 4000000 | tf_op jit(solution)/shard_map/pallas_call | solution.py:250
  (5 shorter events, 0.1 us)
Async XLA Ops:
  0.6 17.4 %collective-permute-start.3 = (bf16[8,128,128]{2,1,0:T(8,128)(2,1)}, bf16[8,128,128]{2,1,0:T(8,128)(2,1)S(1)}, u32[]{:S(2)}, u32[]{:S(2)}) collective-permute-start(bf16[8,128,128]{2,1,0:T(8,128)(2,1)} %bitcast.14), channel_id=1, source_target_pairs={{8,16},{24,32},{40,48},{56,64},{72,80},{88,96},{104,112},{16,8},{3... | collective-permute-start | bytes 786440 | tf_op jit(solution)/shard_map/ppermute | solution.py:280
  1.3 16.7 %collective-permute-start.2 = (bf16[8,128,128]{2,1,0:T(8,128)(2,1)}, bf16[8,128,128]{2,1,0:T(8,128)(2,1)S(1)}, u32[]{:S(2)}, u32[]{:S(2)}) collective-permute-start(bf16[8,128,128]{2,1,0:T(8,128)(2,1)} %bitcast.15), channel_id=1, source_target_pairs={{0,8},{8,0},{16,24},{24,16},{32,40},{40,32},{48,56},{56,48},{64,72... | collective-permute-start | bytes 786440 | tf_op jit(solution)/shard_map/ppermute | solution.py:274
  6.3 7.9 %copy-start.3 = (bf16[3,128,128]{2,1,0:T(8,128)(2,1)S(1)}, bf16[3,128,128]{2,1,0:T(8,128)(2,1)}, u32[]{:S(2)}) copy-start(bf16[3,128,128]{2,1,0:T(8,128)(2,1)} %wd_ref.7) | copy-start | bytes 294916
  7.2 6.9 %copy-start.2 = (bf16[3,128,128]{2,1,0:T(8,128)(2,1)S(1)}, bf16[3,128,128]{2,1,0:T(8,128)(2,1)}, u32[]{:S(2)}) copy-start(bf16[3,128,128]{2,1,0:T(8,128)(2,1)} %wt_ref.5) | copy-start | bytes 294916
  7.2 4.4 %collective-permute-start = (bf16[2,128,128]{2,1,0:T(8,128)(2,1)S(1)}, bf16[2,128,128]{2,1,0:T(8,128)(2,1)S(1)}, u32[]{:S(2)}, u32[]{:S(2)}) collective-permute-start(bf16[2,128,128]{2,1,0:T(8,128)(2,1)S(1)} %get-tuple-element.37), channel_id=1, source_target_pairs={{0,1},{1,0},{2,3},{3,2},{4,5},{5,4},{6,7},{7,6},{8,9},{9,8},{10,11... | collective-permute-start | bytes 196616 | tf_op jit(solution)/shard_map/ppermute | solution.py:274
  8.6 5.6 %collective-permute-start.1 = (bf16[2,128,128]{2,1,0:T(8,128)(2,1)S(1)}, bf16[2,128,128]{2,1,0:T(8,128)(2,1)S(1)}, u32[]{:S(2)}, u32[]{:S(2)}) collective-permute-start(bf16[2,128,128]{2,1,0:T(8,128)(2,1)S(1)} %get-tuple-element.38), channel_id=1, source_target_pairs={{1,2},{3,4},{5,6},{2,1},{4,3},{6,5},{9,10},{11,12},{13,14},{10,9},... | collective-permute-start | bytes 196616 | tf_op jit(solution)/shard_map/ppermute | solution.py:280
  14.2 1.0 %copy-start = (bf16[1,2,8,128,128]{4,3,2,1,0:T(8,128)(2,1)S(1)}, bf16[1,2,8,128,128]{4,3,2,1,0:T(8,128)(2,1)}, u32[]{:S(2)}) copy-start(bf16[1,2,8,128,128]{4,3,2,1,0:T(8,128)(2,1)} %param.5) | copy-start | bytes 1572868
  15.2 1.0 %copy-start.4 = (bf16[3,3,128,128]{3,2,1,0:T(8,128)(2,1)S(1)}, bf16[3,3,128,128]{3,2,1,0:T(8,128)(2,1)}, u32[]{:S(2)}) copy-start(bf16[3,3,128,128]{3,2,1,0:T(8,128)(2,1)} %w_ref.3) | copy-start | bytes 884740
  16.2 1.9 %copy-start.6 = (bf16[1,1,8,128,128]{4,3,2,1,0:T(8,128)(2,1)S(1)}, bf16[1,1,8,128,128]{4,3,2,1,0:T(8,128)(2,1)}, u32[]{:S(2)}) copy-start(bf16[1,1,8,128,128]{4,3,2,1,0:T(8,128)(2,1)} %param.9) | copy-start | bytes 786436
  21.1 2.4 %copy-start.7 = (bf16[2,8,128,128]{3,2,1,0:T(8,128)(2,1)}, bf16[2,8,128,128]{3,2,1,0:T(8,128)(2,1)S(1)}, u32[]{:S(2)}) copy-start(bf16[2,8,128,128]{3,2,1,0:T(8,128)(2,1)S(1)} %get-tuple-element.57.gpre_ref) | copy-start | bytes 1572868
  21.1 1.6 %collective-permute-start.4 = (bf16[15,64,128]{2,1,0:T(8,128)(2,1)S(1)}, bf16[15,64,128]{2,1,0:T(8,128)(2,1)S(1)}, u32[]{:S(2)}, u32[]{:S(2)}) collective-permute-start(bf16[15,64,128]{2,1,0:T(8,128)(2,1)S(1)} %get-tuple-element.43), channel_id=1, source_target_pairs={{0,1},{1,0},{2,3},{3,2},{4,5},{5,4},{6,7},{7,6},{8,9},{9,8},{10,11... | collective-permute-start | bytes 737288 | tf_op jit(solution)/shard_map/ppermute | solution.py:274
  23.4 30.9 %copy-start.1 = (bf16[1,2,8,128,128]{4,3,2,1,0:T(8,128)(2,1)S(1)}, bf16[1,2,8,128,128]{4,3,2,1,0:T(8,128)(2,1)}, u32[]{:S(2)}) copy-start(bf16[1,2,8,128,128]{4,3,2,1,0:T(8,128)(2,1)} %param.5) | copy-start | bytes 1572868
  23.4 15.2 %all-to-all-start = ((bf16[16,64,128]{2,1,0:T(8,128)(2,1)}), bf16[16,64,128]{2,1,0:T(8,128)(2,1)S(1)}, u32[]{:S(2)}, u32[]{:S(2)}) async-start(bf16[16,64,128]{2,1,0:T(8,128)(2,1)} %shard_map.95), calls=%async_computation | async-start | bytes 524288 | tf_op jit(solution)/shard_map/all_to_all | solution.py:306
  30.5 20.0 %collective-permute-start.7 = (bf16[8,128,128]{2,1,0:T(8,128)(2,1)S(1)}, bf16[8,128,128]{2,1,0:T(8,128)(2,1)S(1)}, u32[]{:S(2)}, u32[]{:S(2)}) collective-permute-start(bf16[8,128,128]{2,1,0:T(8,128)(2,1)S(1)} %get-tuple-element.47), channel_id=1, source_target_pairs={{0,8},{8,0},{16,24},{24,16},{32,40},{40,32},{48,56},{56,48},{64,72... | collective-permute-start | bytes 786440 | tf_op jit(solution)/shard_map/ppermute | solution.py:274
  31.9 18.6 %collective-permute-start.8 = (bf16[8,128,128]{2,1,0:T(8,128)(2,1)S(1)}, bf16[8,128,128]{2,1,0:T(8,128)(2,1)S(1)}, u32[]{:S(2)}, u32[]{:S(2)}) collective-permute-start(bf16[8,128,128]{2,1,0:T(8,128)(2,1)S(1)} %get-tuple-element.48), channel_id=1, source_target_pairs={{8,16},{24,32},{40,48},{56,64},{72,80},{88,96},{104,112},{16,8},{3... | collective-permute-start | bytes 786440 | tf_op jit(solution)/shard_map/ppermute | solution.py:280
  38.7 5.8 %collective-permute-start.5 = (f32[64,128]{1,0:T(8,128)S(1)}, f32[64,128]{1,0:T(8,128)S(1)}, u32[]{:S(2)}, u32[]{:S(2)}) collective-permute-start(f32[64,128]{1,0:T(8,128)S(1)} %convert_reduce_fusion), channel_id=1, source_target_pairs={{0,16},{16,0},{32,48},{48,32},{64,80},{80,64},{96,112},{112,96},{1... | collective-permute-start | bytes 98312 | tf_op jit(solution)/shard_map/ppermute | solution.py:274
  40.6 9.9 %collective-permute-start.9 = (bf16[2,128,128]{2,1,0:T(8,128)(2,1)S(1)}, bf16[2,128,128]{2,1,0:T(8,128)(2,1)S(1)}, u32[]{:S(2)}, u32[]{:S(2)}) collective-permute-start(bf16[2,128,128]{2,1,0:T(8,128)(2,1)S(1)} %get-tuple-element.49), channel_id=1, source_target_pairs={{0,1},{1,0},{2,3},{3,2},{4,5},{5,4},{6,7},{7,6},{8,9},{9,8},{10,11... | collective-permute-start | bytes 196616 | tf_op jit(solution)/shard_map/ppermute | solution.py:274
  42.4 8.1 %collective-permute-start.10 = (bf16[2,128,128]{2,1,0:T(8,128)(2,1)S(1)}, bf16[2,128,128]{2,1,0:T(8,128)(2,1)S(1)}, u32[]{:S(2)}, u32[]{:S(2)}) collective-permute-start(bf16[2,128,128]{2,1,0:T(8,128)(2,1)S(1)} %get-tuple-element.50), channel_id=1, source_target_pairs={{1,2},{3,4},{5,6},{2,1},{4,3},{6,5},{9,10},{11,12},{13,14},{10,9},... | collective-permute-start | bytes 196616 | tf_op jit(solution)/shard_map/ppermute | solution.py:280
  44.5 6.0 %collective-permute-start.6 = (f32[64,128]{1,0:T(8,128)S(1)}, f32[64,128]{1,0:T(8,128)S(1)}, u32[]{:S(2)}, u32[]{:S(2)}) collective-permute-start(f32[64,128]{1,0:T(8,128)S(1)} %add.9), channel_id=1, source_target_pairs={{0,32},{16,48},{32,0},{48,16},{64,96},{80,112},{96,64},{112,80},{1... | collective-permute-start | bytes 98312 | tf_op jit(solution)/shard_map/ppermute | solution.py:274
  50.5 6.8 %collective-permute-start.11 = (f32[64,128]{1,0:T(8,128)S(1)}, f32[64,128]{1,0:T(8,128)S(1)}, u32[]{:S(2)}, u32[]{:S(2)}) collective-permute-start(f32[64,128]{1,0:T(8,128)S(1)} %add.10), channel_id=1, source_target_pairs={{0,64},{16,80},{32,96},{48,112},{64,0},{80,16},{96,32},{112,48},{1... | collective-permute-start | bytes 98312 | tf_op jit(solution)/shard_map/ppermute | solution.py:274
  55.9 6.5 %copy-start.8 = (bf16[2,8,128,128]{3,2,1,0:T(8,128)(2,1)S(1)}, bf16[2,8,128,128]{3,2,1,0:T(8,128)(2,1)}, u32[]{:S(2)}) copy-start(bf16[2,8,128,128]{3,2,1,0:T(8,128)(2,1)} %copy-done.7) | copy-start | bytes 1572868
  58.0 4.5 %copy-start.5 = (bf16[3,3,128,128]{3,2,1,0:T(8,128)(2,1)S(1)}, bf16[3,3,128,128]{3,2,1,0:T(8,128)(2,1)}, u32[]{:S(2)}) copy-start(bf16[3,3,128,128]{3,2,1,0:T(8,128)(2,1)} %w_ref.3) | copy-start | bytes 884740
  58.0 12.1 %all-to-all-start.1 = ((bf16[16,64,128]{2,1,0:T(8,128)(2,1)}), bf16[16,64,128]{2,1,0:T(8,128)(2,1)S(1)}, u32[]{:S(2)}, u32[]{:S(2)}) async-start(bf16[16,64,128]{2,1,0:T(8,128)(2,1)} %broadcast_in_dim.7), calls=%async_computation.1 | async-start | bytes 524288 | tf_op jit(solution)/shard_map/all_to_all | solution.py:320
  70.1 5.0 %collective-permute-start.12 = (bf16[16,64,128]{2,1,0:T(8,128)(2,1)S(1)}, bf16[16,64,128]{2,1,0:T(8,128)(2,1)S(1)}, u32[]{:S(2)}, u32[]{:S(2)}) collective-permute-start(bf16[16,64,128]{2,1,0:T(8,128)(2,1)S(1)} %all-to-all-done.1.mine_ref), channel_id=1, source_target_pairs={{0,1},{1,0},{2,3},{3,2},{4,5},{5,4},{6,7},{7,6},{8,9},{9,8},{10,11... | collective-permute-start | bytes 786440 | tf_op jit(solution)/shard_map/ppermute | solution.py:274

commit v4 on v3

--- a/solution.py
+++ b/solution.py
@@ -55,20 +55,43 @@
         after_ref[...] = near_ref[...]
 
 
+def sort_rows(near_ref, far_ref, low_ref, high_ref):
+    @pl.when(lax.axis_index("core") == 1)
+    def _():
+        low_ref[...] = near_ref[...].reshape(128, C)
+        high_ref[...] = far_ref[...]
+
+    @pl.when(lax.axis_index("core") == 0)
+    def _():
+        low_ref[...] = far_ref[...]
+        high_ref[...] = near_ref[...].reshape(128, C)
+
+
 def pick_kernel(low_ref, high_ref, near_ref, far_ref):
     sort_sides(lax.axis_index("core") == 1, low_ref, high_ref, near_ref, far_ref)
 
 
-def forward_kernel(
-    x_ref, near_ref, far_ref, w_ref, wt_ref, wd_ref,
-    slope_ref, act_ref, xt_ref, at_ref, to_near_ref, to_far_ref, wide_ref, rows_ref,
-):
+def prepare_kernel(x_hbm, w_hbm, x_ref, wide_ref, w_ref, sem):
+    copies = [
+        pltpu.make_async_copy(w_hbm, w_ref, sem.at[0]),
+        pltpu.make_async_copy(x_hbm, x_ref, sem.at[1]),
+    ]
+    for copy in copies:
+        copy.start()
     wide_ref[...] = jnp.zeros_like(wide_ref)
+    copies[0].wait()
     for out in range(2):
         for dy in range(3):
             for dx in range(3):
                 start = ((dy + out) * 3 + dx) * C
                 wide_ref[start : start + C, out * C : (out + 1) * C] = w_ref[dy, dx]
+    copies[1].wait()
+
+
+def forward_kernel(
+    x_ref, near_ref, far_ref, wide_ref, wt_ref, wd_ref,
+    slope_ref, act_ref, xt_ref, at_ref, to_near_ref, to_far_ref, rows_ref,
+):
     sort_sides(lax.axis_index("core") == 1, near_ref, far_ref, rows_ref.at[:, 0], rows_ref.at[:, 9])
     rows_ref[:, 1:9] = x_ref[...]
     for f in range(2):
@@ -111,7 +134,7 @@
 
 def grads_kernel(
     slope_ref, xt_ref, at_ref, cot_ref, near_ref, far_ref, wt_ref, wd_ref,
-    gpre_ref, to_near_ref, to_far_ref, send_ref, keep_ref, mats_ref, before_ref, after_ref,
+    gpre_ref, to_far_ref, send_ref, keep_ref, mats_ref, before_ref, after_ref,
 ):
     first = frame_index() == 0
     core = lax.axis_index("core")
@@ -148,7 +171,7 @@
         spatial = term if spatial is None else spatial + term
     row = 7 * (1 - core)
     for f in range(2):
-        to_near_ref[f] = gpre_ref[f, row]
+        send_ref[15 + 2 * f : 17 + 2 * f] = gpre_ref[f, row].reshape(2, 64, C)
         to_far_ref[f] = gpre_ref[f, 7 - row]
     for dy in range(3):
         for dx in range(3):
@@ -178,12 +201,12 @@
             rest = (m - top.astype(F32)).astype(BF16)
             total = total + mm_tn(wt_ref[tap], top) + mm_tn(wt_ref[tap], rest)
         mats_ref[12 + k] = total.reshape(2, 64, C)
-    send_ref[...] = mats_ref[:, 1 - core].astype(BF16)
+    send_ref[:15] = mats_ref[:, 1 - core].astype(BF16)
     keep_ref[...] = mats_ref[:, core]
 
 
 def merge_kernel(keep_ref, got_ref, out_ref):
-    out_ref[:15] = (keep_ref[...] + got_ref[...].astype(F32)).astype(BF16)
+    out_ref[:15] = (keep_ref[...] + got_ref[:15].astype(F32)).astype(BF16)
     out_ref[15] = jnp.zeros((64, C), BF16)
 
 
@@ -212,7 +235,7 @@
 
 
 def features_kernel(
-    gpre_ref, g_near_ref, g_far_ref, cot_ref, near_ref, far_ref, w_ref, wd_ref,
+    gpre_ref, sent_ref, g_far_ref, cot_ref, near_ref, far_ref, w_ref, wd_ref,
     out_ref, wide_ref, rows_ref, before_ref, after_ref,
 ):
     wide_ref[...] = jnp.zeros_like(wide_ref)
@@ -230,7 +253,9 @@
         axis=0,
     )
     sort_sides(lax.axis_index("yl") == 1, near_ref, far_ref, before_ref, after_ref)
-    sort_sides(lax.axis_index("core") == 1, g_near_ref, g_far_ref, rows_ref.at[:, 0], rows_ref.at[:, 9])
+    for f in range(2):
+        near_ref_f = sent_ref.at[15 + 2 * f : 17 + 2 * f]
+        sort_rows(near_ref_f, g_far_ref.at[f], rows_ref.at[f, 0], rows_ref.at[f, 9])
     rows_ref[:, 1:9] = gpre_ref[...]
     cot, after = (r[...].reshape(1024, C) for r in (cot_ref, after_ref))
     resid = mm_nt(jnp.concatenate([cot, after], axis=1), w_pair)
@@ -270,6 +295,11 @@
         ref[:, 64:] = high[first : first + count]
 
 
+def exchange(x, axis, count):
+    groups = [list(range(count - 1, -1, -1))]
+    return lax.all_to_all(x, axis, 0, 0, axis_index_groups=groups, tiled=True)
+
+
 def swap(x, axis, mask):
     return lax.ppermute(x, axis, [(i, i ^ mask) for i in range(lax.axis_size(axis))])
 
@@ -289,41 +319,50 @@
     low, high = lax.optimization_barrier((x[:, 0], x[:, 7]))
     to_near, to_far = call(pick_kernel, [edge, edge], (low, high), 0)
     x_near, x_far = swap(to_near, rows, 1), swap_far(to_far, rows)
+    source, _ = lax.optimization_barrier((x, to_near))
+    here, wide = pl.pallas_call(
+        prepare_kernel,
+        out_shape=[jax.ShapeDtypeStruct((2, 8, 128, C), BF16), jax.ShapeDtypeStruct((12 * C, 2 * C), BF16)],
+        in_specs=[pl.BlockSpec(memory_space=pl.ANY)] * 2,
+        out_specs=[VMEM] * 2,
+        scratch_shapes=[pltpu.VMEM((3, 3, C, C), BF16), pltpu.SemaphoreType.DMA((2,))],
+        compiler_params=pltpu.CompilerParams(vmem_limit_bytes=24 * 1024 * 1024),
+    )(source, w_spatial)
     slope, act, xt, at, to_near, to_far = call(
         forward_kernel,
         [((2, 4, 2, 128, C), F32), ((2, 4, 2, 128, C), BF16), ((2, C, 1280), BF16), ((2, C, 1024), BF16), frame, frame],
-        (x, x_near, x_far, w_spatial, w_temporal, w_down), 11,
-        scratch=[pltpu.VMEM((12 * C, 2 * C), BF16), rows_scratch],
+        (here, x_near, x_far, wide, w_temporal, w_down), 11,
+        scratch=[rows_scratch],
     )
     t_near, t_far = swap(to_near, time, 1), swap_far(to_far, time)
-    gpre, to_near, to_far, send, keep = call(
+    gpre, to_far, send, keep = call(
         grads_kernel,
-        [((2, 8, 128, C), BF16), edge, edge, ((15, 64, C), BF16), ((15, 64, C), F32)],
+        [((2, 8, 128, C), BF16), edge, ((19, 64, C), BF16), ((15, 64, C), F32)],
         (slope, xt, at, cot, cot_near, cot_far, w_temporal, w_down), 21,
         scratch=[pltpu.VMEM((15, 2, 64, C), F32), frame_scratch, frame_scratch],
     )
-    (half,) = call(merge_kernel, [((16, 64, C), BF16)], (keep, swap(send, "core", 1)), 0)
-    got = lax.all_to_all(half, PLANE, 0, 0, tiled=True)
-    got, to_near, to_far = lax.optimization_barrier((got, to_near, to_far))
+    near = swap(send, "core", 1)
+    (half,) = call(merge_kernel, [((16, 64, C), BF16)], (keep, near), 0)
+    got = exchange(half, PLANE, 16)
+    got, to_far = lax.optimization_barrier((got, to_far))
     total = jnp.sum(got.astype(F32), axis=0)
-    g_near, g_far = swap(to_near, rows, 1), swap_far(to_far, rows)
-    total = total + swap(total, "z", 1)
-    total = total + swap(total, "z", 2)
-    total, t_near, t_far, g_near, g_far = lax.optimization_barrier((total, t_near, t_far, g_near, g_far))
+    g_far = swap_far(to_far, rows)
+    column = jnp.broadcast_to(total.astype(BF16), (8, 64, C))
+    column = exchange(column, "z", 8)
+    column, g_far, t_near, t_far = lax.optimization_barrier((column, g_far, t_near, t_far))
+    total = jnp.sum(column.astype(F32), axis=0)
+    out = jnp.broadcast_to(total.astype(BF16), (16, 64, C))
+    out = exchange(out, PLANE, 16)
     (down,) = call(
         down_kernel, [frame], (x, act.reshape(2, 8, 128, C), t_near, t_far, w_temporal, w_down), 5,
         scratch=[frame_scratch, frame_scratch],
     )
-    total = total + swap(total, "z", 4)
-    total, down = lax.optimization_barrier((total, down))
-    out = jnp.broadcast_to(total.astype(BF16), (16, 64, C))
-    out = lax.all_to_all(out, PLANE, 0, 0, tiled=True)
     (grad_features,) = call(
         features_kernel, [((2, 4, 2, 128, C), BF16)],
-        (gpre, g_near, g_far, cot, cot_near, cot_far, w_spatial, w_down), 11,
+        (gpre, near, g_far, cot, cot_near, cot_far, w_spatial, w_down), 11,
         scratch=[pltpu.VMEM((2 * C, 12 * C), BF16), rows_scratch, frame_scratch, frame_scratch],
     )
-    out, grad_features = lax.optimization_barrier((out, grad_features))
+    out, down, grad_features = lax.optimization_barrier((out, down, grad_features))
     grads = call(
         gather_kernel, [((n, C, C), F32) for n in (9, 3, 3)], (out, swap(out, "core", 1)), 0,
     )

time: 76.6 us -> 69.8 us (0.911)
  waiting for transfers between devices: 19.9 us -> 9.77 us
  starting transfers between devices: 41.4 us -> 43.1 us
  other arithmetic: 0.06 us -> 0.97 us
  Pallas kernels: 10.3 us -> 11.2 us
    ppermute x9 -> x5, starting transfers between devices: 23.4 us -> 8.21 us  [swap(): lax.ppermute(x, axis, [(i, i ^ mask) for i in range(lax.axis_size(axis))])]
    all_to_all x2 -> x3, starting transfers between devices: 11.5 us -> 26.3 us  [exchange(): return lax.all_to_all(x, axis, 0, 0, axis_index_groups=groups, tiled=True)]
    all_to_all x2 -> x3, waiting for transfers between devices: 11.6 us -> 3.63 us  [exchange(): return lax.all_to_all(x, axis, 0, 0, axis_index_groups=groups, tiled=True)]
    ppermute x9 -> x5, waiting for transfers between devices: 5.76 us -> 2.4 us  [swap(): lax.ppermute(x, axis, [(i, i ^ mask) for i in range(lax.axis_size(axis))])]
    ppermute x4, starting transfers between devices: 6.43 us -> 8.58 us  [swap_far(): return lax.ppermute(x, axis, pairs + [(b, a) for a, b in pairs])]
    ppermute x4, waiting for transfers between devices: 2.54 us -> 3.74 us  [swap_far(): return lax.ppermute(x, axis, pairs + [(b, a) for a, b in pairs])]
    unnamed x18 -> x16, local copies, waits for them, and re-layouts: 2.03 us -> 1.07 us
    reduce_sum x0 -> x1, other arithmetic: none -> 0.93 us  [per_device(): total = jnp.sum(column.astype(F32), axis=0)]
  transfers between devices with their start and end apart: 15 -> 12, of which waited for: 7 -> 6; matrix products, arithmetic and copies ran while one was open for 1% -> 2% of each run, Pallas kernels for 7% -> 9%
where the time goes in v4:
time: 69.8 us; the launch traced here: 69.2 us
  starting transfers between devices  43.1 us (62%)
  Pallas kernels  11.2 us (16%)
  waiting for transfers between devices  9.77 us (14%)
  local copies, waits for them, and re-layouts  3.39 us (5%)
  other arithmetic  0.97 us (1%)
  between operations  0.77 us (1%)
    all_to_all x3, starting transfers between devices, exchange(): return lax.all_to_all(x, axis, 0, 0, axis_index_groups=groups, tiled=True)  26.3 us
    pallas_call x7, Pallas kernels, call(): pl.pallas_call(kernel, out_shape=[jax.ShapeDtypeStruct(s, d) for s, d in...  10.9 us
    ppermute x4, starting transfers between devices, swap_far(): return lax.ppermute(x, axis, pairs + [(b, a) for a, b in pairs])  8.58 us
    ppermute x5, starting transfers between devices, swap(): lax.ppermute(x, axis, [(i, i ^ mask) for i in range(lax.axis_size(axis))])  8.21 us
    ppermute x4, waiting for transfers between devices, swap_far(): return lax.ppermute(x, axis, pairs + [(b, a) for a, b in pairs])  3.74 us
    all_to_all x3, waiting for transfers between devices, exchange(): return lax.all_to_all(x, axis, 0, 0, axis_index_groups=groups, tiled=True)  3.63 us
    ppermute x5, waiting for transfers between devices, swap(): lax.ppermute(x, axis, [(i, i ^ mask) for i in range(lax.axis_size(axis))])  2.4 us
  transfers between devices with their start and end apart: 12, of which 6 were waited for; matrix products, arithmetic and copies ran while one was open for 2% of the time, Pallas kernels for 9%

profile of v4, /device:TPU:1, one launch (start us, length us, event | category | flops | bytes accessed | tf_op | source)
XLA Modules:
  0.0 69.2 jit_solution(10865725993925997809)
XLA Ops:
  0.6 0.0 copy-start.2
  0.6 2.2 %collective-permute-start.2 = (bf16[8,128,128]{2,1,0:T(8,128)(2,1)}, bf16[8,128,128]{2,1,0:T(8,128)(2,1)S(1)}, u32[]{:S(2)}, u32[]{:S(2)}) collective-permute-start(bf16[8,128,128]{2,1,0:T(8,128)(2,1)} %bitcast.14), channel_id=1, source_target_pairs={{0,8},{8,0},{16,24},{24,16},{32,40},{40,32},{48,56},{56,48},{64,72... | collective-permute-start | bytes 786440 | tf_op jit(solution)/shard_map/ppermute | solution.py:304
  2.9 0.7 collective-permute-start.3
  3.5 0.9 %slice_bitcast_fusion = (bf16[2,128,128]{2,1,0:T(8,128)(2,1)S(1)}, bf16[2,128,128]{2,1,0:T(8,128)(2,1)S(1)}) fusion(bf16[2,8,128,128]{3,2,1,0:T(8,128)(2,1)} %bitcast.10), kind=kLoop, calls=%fused_computation | loop fusion | bytes 262144 | tf_op jit(solution)/shard_map/squeeze | solution.py:319
  4.5 1.2 %collective-permute-start = (bf16[2,128,128]{2,1,0:T(8,128)(2,1)S(1)}, bf16[2,128,128]{2,1,0:T(8,128)(2,1)S(1)}, u32[]{:S(2)}, u32[]{:S(2)}) collective-permute-start(bf16[2,128,128]{2,1,0:T(8,128)(2,1)S(1)} %get-tuple-element.36), channel_id=1, source_target_pairs={{0,1},{1,0},{2,3},{3,2},{4,5},{5,4},{6,7},{7,6},{8,9},{9,8},{10,11... | collective-permute-start | bytes 196616 | tf_op jit(solution)/shard_map/ppermute | solution.py:304
  5.7 2.8 %collective-permute-start.1 = (bf16[2,128,128]{2,1,0:T(8,128)(2,1)S(1)}, bf16[2,128,128]{2,1,0:T(8,128)(2,1)S(1)}, u32[]{:S(2)}, u32[]{:S(2)}) collective-permute-start(bf16[2,128,128]{2,1,0:T(8,128)(2,1)S(1)} %get-tuple-element.39), channel_id=1, source_target_pairs={{1,2},{3,4},{5,6},{2,1},{4,3},{6,5},{9,10},{11,12},{13,14},{10,9},... | collective-permute-start | bytes 196616 | tf_op jit(solution)/shard_map/ppermute | solution.py:310
  8.5 0.0 copy-done.2
  8.5 0.0 copy-start
  8.5 1.0 %copy-done = bf16[1,2,8,128,128]{4,3,2,1,0:T(8,128)(2,1)S(1)} copy-done((bf16[1,2,8,128,128]{4,3,2,1,0:T(8,128)(2,1)S(1)}, bf16[1,2,8,128,128]{4,3,2,1,0:T(8,128)(2,1)}, u32[]{:S(2)}) %copy-start) | copy-done | bytes 524312
  9.6 0.0 copy-start.3
  9.6 0.0 copy-start.4
  9.6 0.2 shard_map.93
  9.8 0.0 collective-permute-done.near_ref
  9.8 1.4 %collective-permute-done.1.far_ref = bf16[2,128,128]{2,1,0:T(8,128)(2,1)S(1)} collective-permute-done((bf16[2,128,128]{2,1,0:T(8,128)(2,1)S(1)}, bf16[2,128,128]{2,1,0:T(8,128)(2,1)S(1)}, u32[]{:S(2)}, u32[]{:S(2)}) %collective-permute-start.1) | collective-permute-done | bytes 65568 | tf_op jit(solution)/shard_map/ppermute | solution.py:310
  11.3 0.0 copy-done.3
  11.3 0.0 copy-done.4
  11.3 0.0 copy-start.5
  11.3 2.5 %shard_map.94 = (f32[2,4,2,128,128]{4,3,2,1,0:T(8,128)S(1)}, bf16[2,4,2,128,128]{4,3,2,1,0:T(8,128)(2,1)S(1)}, bf16[2,128,1280]{2,1,0:T(8,128)(2,1)S(1)}, bf16[2...) custom-call(bf16[2,8,128,128]{3,2,1,0:T(8,128)(2,1)S(1)} %get-tuple-element.38.x_ref, ...), custom_call_target="tpu_custom_call" | custom-call | flops 738197504 | bytes 4000000 | tf_op jit(solution)/shard_map/pallas_call | solution.py:275
  13.7 0.0 collective-permute-done.2.near_ref
  13.7 0.0 collective-permute-done.3.far_ref
  13.7 0.0 copy-done.5
  13.7 3.0 %shard_map.95 = (bf16[2,8,128,128]{3,2,1,0:T(8,128)(2,1)S(1)}, bf16[2,128,128]{2,1,0:T(8,128)(2,1)S(1)}, bf16[19,64,128]{2,1,0:T(8,128)(2,1)S(1)}, f32[15,64,128]{2,1,0:T(8,128)S(1)}) custom-call(f32[2,4,2,128,128]{4,3,2,1,0:T(8,128)S(1)} %get-tuple-element.41.slope_ref, bf16[2,128,1280]{2,1,0:T(8,128)(2,1)S(1)} %get-tuple-element.42.xt_ref, ...), custom_call_target="tpu_custom_call" | custom-call | flops 1409286144 | bytes 4000000 | tf_op jit(solution)/shard_map/pallas_call | solution.py:275
  16.7 0.0 copy-start.6
  16.8 1.7 %collective-permute-start.4 = (bf16[19,64,128]{2,1,0:T(8,128)(2,1)S(1)}, bf16[19,64,128]{2,1,0:T(8,128)(2,1)S(1)}, u32[]{:S(2)}, u32[]{:S(2)}) collective-permute-start(bf16[19,64,128]{2,1,0:T(8,128)(2,1)S(1)} %get-tuple-element.45), channel_id=1, source_target_pairs={{0,1},{1,0},{2,3},{3,2},{4,5},{5,4},{6,7},{7,6},{8,9},{9,8},{10,11... | collective-permute-start | bytes 933896 | tf_op jit(solution)/shard_map/ppermute | solution.py:304
  18.4 1.2 %collective-permute-done.4.got_ref.sent_ref = bf16[19,64,128]{2,1,0:T(8,128)(2,1)S(1)} collective-permute-done((bf16[19,64,128]{2,1,0:T(8,128)(2,1)S(1)}, bf16[19,64,128]{2,1,0:T(8,128)(2,1)S(1)}, u32[]{:S(2)}, u32[]{:S(2)}) %collective-permute-start.4) | collective-permute-done | bytes 311328 | tf_op jit(solution)/shard_map/ppermute | solution.py:304
  19.6 0.7 %shard_map.96 = bf16[16,64,128]{2,1,0:T(8,128)(2,1)} custom-call(f32[15,64,128]{2,1,0:T(8,128)S(1)} %get-tuple-element.44.keep_ref, bf16[19,64,128]{2,1,0:T(8,128)(2,1)S(1)} %collective-permute-done.4.got_ref.sent_ref), custom_call_target="tpu_custom_call" | custom-call | bytes 4000000 | tf_op jit(solution)/shard_map/pallas_call | solution.py:275
  20.4 0.0 copy-done.6
  20.4 10.0 %all-to-all-start = ((bf16[16,64,128]{2,1,0:T(8,128)(2,1)}), bf16[16,64,128]{2,1,0:T(8,128)(2,1)S(1)}, u32[]{:S(2)}, u32[]{:S(2)}) async-start(bf16[16,64,128]{2,1,0:T(8,128)(2,1)} %shard_map.96), calls=%async_computation | async-start | bytes 524288 | tf_op jit(solution)/shard_map/all_to_all | solution.py:300
  30.3 0.6 collective-permute-start.6
  30.9 0.7 collective-permute-start.7
  31.6 3.3 %all-to-all-done = bf16[16,64,128]{2,1,0:T(8,128)(2,1)S(1)} async-done(((bf16[16,64,128]{2,1,0:T(8,128)(2,1)}), bf16[16,64,128]{2,1,0:T(8,128)(2,1)S(1)}, u32[]{:S(2)}, u32[]{:S(2)}) %all-to-all-start) | async-done | bytes 262176 | tf_op jit(solution)/shard_map/all_to_all | solution.py:300
  35.0 0.7 broadcast_in_dim.9
  35.6 9.2 %all-to-all-start.1 = ((bf16[8,64,128]{2,1,0:T(8,128)(2,1)}), bf16[8,64,128]{2,1,0:T(8,128)(2,1)}, u32[]{:S(2)}, u32[]{:S(2)}) async-start(bf16[8,64,128]{2,1,0:T(8,128)(2,1)} %broadcast_in_dim.9), calls=%async_computation.1 | async-start | bytes 262144 | tf_op jit(solution)/shard_map/all_to_all | solution.py:300
  44.9 0.0 copy-start.1
  44.9 4.4 %collective-permute-start.5 = (bf16[2,128,128]{2,1,0:T(8,128)(2,1)S(1)}, bf16[2,128,128]{2,1,0:T(8,128)(2,1)S(1)}, u32[]{:S(2)}, u32[]{:S(2)}) collective-permute-start(bf16[2,128,128]{2,1,0:T(8,128)(2,1)S(1)} %get-tuple-element.48), channel_id=1, source_target_pairs={{1,2},{3,4},{5,6},{2,1},{4,3},{6,5},{9,10},{11,12},{13,14},{10,9},... | collective-permute-start | bytes 196616 | tf_op jit(solution)/shard_map/ppermute | solution.py:310
  49.3 0.0 collective-permute-done.6.near_ref
  49.3 0.0 collective-permute-done.7.far_ref
  49.3 2.3 %collective-permute-done.5.g_far_ref = bf16[2,128,128]{2,1,0:T(8,128)(2,1)S(1)} collective-permute-done((bf16[2,128,128]{2,1,0:T(8,128)(2,1)S(1)}, bf16[2,128,128]{2,1,0:T(8,128)(2,1)S(1)}, u32[]{:S(2)}, u32[]{:S(2)}) %collective-permute-start.5) | collective-permute-done | bytes 65568 | tf_op jit(solution)/shard_map/ppermute | solution.py:310
  51.6 0.0 all-to-all-done.1
  51.6 0.9 %reduce_sum.25 = bf16[64,128]{1,0:T(8,128)(2,1)S(1)} reduce(bf16[8,64,128]{2,1,0:T(8,128)(2,1)} %all-to-all-done.1, bf16[]{:T(256)} %constant.3.clone.1), dimensions={0}, to_apply=%region_1.0 | reduce | flops 57344 | bytes 147458 | tf_op jit(solution)/shard_map/reduce_sum | solution.py:353
  52.5 0.8 %broadcast_in_dim.10 = bf16[16,64,128]{2,1,0:T(8,128)(2,1)} broadcast(bf16[64,128]{1,0:T(8,128)(2,1)S(1)} %reduce_sum.25), dimensions={1,2} | broadcast | bytes 278528 | tf_op jit(solution)/shard_map/broadcast_in_dim | solution.py:354
  53.3 7.2 %all-to-all-start.2 = ((bf16[16,64,128]{2,1,0:T(8,128)(2,1)}), bf16[16,64,128]{2,1,0:T(8,128)(2,1)S(1)}, u32[]{:S(2)}, u32[]{:S(2)}) async-start(bf16[16,64,128]{2,1,0:T(8,128)(2,1)} %broadcast_in_dim.10), calls=%async_computation.2 | async-start | bytes 524288 | tf_op jit(solution)/shard_map/all_to_all | solution.py:300
  60.5 0.0 copy-done.1
  60.5 0.0 copy-start.7
  60.5 1.6 %shard_map.97 = bf16[8,128,128]{2,1,0:T(8,128)(2,1)} custom-call(bf16[2,8,128,128]{3,2,1,0:T(8,128)(2,1)S(1)} %bitcast.12, bf16[2,8,128,128]{3,2,1,0:T(8,128)(2,1)S(1)} %bitcast.13, bf16[8,128,128]{2,1,0:T(8,128)(2,1)S(1)} %collective-permute-done.6.near_ref, bf16[8,128,128]{2,1,0:T(8,128)(2,1)S(1)} %collective-permute-done.7.far_ref, ...), custom_call_target="tpu_custom_call" | custom-call | flops 335544320 | bytes 4000000 | tf_op jit(solution)/shard_map/pallas_call | solution.py:275
  62.1 0.0 copy-done.7
  62.1 2.1 %shard_map.98 = bf16[2,4,2,128,128]{4,3,2,1,0:T(8,128)(2,1)} custom-call(bf16[2,8,128,128]{3,2,1,0:T(8,128)(2,1)S(1)} %copy-done.7, bf16[19,64,128]{2,1,0:T(8,128)(2,1)S(1)} %collective-permute-done.4.got_ref.sent_ref, bf16[2,128,128]{2,1,0:T(8,128)(2,1)S(1)} %collective-permute-done.5.g_far_ref, bf16[8,128,128]{2,1,0:T(8,128)(2,1)S(1)} %bitcast.17, ...), custom_call_target="tpu_custom_call" | custom-call | flops 738197504 | bytes 4000000 | tf_op jit(solution)/shard_map/pallas_call | solution.py:275
  64.2 0.3 all-to-all-done.2.mine_ref
  64.5 2.5 %collective-permute-start.8 = (bf16[16,64,128]{2,1,0:T(8,128)(2,1)S(1)}, bf16[16,64,128]{2,1,0:T(8,128)(2,1)S(1)}, u32[]{:S(2)}, u32[]{:S(2)}) collective-permute-start(bf16[16,64,128]{2,1,0:T(8,128)(2,1)S(1)} %all-to-all-done.2.mine_ref), channel_id=1, source_target_pairs={{0,1},{1,0},{2,3},{3,2},{4,5},{5,4},{6,7},{7,6},{8,9},{9,8},{10,11... | collective-permute-start | bytes 786440 | tf_op jit(solution)/shard_map/ppermute | solution.py:304
  67.0 1.2 %collective-permute-done.8.other_ref = bf16[16,64,128]{2,1,0:T(8,128)(2,1)S(1)} collective-permute-done((bf16[16,64,128]{2,1,0:T(8,128)(2,1)S(1)}, bf16[16,64,128]{2,1,0:T(8,128)(2,1)S(1)}, u32[]{:S(2)}, u32[]{:S(2)}) %collective-permute-start.8) | collective-permute-done | bytes 262176 | tf_op jit(solution)/shard_map/ppermute | solution.py:304
  68.2 1.0 %shard_map.99 = (f32[9,128,128]{2,1,0:T(8,128)}, f32[3,128,128]{2,1,0:T(8,128)}, f32[3,128,128]{2,1,0:T(8,128)}) custom-call(bf16[16,64,128]{2,1,0:T(8,128)(2,1)S(1)} %all-to-all-done.2.mine_ref, bf16[16,64,128]{2,1,0:T(8,128)(2,1)S(1)} %collective-permute-done.8.other_ref), custom_call_target="tpu_custom_call" | custom-call | bytes 4000000 | tf_op jit(solution)/shard_map/pallas_call | solution.py:275
  (2 shorter events, 0.1 us)
Async XLA Ops:
  0.6 7.9 %copy-start.2 = (bf16[3,3,128,128]{3,2,1,0:T(8,128)(2,1)S(1)}, bf16[3,3,128,128]{3,2,1,0:T(8,128)(2,1)}, u32[]{:S(2)}) copy-start(bf16[3,3,128,128]{3,2,1,0:T(8,128)(2,1)} %w_ref.1) | copy-start | bytes 884740
  0.6 13.1 %collective-permute-start.2 = (bf16[8,128,128]{2,1,0:T(8,128)(2,1)}, bf16[8,128,128]{2,1,0:T(8,128)(2,1)S(1)}, u32[]{:S(2)}, u32[]{:S(2)}) collective-permute-start(bf16[8,128,128]{2,1,0:T(8,128)(2,1)} %bitcast.14), channel_id=1, source_target_pairs={{0,8},{8,0},{16,24},{24,16},{32,40},{40,32},{48,56},{56,48},{64,72... | collective-permute-start | bytes 786440 | tf_op jit(solution)/shard_map/ppermute | solution.py:304
  2.9 10.9 %collective-permute-start.3 = (bf16[8,128,128]{2,1,0:T(8,128)(2,1)}, bf16[8,128,128]{2,1,0:T(8,128)(2,1)S(1)}, u32[]{:S(2)}, u32[]{:S(2)}) collective-permute-start(bf16[8,128,128]{2,1,0:T(8,128)(2,1)} %bitcast.15), channel_id=1, source_target_pairs={{8,16},{24,32},{40,48},{56,64},{72,80},{88,96},{104,112},{16,8},{3... | collective-permute-start | bytes 786440 | tf_op jit(solution)/shard_map/ppermute | solution.py:310
  4.5 5.4 %collective-permute-start = (bf16[2,128,128]{2,1,0:T(8,128)(2,1)S(1)}, bf16[2,128,128]{2,1,0:T(8,128)(2,1)S(1)}, u32[]{:S(2)}, u32[]{:S(2)}) collective-permute-start(bf16[2,128,128]{2,1,0:T(8,128)(2,1)S(1)} %get-tuple-element.36), channel_id=1, source_target_pairs={{0,1},{1,0},{2,3},{3,2},{4,5},{5,4},{6,7},{7,6},{8,9},{9,8},{10,11... | collective-permute-start | bytes 196616 | tf_op jit(solution)/shard_map/ppermute | solution.py:304
  5.7 5.6 %collective-permute-start.1 = (bf16[2,128,128]{2,1,0:T(8,128)(2,1)S(1)}, bf16[2,128,128]{2,1,0:T(8,128)(2,1)S(1)}, u32[]{:S(2)}, u32[]{:S(2)}) collective-permute-start(bf16[2,128,128]{2,1,0:T(8,128)(2,1)S(1)} %get-tuple-element.39), channel_id=1, source_target_pairs={{1,2},{3,4},{5,6},{2,1},{4,3},{6,5},{9,10},{11,12},{13,14},{10,9},... | collective-permute-start | bytes 196616 | tf_op jit(solution)/shard_map/ppermute | solution.py:310
  8.5 1.0 %copy-start = (bf16[1,2,8,128,128]{4,3,2,1,0:T(8,128)(2,1)S(1)}, bf16[1,2,8,128,128]{4,3,2,1,0:T(8,128)(2,1)}, u32[]{:S(2)}) copy-start(bf16[1,2,8,128,128]{4,3,2,1,0:T(8,128)(2,1)} %param.5) | copy-start | bytes 1572868
  9.6 1.7 %copy-start.3 = (bf16[3,128,128]{2,1,0:T(8,128)(2,1)S(1)}, bf16[3,128,128]{2,1,0:T(8,128)(2,1)}, u32[]{:S(2)}) copy-start(bf16[3,128,128]{2,1,0:T(8,128)(2,1)} %wt_ref.5) | copy-start | bytes 294916
  9.6 1.7 %copy-start.4 = (bf16[3,128,128]{2,1,0:T(8,128)(2,1)S(1)}, bf16[3,128,128]{2,1,0:T(8,128)(2,1)}, u32[]{:S(2)}) copy-start(bf16[3,128,128]{2,1,0:T(8,128)(2,1)} %wd_ref.7) | copy-start | bytes 294916
  11.3 2.5 %copy-start.5 = (bf16[1,1,8,128,128]{4,3,2,1,0:T(8,128)(2,1)S(1)}, bf16[1,1,8,128,128]{4,3,2,1,0:T(8,128)(2,1)}, u32[]{:S(2)}) copy-start(bf16[1,1,8,128,128]{4,3,2,1,0:T(8,128)(2,1)} %param.9) | copy-start | bytes 786436
  16.7 3.6 %copy-start.6 = (bf16[2,8,128,128]{3,2,1,0:T(8,128)(2,1)}, bf16[2,8,128,128]{3,2,1,0:T(8,128)(2,1)S(1)}, u32[]{:S(2)}) copy-start(bf16[2,8,128,128]{3,2,1,0:T(8,128)(2,1)S(1)} %get-tuple-element.55.gpre_ref) | copy-start | bytes 1572868
  16.8 2.9 %collective-permute-start.4 = (bf16[19,64,128]{2,1,0:T(8,128)(2,1)S(1)}, bf16[19,64,128]{2,1,0:T(8,128)(2,1)S(1)}, u32[]{:S(2)}, u32[]{:S(2)}) collective-permute-start(bf16[19,64,128]{2,1,0:T(8,128)(2,1)S(1)} %get-tuple-element.45), channel_id=1, source_target_pairs={{0,1},{1,0},{2,3},{3,2},{4,5},{5,4},{6,7},{7,6},{8,9},{9,8},{10,11... | collective-permute-start | bytes 933896 | tf_op jit(solution)/shard_map/ppermute | solution.py:304
  20.4 14.5 %all-to-all-start = ((bf16[16,64,128]{2,1,0:T(8,128)(2,1)}), bf16[16,64,128]{2,1,0:T(8,128)(2,1)S(1)}, u32[]{:S(2)}, u32[]{:S(2)}) async-start(bf16[16,64,128]{2,1,0:T(8,128)(2,1)} %shard_map.96), calls=%async_computation | async-start | bytes 524288 | tf_op jit(solution)/shard_map/all_to_all | solution.py:300
  30.3 18.9 %collective-permute-start.6 = (bf16[8,128,128]{2,1,0:T(8,128)(2,1)}, bf16[8,128,128]{2,1,0:T(8,128)(2,1)S(1)}, u32[]{:S(2)}, u32[]{:S(2)}) collective-permute-start(bf16[8,128,128]{2,1,0:T(8,128)(2,1)} %get-tuple-element.49), channel_id=1, source_target_pairs={{0,8},{8,0},{16,24},{24,16},{32,40},{40,32},{48,56},{56,48},{64,72... | collective-permute-start | bytes 786440 | tf_op jit(solution)/shard_map/ppermute | solution.py:304
  30.9 18.4 %collective-permute-start.7 = (bf16[8,128,128]{2,1,0:T(8,128)(2,1)S(1)}, bf16[8,128,128]{2,1,0:T(8,128)(2,1)S(1)}, u32[]{:S(2)}, u32[]{:S(2)}) collective-permute-start(bf16[8,128,128]{2,1,0:T(8,128)(2,1)S(1)} %get-tuple-element.50), channel_id=1, source_target_pairs={{8,16},{24,32},{40,48},{56,64},{72,80},{88,96},{104,112},{16,8},{3... | collective-permute-start | bytes 786440 | tf_op jit(solution)/shard_map/ppermute | solution.py:310
  35.6 16.0 %all-to-all-start.1 = ((bf16[8,64,128]{2,1,0:T(8,128)(2,1)}), bf16[8,64,128]{2,1,0:T(8,128)(2,1)}, u32[]{:S(2)}, u32[]{:S(2)}) async-start(bf16[8,64,128]{2,1,0:T(8,128)(2,1)} %broadcast_in_dim.9), calls=%async_computation.1 | async-start | bytes 262144 | tf_op jit(solution)/shard_map/all_to_all | solution.py:300
  44.9 15.6 %copy-start.1 = (bf16[1,2,8,128,128]{4,3,2,1,0:T(8,128)(2,1)S(1)}, bf16[1,2,8,128,128]{4,3,2,1,0:T(8,128)(2,1)}, u32[]{:S(2)}) copy-start(bf16[1,2,8,128,128]{4,3,2,1,0:T(8,128)(2,1)} %param.5) | copy-start | bytes 1572868
  44.9 6.8 %collective-permute-start.5 = (bf16[2,128,128]{2,1,0:T(8,128)(2,1)S(1)}, bf16[2,128,128]{2,1,0:T(8,128)(2,1)S(1)}, u32[]{:S(2)}, u32[]{:S(2)}) collective-permute-start(bf16[2,128,128]{2,1,0:T(8,128)(2,1)S(1)} %get-tuple-element.48), channel_id=1, source_target_pairs={{1,2},{3,4},{5,6},{2,1},{4,3},{6,5},{9,10},{11,12},{13,14},{10,9},... | collective-permute-start | bytes 196616 | tf_op jit(solution)/shard_map/ppermute | solution.py:310
  53.3 11.2 %all-to-all-start.2 = ((bf16[16,64,128]{2,1,0:T(8,128)(2,1)}), bf16[16,64,128]{2,1,0:T(8,128)(2,1)S(1)}, u32[]{:S(2)}, u32[]{:S(2)}) async-start(bf16[16,64,128]{2,1,0:T(8,128)(2,1)} %broadcast_in_dim.10), calls=%async_computation.2 | async-start | bytes 524288 | tf_op jit(solution)/shard_map/all_to_all | solution.py:300
  60.5 1.6 %copy-start.7 = (bf16[2,8,128,128]{3,2,1,0:T(8,128)(2,1)S(1)}, bf16[2,8,128,128]{3,2,1,0:T(8,128)(2,1)}, u32[]{:S(2)}) copy-start(bf16[2,8,128,128]{3,2,1,0:T(8,128)(2,1)} %copy-done.6) | copy-start | bytes 1572868
  64.5 3.7 %collective-permute-start.8 = (bf16[16,64,128]{2,1,0:T(8,128)(2,1)S(1)}, bf16[16,64,128]{2,1,0:T(8,128)(2,1)S(1)}, u32[]{:S(2)}, u32[]{:S(2)}) collective-permute-start(bf16[16,64,128]{2,1,0:T(8,128)(2,1)S(1)} %all-to-all-done.2.mine_ref), channel_id=1, source_target_pairs={{0,1},{1,0},{2,3},{3,2},{4,5},{5,4},{6,7},{7,6},{8,9},{9,8},{10,11... | collective-permute-start | bytes 786440 | tf_op jit(solution)/shard_map/ppermute | solution.py:304

commit v5 on v4

--- a/solution.py
+++ b/solution.py
@@ -334,7 +334,7 @@
         (here, x_near, x_far, wide, w_temporal, w_down), 11,
         scratch=[rows_scratch],
     )
-    t_near, t_far = swap(to_near, time, 1), swap_far(to_far, time)
+    to_t_near, to_t_far = to_near, to_far
     gpre, to_far, send, keep = call(
         grads_kernel,
         [((2, 8, 128, C), BF16), edge, ((19, 64, C), BF16), ((15, 64, C), F32)],
@@ -344,12 +344,13 @@
     near = swap(send, "core", 1)
     (half,) = call(merge_kernel, [((16, 64, C), BF16)], (keep, near), 0)
     got = exchange(half, PLANE, 16)
-    got, to_far = lax.optimization_barrier((got, to_far))
+    got, to_far, to_t_near, to_t_far = lax.optimization_barrier((got, to_far, to_t_near, to_t_far))
     total = jnp.sum(got.astype(F32), axis=0)
+    t_near, t_far = swap(to_t_near, time, 1), swap_far(to_t_far, time)
     g_far = swap_far(to_far, rows)
     column = jnp.broadcast_to(total.astype(BF16), (8, 64, C))
     column = exchange(column, "z", 8)
-    column, g_far, t_near, t_far = lax.optimization_barrier((column, g_far, t_near, t_far))
+    column, g_far = lax.optimization_barrier((column, g_far))
     total = jnp.sum(column.astype(F32), axis=0)
     out = jnp.broadcast_to(total.astype(BF16), (16, 64, C))
     out = exchange(out, PLANE, 16)

time: 69.8 us -> 68.2 us (0.977)
  blocking collectives: 0 us -> 13.6 us
  starting transfers between devices: 43.1 us -> 33.6 us
  waiting for transfers between devices: 9.77 us -> 5.38 us
  Pallas kernels: 11.2 us -> 9.75 us
  local copies, waits for them, and re-layouts: 3.39 us -> 4.42 us
  other arithmetic: 0.97 us -> 0.07 us
    all_to_all x0 -> x1, blocking collectives: none -> 13.6 us  [exchange(): return lax.all_to_all(x, axis, 0, 0, axis_index_groups=groups, tiled=True)]
    all_to_all x3 -> x2, starting transfers between devices: 26.3 us -> 18.3 us  [exchange(): return lax.all_to_all(x, axis, 0, 0, axis_index_groups=groups, tiled=True)]
    all_to_all x3 -> x2, waiting for transfers between devices: 3.63 us -> 0.01 us  [exchange(): return lax.all_to_all(x, axis, 0, 0, axis_index_groups=groups, tiled=True)]
    pallas_call x7, Pallas kernels: 10.9 us -> 9.51 us  [call(): pl.pallas_call(kernel, out_shape=[jax.ShapeDtypeStruct(s, d) for s, d in...]
    ppermute x4, waiting for transfers between devices: 3.74 us -> 2.43 us  [swap_far(): return lax.ppermute(x, axis, pairs + [(b, a) for a, b in pairs])]
    ppermute x5, starting transfers between devices: 8.21 us -> 6.92 us  [swap(): lax.ppermute(x, axis, [(i, i ^ mask) for i in range(lax.axis_size(axis))])]
    unnamed x16, local copies, waits for them, and re-layouts: 1.07 us -> 2.1 us
    reduce_sum x1, other arithmetic: 0.93 us -> 0.02 us  [per_device(): total = jnp.sum(column.astype(F32), axis=0)]
  transfers between devices with their start and end apart: 12 -> 11, of which waited for: 6 -> 5; matrix products, arithmetic and copies ran while one was open for 2% -> 2% of each run, Pallas kernels for 9% -> 8%
where the time goes in v5:
time: 68.2 us; the launch traced here: 67.6 us
  starting transfers between devices  33.6 us (49%)
  blocking collectives  13.6 us (20%)
  Pallas kernels  9.75 us (14%)
  waiting for transfers between devices  5.38 us (8%)
  local copies, waits for them, and re-layouts  4.42 us (6%)
  between operations  0.77 us (1%)
    all_to_all x2, starting transfers between devices, exchange(): return lax.all_to_all(x, axis, 0, 0, axis_index_groups=groups, tiled=True)  18.3 us
    all_to_all x1, blocking collectives, exchange(): return lax.all_to_all(x, axis, 0, 0, axis_index_groups=groups, tiled=True)  13.6 us
    pallas_call x7, Pallas kernels, call(): pl.pallas_call(kernel, out_shape=[jax.ShapeDtypeStruct(s, d) for s, d in...  9.51 us
    ppermute x4, starting transfers between devices, swap_far(): return lax.ppermute(x, axis, pairs + [(b, a) for a, b in pairs])  8.43 us
    ppermute x5, starting transfers between devices, swap(): lax.ppermute(x, axis, [(i, i ^ mask) for i in range(lax.axis_size(axis))])  6.92 us
    ppermute x5, waiting for transfers between devices, swap(): lax.ppermute(x, axis, [(i, i ^ mask) for i in range(lax.axis_size(axis))])  2.95 us
    ppermute x4, waiting for transfers between devices, swap_far(): return lax.ppermute(x, axis, pairs + [(b, a) for a, b in pairs])  2.43 us
    unnamed x16, local copies, waits for them, and re-layouts  2.1 us
  transfers between devices with their start and end apart: 11, of which 5 were waited for; matrix products, arithmetic and copies ran while one was open for 2% of the time, Pallas kernels for 8%

profile of v5, /device:TPU:1, one launch (start us, length us, event | category | flops | bytes accessed | tf_op | source)
XLA Modules:
  0.0 67.6 jit_solution(14816173184208725740)
XLA Ops:
  0.6 0.0 copy-start.2
  0.6 2.2 %collective-permute-start.2 = (bf16[8,128,128]{2,1,0:T(8,128)(2,1)}, bf16[8,128,128]{2,1,0:T(8,128)(2,1)S(1)}, u32[]{:S(2)}, u32[]{:S(2)}) collective-permute-start(bf16[8,128,128]{2,1,0:T(8,128)(2,1)} %bitcast.14), channel_id=1, source_target_pairs={{0,8},{8,0},{16,24},{24,16},{32,40},{40,32},{48,56},{56,48},{64,72... | collective-permute-start | bytes 786440 | tf_op jit(solution)/shard_map/ppermute | solution.py:304
  2.9 0.7 collective-permute-start.3
  3.5 0.9 %slice_bitcast_fusion = (bf16[2,128,128]{2,1,0:T(8,128)(2,1)S(1)}, bf16[2,128,128]{2,1,0:T(8,128)(2,1)S(1)}) fusion(bf16[2,8,128,128]{3,2,1,0:T(8,128)(2,1)} %bitcast.10), kind=kLoop, calls=%fused_computation | loop fusion | bytes 262144 | tf_op jit(solution)/shard_map/squeeze | solution.py:319
  4.5 1.2 %collective-permute-start = (bf16[2,128,128]{2,1,0:T(8,128)(2,1)S(1)}, bf16[2,128,128]{2,1,0:T(8,128)(2,1)S(1)}, u32[]{:S(2)}, u32[]{:S(2)}) collective-permute-start(bf16[2,128,128]{2,1,0:T(8,128)(2,1)S(1)} %get-tuple-element.36), channel_id=1, source_target_pairs={{0,1},{1,0},{2,3},{3,2},{4,5},{5,4},{6,7},{7,6},{8,9},{9,8},{10,11... | collective-permute-start | bytes 196616 | tf_op jit(solution)/shard_map/ppermute | solution.py:304
  5.7 2.8 %collective-permute-start.1 = (bf16[2,128,128]{2,1,0:T(8,128)(2,1)S(1)}, bf16[2,128,128]{2,1,0:T(8,128)(2,1)S(1)}, u32[]{:S(2)}, u32[]{:S(2)}) collective-permute-start(bf16[2,128,128]{2,1,0:T(8,128)(2,1)S(1)} %get-tuple-element.39), channel_id=1, source_target_pairs={{1,2},{3,4},{5,6},{2,1},{4,3},{6,5},{9,10},{11,12},{13,14},{10,9},... | collective-permute-start | bytes 196616 | tf_op jit(solution)/shard_map/ppermute | solution.py:310
  8.5 0.0 copy-done.2
  8.5 0.0 copy-start
  8.5 1.0 %copy-done = bf16[1,2,8,128,128]{4,3,2,1,0:T(8,128)(2,1)S(1)} copy-done((bf16[1,2,8,128,128]{4,3,2,1,0:T(8,128)(2,1)S(1)}, bf16[1,2,8,128,128]{4,3,2,1,0:T(8,128)(2,1)}, u32[]{:S(2)}) %copy-start) | copy-done | bytes 524312
  9.6 0.0 copy-start.3
  9.6 0.0 copy-start.4
  9.6 0.2 shard_map.93
  9.8 0.0 collective-permute-done.near_ref
  9.8 1.4 %collective-permute-done.1.far_ref = bf16[2,128,128]{2,1,0:T(8,128)(2,1)S(1)} collective-permute-done((bf16[2,128,128]{2,1,0:T(8,128)(2,1)S(1)}, bf16[2,128,128]{2,1,0:T(8,128)(2,1)S(1)}, u32[]{:S(2)}, u32[]{:S(2)}) %collective-permute-start.1) | collective-permute-done | bytes 65568 | tf_op jit(solution)/shard_map/ppermute | solution.py:310
  11.3 0.0 copy-done.3
  11.3 0.0 copy-done.4
  11.3 0.0 copy-start.5
  11.3 1.8 %shard_map.94 = (f32[2,4,2,128,128]{4,3,2,1,0:T(8,128)S(1)}, bf16[2,4,2,128,128]{4,3,2,1,0:T(8,128)(2,1)S(1)}, bf16[2,128,1280]{2,1,0:T(8,128)(2,1)S(1)}, bf16[2...) custom-call(bf16[2,8,128,128]{3,2,1,0:T(8,128)(2,1)S(1)} %get-tuple-element.38.x_ref,, ...), custom_call_target="tpu_custom_call" | custom-call | flops 738197504 | bytes 4000000 | tf_op jit(solution)/shard_map/pallas_call | solution.py:275
  13.0 0.5 collective-permute-done.2.near_ref
  13.6 0.0 collective-permute-done.3.far_ref
  13.6 0.0 copy-done.5
  13.6 3.0 %shard_map.95 = (bf16[2,8,128,128]{3,2,1,0:T(8,128)(2,1)S(1)}, bf16[2,128,128]{2,1,0:T(8,128)(2,1)S(1)}, bf16[19,64,128]{2,1,0:T(8,128)(2,1)S(1)}, f32[15,64,128]{2,1,0:T(8,128)S(1)}) custom-call(f32[2,4,2,128,128]{4,3,2,1,0:T(8,128)S(1)} %get-tuple-element.41.slope_ref, bf16[2,128,1280]{2,1,0:T(8,128)(2,1)S(1)} %get-tuple-element.42.xt_ref, ...), custom_call_target="tpu_custom_call" | custom-call | flops 1409286144 | bytes 4000000 | tf_op jit(solution)/shard_map/pallas_call | solution.py:275
  16.6 0.0 copy-start.6
  16.6 1.8 %collective-permute-start.4 = (bf16[19,64,128]{2,1,0:T(8,128)(2,1)S(1)}, bf16[19,64,128]{2,1,0:T(8,128)(2,1)S(1)}, u32[]{:S(2)}, u32[]{:S(2)}) collective-permute-start(bf16[19,64,128]{2,1,0:T(8,128)(2,1)S(1)} %get-tuple-element.45), channel_id=1, source_target_pairs={{0,1},{1,0},{2,3},{3,2},{4,5},{5,4},{6,7},{7,6},{8,9},{9,8},{10,11... | collective-permute-start | bytes 933896 | tf_op jit(solution)/shard_map/ppermute | solution.py:304
  18.4 1.2 %collective-permute-done.4.got_ref.sent_ref = bf16[19,64,128]{2,1,0:T(8,128)(2,1)S(1)} collective-permute-done((bf16[19,64,128]{2,1,0:T(8,128)(2,1)S(1)}, bf16[19,64,128]{2,1,0:T(8,128)(2,1)S(1)}, u32[]{:S(2)}, u32[]{:S(2)}) %collective-permute-start.4) | collective-permute-done | bytes 311328 | tf_op jit(solution)/shard_map/ppermute | solution.py:304
  19.7 0.0 copy-done.6
  19.7 13.6 %all_to_all.15 = bf16[16,64,128]{2,1,0:T(8,128)(2,1)S(1)} all-to-all(bf16[16,64,128]{2,1,0:T(8,128)(2,1)S(1)} %shard_map.96), channel_id=1, replica_groups={{142,140,138,136,134,132,130,128,14,12,10,8,6,4,2,0},{143,141,139,137,1..., dimensions={0} | all-to-all | bytes 524288 | tf_op jit(solution)/shard_map/all_to_all | solution.py:300
  33.4 0.7 broadcast_in_dim.9
  34.1 9.2 %all-to-all-start.1 = ((bf16[8,64,128]{2,1,0:T(8,128)(2,1)}), bf16[8,64,128]{2,1,0:T(8,128)(2,1)S(1)}, u32[]{:S(2)}, u32[]{:S(2)}) async-start(bf16[8,64,128]{2,1,0:T(8,128)(2,1)} %broadcast_in_dim.9), calls=%async_computation.1 | async-start | bytes 262144 | tf_op jit(solution)/shard_map/all_to_all | solution.py:300
  43.3 4.3 %collective-permute-start.5 = (bf16[2,128,128]{2,1,0:T(8,128)(2,1)S(1)}, bf16[2,128,128]{2,1,0:T(8,128)(2,1)S(1)}, u32[]{:S(2)}, u32[]{:S(2)}) collective-permute-start(bf16[2,128,128]{2,1,0:T(8,128)(2,1)S(1)} %get-tuple-element.50), channel_id=1, source_target_pairs={{1,2},{3,4},{5,6},{2,1},{4,3},{6,5},{9,10},{11,12},{13,14},{10,9},... | collective-permute-start | bytes 196616 | tf_op jit(solution)/shard_map/ppermute | solution.py:310
  47.5 0.5 collective-permute-start.6
  48.1 0.7 collective-permute-start.7
  48.8 1.0 %collective-permute-done.5.g_far_ref = bf16[2,128,128]{2,1,0:T(8,128)(2,1)S(1)} collective-permute-done((bf16[2,128,128]{2,1,0:T(8,128)(2,1)S(1)}, bf16[2,128,128]{2,1,0:T(8,128)(2,1)S(1)}, u32[]{:S(2)}, u32[]{:S(2)}) %collective-permute-start.5) | collective-permute-done | bytes 65568 | tf_op jit(solution)/shard_map/ppermute | solution.py:310
  49.8 0.0 all-to-all-done.1
  49.8 0.8 %broadcast_in_dim.10 = bf16[16,64,128]{2,1,0:T(8,128)(2,1)} broadcast(bf16[64,128]{1,0:T(8,128)(2,1)S(1)} %reduce_sum.25), dimensions={1,2} | broadcast | bytes 278528 | tf_op jit(solution)/shard_map/broadcast_in_dim | solution.py:355
  50.6 9.0 %all-to-all-start.2 = ((bf16[16,64,128]{2,1,0:T(8,128)(2,1)}), bf16[16,64,128]{2,1,0:T(8,128)(2,1)S(1)}, u32[]{:S(2)}, u32[]{:S(2)}) async-start(bf16[16,64,128]{2,1,0:T(8,128)(2,1)} %broadcast_in_dim.10), calls=%async_computation.2 | async-start | bytes 524288 | tf_op jit(solution)/shard_map/all_to_all | solution.py:300
  59.6 0.0 copy-start.7
  59.6 1.0 %copy-done.7 = bf16[2,8,128,128]{3,2,1,0:T(8,128)(2,1)S(1)} copy-done((bf16[2,8,128,128]{3,2,1,0:T(8,128)(2,1)S(1)}, bf16[2,8,128,128]{3,2,1,0:T(8,128)(2,1)}, u32[]{:S(2)}) %copy-start.7) | copy-done | bytes 524312
  60.7 0.0 copy-start.1
  60.7 2.1 %shard_map.98 = bf16[2,4,2,128,128]{4,3,2,1,0:T(8,128)(2,1)} custom-call(bf16[2,8,128,128]{3,2,1,0:T(8,128)(2,1)S(1)} %copy-done.7, bf16[19,64,128]{2,1,0:T(8,128)(2,1)S(1)} %collective-permute-done.4.got_ref.sent_ref, bf16[2,128,128]{2,1,0:T(8,128)(2,1)S(1)} %collective-permute-done.5.g_far_ref, bf16[8,128,128]{2,1,0:T(8,128)(2,1)S(1)} %bitcast.17, ...), custom_call_target="tpu_custom_call" | custom-call | flops 738197504 | bytes 4000000 | tf_op jit(solution)/shard_map/pallas_call | solution.py:275
  62.8 0.0 collective-permute-done.6.near_ref
  62.8 0.0 collective-permute-done.7.far_ref
  62.8 0.0 copy-done.1
  62.8 1.6 %shard_map.97 = bf16[8,128,128]{2,1,0:T(8,128)(2,1)} custom-call(bf16[2,8,128,128]{3,2,1,0:T(8,128)(2,1)S(1)} %bitcast.12, bf16[2,8,128,128]{3,2,1,0:T(8,128)(2,1)S(1)} %bitcast.13, bf16[8,128,128]{2,1,0:T(8,128)(2,1)S(1)} %collective-permute-done.6.near_ref, bf16[8,128,128]{2,1,0:T(8,128)(2,1)S(1)} %collective-permute-done.7.far_ref, ...), custom_call_target="tpu_custom_call" | custom-call | flops 335544320 | bytes 4000000 | tf_op jit(solution)/shard_map/pallas_call | solution.py:275
  64.4 0.0 all-to-all-done.2.mine_ref
  64.4 1.1 %collective-permute-start.8 = (bf16[16,64,128]{2,1,0:T(8,128)(2,1)S(1)}, bf16[16,64,128]{2,1,0:T(8,128)(2,1)S(1)}, u32[]{:S(2)}, u32[]{:S(2)}) collective-permute-start(bf16[16,64,128]{2,1,0:T(8,128)(2,1)S(1)} %all-to-all-done.2.mine_ref), channel_id=1, source_target_pairs={{0,1},{1,0},{2,3},{3,2},{4,5},{5,4},{6,7},{7,6},{8,9},{9,8},{10,11... | collective-permute-start | bytes 786440 | tf_op jit(solution)/shard_map/ppermute | solution.py:304
  65.5 1.2 %collective-permute-done.8.other_ref = bf16[16,64,128]{2,1,0:T(8,128)(2,1)S(1)} collective-permute-done((bf16[16,64,128]{2,1,0:T(8,128)(2,1)S(1)}, bf16[16,64,128]{2,1,0:T(8,128)(2,1)S(1)}, u32[]{:S(2)}, u32[]{:S(2)}) %collective-permute-start.8) | collective-permute-done | bytes 262176 | tf_op jit(solution)/shard_map/ppermute | solution.py:304
  66.6 1.0 %shard_map.99 = (f32[9,128,128]{2,1,0:T(8,128)}, f32[3,128,128]{2,1,0:T(8,128)}, f32[3,128,128]{2,1,0:T(8,128)}) custom-call(bf16[16,64,128]{2,1,0:T(8,128)(2,1)S(1)} %all-to-all-done.2.mine_ref, bf16[16,64,128]{2,1,0:T(8,128)(2,1)S(1)} %collective-permute-done.8.other_ref), custom_call_target="tpu_custom_call" | custom-call | bytes 4000000 | tf_op jit(solution)/shard_map/pallas_call | solution.py:275
  (4 shorter events, 0.1 us)
Async XLA Ops:
  0.6 7.9 %copy-start.2 = (bf16[3,3,128,128]{3,2,1,0:T(8,128)(2,1)S(1)}, bf16[3,3,128,128]{3,2,1,0:T(8,128)(2,1)}, u32[]{:S(2)}) copy-start(bf16[3,3,128,128]{3,2,1,0:T(8,128)(2,1)} %w_ref.1) | copy-start | bytes 884740
  0.6 12.9 %collective-permute-start.2 = (bf16[8,128,128]{2,1,0:T(8,128)(2,1)}, bf16[8,128,128]{2,1,0:T(8,128)(2,1)S(1)}, u32[]{:S(2)}, u32[]{:S(2)}) collective-permute-start(bf16[8,128,128]{2,1,0:T(8,128)(2,1)} %bitcast.14), channel_id=1, source_target_pairs={{0,8},{8,0},{16,24},{24,16},{32,40},{40,32},{48,56},{56,48},{64,72... | collective-permute-start | bytes 786440 | tf_op jit(solution)/shard_map/ppermute | solution.py:304
  2.9 10.7 %collective-permute-start.3 = (bf16[8,128,128]{2,1,0:T(8,128)(2,1)}, bf16[8,128,128]{2,1,0:T(8,128)(2,1)S(1)}, u32[]{:S(2)}, u32[]{:S(2)}) collective-permute-start(bf16[8,128,128]{2,1,0:T(8,128)(2,1)} %bitcast.15), channel_id=1, source_target_pairs={{8,16},{24,32},{40,48},{56,64},{72,80},{88,96},{104,112},{16,8},{3... | collective-permute-start | bytes 786440 | tf_op jit(solution)/shard_map/ppermute | solution.py:310
  4.5 5.4 %collective-permute-start = (bf16[2,128,128]{2,1,0:T(8,128)(2,1)S(1)}, bf16[2,128,128]{2,1,0:T(8,128)(2,1)S(1)}, u32[]{:S(2)}, u32[]{:S(2)}) collective-permute-start(bf16[2,128,128]{2,1,0:T(8,128)(2,1)S(1)} %get-tuple-element.36), channel_id=1, source_target_pairs={{0,1},{1,0},{2,3},{3,2},{4,5},{5,4},{6,7},{7,6},{8,9},{9,8},{10,11... | collective-permute-start | bytes 196616 | tf_op jit(solution)/shard_map/ppermute | solution.py:304
  5.7 5.6 %collective-permute-start.1 = (bf16[2,128,128]{2,1,0:T(8,128)(2,1)S(1)}, bf16[2,128,128]{2,1,0:T(8,128)(2,1)S(1)}, u32[]{:S(2)}, u32[]{:S(2)}) collective-permute-start(bf16[2,128,128]{2,1,0:T(8,128)(2,1)S(1)} %get-tuple-element.39), channel_id=1, source_target_pairs={{1,2},{3,4},{5,6},{2,1},{4,3},{6,5},{9,10},{11,12},{13,14},{10,9},... | collective-permute-start | bytes 196616 | tf_op jit(solution)/shard_map/ppermute | solution.py:310
  8.5 1.0 %copy-start = (bf16[1,2,8,128,128]{4,3,2,1,0:T(8,128)(2,1)S(1)}, bf16[1,2,8,128,128]{4,3,2,1,0:T(8,128)(2,1)}, u32[]{:S(2)}) copy-start(bf16[1,2,8,128,128]{4,3,2,1,0:T(8,128)(2,1)} %param.5) | copy-start | bytes 1572868
  9.6 1.7 %copy-start.3 = (bf16[3,128,128]{2,1,0:T(8,128)(2,1)S(1)}, bf16[3,128,128]{2,1,0:T(8,128)(2,1)}, u32[]{:S(2)}) copy-start(bf16[3,128,128]{2,1,0:T(8,128)(2,1)} %wt_ref.5) | copy-start | bytes 294916
  9.6 1.7 %copy-start.4 = (bf16[3,128,128]{2,1,0:T(8,128)(2,1)S(1)}, bf16[3,128,128]{2,1,0:T(8,128)(2,1)}, u32[]{:S(2)}) copy-start(bf16[3,128,128]{2,1,0:T(8,128)(2,1)} %wd_ref.7) | copy-start | bytes 294916
  11.3 2.3 %copy-start.5 = (bf16[1,1,8,128,128]{4,3,2,1,0:T(8,128)(2,1)S(1)}, bf16[1,1,8,128,128]{4,3,2,1,0:T(8,128)(2,1)}, u32[]{:S(2)}) copy-start(bf16[1,1,8,128,128]{4,3,2,1,0:T(8,128)(2,1)} %param.9) | copy-start | bytes 786436
  16.6 3.1 %copy-start.6 = (bf16[2,8,128,128]{3,2,1,0:T(8,128)(2,1)}, bf16[2,8,128,128]{3,2,1,0:T(8,128)(2,1)S(1)}, u32[]{:S(2)}) copy-start(bf16[2,8,128,128]{3,2,1,0:T(8,128)(2,1)S(1)} %get-tuple-element.55.gpre_ref) | copy-start | bytes 1572868
  16.6 3.1 %collective-permute-start.4 = (bf16[19,64,128]{2,1,0:T(8,128)(2,1)S(1)}, bf16[19,64,128]{2,1,0:T(8,128)(2,1)S(1)}, u32[]{:S(2)}, u32[]{:S(2)}) collective-permute-start(bf16[19,64,128]{2,1,0:T(8,128)(2,1)S(1)} %get-tuple-element.45), channel_id=1, source_target_pairs={{0,1},{1,0},{2,3},{3,2},{4,5},{5,4},{6,7},{7,6},{8,9},{9,8},{10,11... | collective-permute-start | bytes 933896 | tf_op jit(solution)/shard_map/ppermute | solution.py:304
  34.1 15.7 %all-to-all-start.1 = ((bf16[8,64,128]{2,1,0:T(8,128)(2,1)}), bf16[8,64,128]{2,1,0:T(8,128)(2,1)S(1)}, u32[]{:S(2)}, u32[]{:S(2)}) async-start(bf16[8,64,128]{2,1,0:T(8,128)(2,1)} %broadcast_in_dim.9), calls=%async_computation.1 | async-start | bytes 262144 | tf_op jit(solution)/shard_map/all_to_all | solution.py:300
  43.3 6.5 %collective-permute-start.5 = (bf16[2,128,128]{2,1,0:T(8,128)(2,1)S(1)}, bf16[2,128,128]{2,1,0:T(8,128)(2,1)S(1)}, u32[]{:S(2)}, u32[]{:S(2)}) collective-permute-start(bf16[2,128,128]{2,1,0:T(8,128)(2,1)S(1)} %get-tuple-element.50), channel_id=1, source_target_pairs={{1,2},{3,4},{5,6},{2,1},{4,3},{6,5},{9,10},{11,12},{13,14},{10,9},... | collective-permute-start | bytes 196616 | tf_op jit(solution)/shard_map/ppermute | solution.py:310
  47.5 15.2 %collective-permute-start.6 = (bf16[8,128,128]{2,1,0:T(8,128)(2,1)S(1)}, bf16[8,128,128]{2,1,0:T(8,128)(2,1)S(1)}, u32[]{:S(2)}, u32[]{:S(2)}) collective-permute-start(bf16[8,128,128]{2,1,0:T(8,128)(2,1)S(1)} %get-tuple-element.53), channel_id=1, source_target_pairs={{0,8},{8,0},{16,24},{24,16},{32,40},{40,32},{48,56},{56,48},{64,72... | collective-permute-start | bytes 786440 | tf_op jit(solution)/shard_map/ppermute | solution.py:304
  48.1 14.7 %collective-permute-start.7 = (bf16[8,128,128]{2,1,0:T(8,128)(2,1)S(1)}, bf16[8,128,128]{2,1,0:T(8,128)(2,1)S(1)}, u32[]{:S(2)}, u32[]{:S(2)}) collective-permute-start(bf16[8,128,128]{2,1,0:T(8,128)(2,1)S(1)} %get-tuple-element.54), channel_id=1, source_target_pairs={{8,16},{24,32},{40,48},{56,64},{72,80},{88,96},{104,112},{16,8},{3... | collective-permute-start | bytes 786440 | tf_op jit(solution)/shard_map/ppermute | solution.py:310
  50.6 13.8 %all-to-all-start.2 = ((bf16[16,64,128]{2,1,0:T(8,128)(2,1)}), bf16[16,64,128]{2,1,0:T(8,128)(2,1)S(1)}, u32[]{:S(2)}, u32[]{:S(2)}) async-start(bf16[16,64,128]{2,1,0:T(8,128)(2,1)} %broadcast_in_dim.10), calls=%async_computation.2 | async-start | bytes 524288 | tf_op jit(solution)/shard_map/all_to_all | solution.py:300
  59.6 1.0 %copy-start.7 = (bf16[2,8,128,128]{3,2,1,0:T(8,128)(2,1)S(1)}, bf16[2,8,128,128]{3,2,1,0:T(8,128)(2,1)}, u32[]{:S(2)}) copy-start(bf16[2,8,128,128]{3,2,1,0:T(8,128)(2,1)} %copy-done.6) | copy-start | bytes 1572868
  60.7 2.1 %copy-start.1 = (bf16[1,2,8,128,128]{4,3,2,1,0:T(8,128)(2,1)S(1)}, bf16[1,2,8,128,128]{4,3,2,1,0:T(8,128)(2,1)}, u32[]{:S(2)}) copy-start(bf16[1,2,8,128,128]{4,3,2,1,0:T(8,128)(2,1)} %param.5) | copy-start | bytes 1572868
  64.4 2.3 %collective-permute-start.8 = (bf16[16,64,128]{2,1,0:T(8,128)(2,1)S(1)}, bf16[16,64,128]{2,1,0:T(8,128)(2,1)S(1)}, u32[]{:S(2)}, u32[]{:S(2)}) collective-permute-start(bf16[16,64,128]{2,1,0:T(8,128)(2,1)S(1)} %all-to-all-done.2.mine_ref), channel_id=1, source_target_pairs={{0,1},{1,0},{2,3},{3,2},{4,5},{5,4},{6,7},{7,6},{8,9},{9,8},{10,11... | collective-permute-start | bytes 786440 | tf_op jit(solution)/shard_map/ppermute | solution.py:304

commit v6 on v5

--- a/solution.py
+++ b/solution.py
@@ -71,7 +71,7 @@
     sort_sides(lax.axis_index("core") == 1, low_ref, high_ref, near_ref, far_ref)
 
 
-def prepare_kernel(x_hbm, w_hbm, x_ref, wide_ref, w_ref, sem):
+def prepare_kernel(x_hbm, w_hbm, x_ref, wide_ref, turn_ref, w_ref, sem):
     copies = [
         pltpu.make_async_copy(w_hbm, w_ref, sem.at[0]),
         pltpu.make_async_copy(x_hbm, x_ref, sem.at[1]),
@@ -86,17 +86,20 @@
                 start = ((dy + out) * 3 + dx) * C
                 wide_ref[start : start + C, out * C : (out + 1) * C] = w_ref[dy, dx]
     copies[1].wait()
+    for f in range(2):
+        turn_ref[f] = x_ref[f].reshape(1024, C).T
 
 
 def forward_kernel(
-    x_ref, near_ref, far_ref, wide_ref, wt_ref, wd_ref,
-    slope_ref, act_ref, xt_ref, at_ref, to_near_ref, to_far_ref, rows_ref,
+    x_ref, near_ref, far_ref, wide_ref, turn_ref, slope_ref, act_ref, xt_ref, at_ref, rows_ref
 ):
     sort_sides(lax.axis_index("core") == 1, near_ref, far_ref, rows_ref.at[:, 0], rows_ref.at[:, 9])
     rows_ref[:, 1:9] = x_ref[...]
     for f in range(2):
         x = rows_ref[f].reshape(1280, C)
-        xt_ref[f] = x.T
+        xt_ref[f, :, :128] = rows_ref[f, 0].T
+        xt_ref[f, :, 128:1152] = turn_ref[f]
+        xt_ref[f, :, 1152:] = rows_ref[f, 9].T
         pre = mm(row_pairs(jnp.concatenate(columns(x), axis=1)), wide_ref[...])
         sig = 1.0 / (1.0 + jnp.exp(-pre))
         act = (pre * sig).astype(BF16)
@@ -106,6 +109,9 @@
             act_ref[f, :, out] = act[:, part].reshape(4, 128, C)
             slope_ref[f, :, out] = slope[:, part].reshape(4, 128, C)
         at_ref[f] = act_ref[f].reshape(1024, C).T
+
+
+def ahead_kernel(x_ref, act_ref, wt_ref, wd_ref, to_near_ref, to_far_ref):
     zero = jnp.zeros((C, C), BF16)
     a0, a1 = act_ref[0].reshape(1024, C), act_ref[1].reshape(1024, C)
     w_time = jnp.concatenate(
@@ -295,8 +301,8 @@
         ref[:, 64:] = high[first : first + count]
 
 
-def exchange(x, axis, count):
-    groups = [list(range(count - 1, -1, -1))]
+def exchange(x, axis, order):
+    groups = [list(order)]
     return lax.all_to_all(x, axis, 0, 0, axis_index_groups=groups, tiled=True)
 
 
@@ -320,21 +326,20 @@
     to_near, to_far = call(pick_kernel, [edge, edge], (low, high), 0)
     x_near, x_far = swap(to_near, rows, 1), swap_far(to_far, rows)
     source, _ = lax.optimization_barrier((x, to_near))
-    here, wide = pl.pallas_call(
+    here, wide, turn = pl.pallas_call(
         prepare_kernel,
-        out_shape=[jax.ShapeDtypeStruct((2, 8, 128, C), BF16), jax.ShapeDtypeStruct((12 * C, 2 * C), BF16)],
+        out_shape=[jax.ShapeDtypeStruct((2, 8, 128, C), BF16), jax.ShapeDtypeStruct((12 * C, 2 * C), BF16), jax.ShapeDtypeStruct((2, C, 1024), BF16)],
         in_specs=[pl.BlockSpec(memory_space=pl.ANY)] * 2,
-        out_specs=[VMEM] * 2,
+        out_specs=[VMEM] * 3,
         scratch_shapes=[pltpu.VMEM((3, 3, C, C), BF16), pltpu.SemaphoreType.DMA((2,))],
         compiler_params=pltpu.CompilerParams(vmem_limit_bytes=24 * 1024 * 1024),
     )(source, w_spatial)
-    slope, act, xt, at, to_near, to_far = call(
+    slope, act, xt, at = call(
         forward_kernel,
-        [((2, 4, 2, 128, C), F32), ((2, 4, 2, 128, C), BF16), ((2, C, 1280), BF16), ((2, C, 1024), BF16), frame, frame],
-        (here, x_near, x_far, wide, w_temporal, w_down), 11,
+        [((2, 4, 2, 128, C), F32), ((2, 4, 2, 128, C), BF16), ((2, C, 1280), BF16), ((2, C, 1024), BF16)],
+        (here, x_near, x_far, wide, turn), 9,
         scratch=[rows_scratch],
     )
-    to_t_near, to_t_far = to_near, to_far
     gpre, to_far, send, keep = call(
         grads_kernel,
         [((2, 8, 128, C), BF16), edge, ((19, 64, C), BF16), ((15, 64, C), F32)],
@@ -343,17 +348,20 @@
     )
     near = swap(send, "core", 1)
     (half,) = call(merge_kernel, [((16, 64, C), BF16)], (keep, near), 0)
-    got = exchange(half, PLANE, 16)
+    _, recent = lax.optimization_barrier((send, act))
+    to_t_near, to_t_far = call(ahead_kernel, [frame, frame], (here, recent, w_temporal, w_down), 2)
+    half, to_t_near, to_t_far = lax.optimization_barrier((half, to_t_near, to_t_far))
+    got = exchange(half, PLANE, range(15, -1, -1))
     got, to_far, to_t_near, to_t_far = lax.optimization_barrier((got, to_far, to_t_near, to_t_far))
     total = jnp.sum(got.astype(F32), axis=0)
     t_near, t_far = swap(to_t_near, time, 1), swap_far(to_t_far, time)
     g_far = swap_far(to_far, rows)
     column = jnp.broadcast_to(total.astype(BF16), (8, 64, C))
-    column = exchange(column, "z", 8)
+    column = exchange(column, "z", [4, 3, 5, 2, 6, 1, 7, 0])
     column, g_far = lax.optimization_barrier((column, g_far))
     total = jnp.sum(column.astype(F32), axis=0)
     out = jnp.broadcast_to(total.astype(BF16), (16, 64, C))
-    out = exchange(out, PLANE, 16)
+    out = exchange(out, PLANE, range(15, -1, -1))
     (down,) = call(
         down_kernel, [frame], (x, act.reshape(2, 8, 128, C), t_near, t_far, w_temporal, w_down), 5,
         scratch=[frame_scratch, frame_scratch],

time: 68.2 us -> 67.6 us (level)
  starting transfers between devices: 33.6 us -> 32.6 us
    all_to_all x2, waiting for transfers between devices: 0.01 us -> 0.73 us  [exchange(): return lax.all_to_all(x, axis, 0, 0, axis_index_groups=groups, tiled=True)]
    ppermute x5, starting transfers between devices: 6.92 us -> 6.2 us  [swap(): lax.ppermute(x, axis, [(i, i ^ mask) for i in range(lax.axis_size(axis))])]
    pallas_call x7 -> x8, Pallas kernels: 9.51 us -> 9.81 us  [call(): pl.pallas_call(kernel, out_shape=[jax.ShapeDtypeStruct(s, d) for s, d in...]
  transfers between devices with their start and end apart: 11 -> 11, of which waited for: 5 -> 6; matrix products, arithmetic and copies ran while one was open for 2% -> 2% of each run, Pallas kernels for 8% -> 9%
where the time goes in v6:
time: 67.6 us; the launch traced here: 67 us
  starting transfers between devices  32.6 us (48%)
  blocking collectives  13.3 us (20%)
  Pallas kernels  10.2 us (15%)
  waiting for transfers between devices  5.62 us (8%)
  local copies, waits for them, and re-layouts  4.42 us (7%)
  between operations  0.78 us (1%)
    all_to_all x2, starting transfers between devices, exchange(): return lax.all_to_all(x, axis, 0, 0, axis_index_groups=groups, tiled=True)  18 us
    all_to_all x1, blocking collectives, exchange(): return lax.all_to_all(x, axis, 0, 0, axis_index_groups=groups, tiled=True)  13.3 us
    pallas_call x8, Pallas kernels, call(): pl.pallas_call(kernel, out_shape=[jax.ShapeDtypeStruct(s, d) for s, d in...  9.81 us
    ppermute x4, starting transfers between devices, swap_far(): return lax.ppermute(x, axis, pairs + [(b, a) for a, b in pairs])  8.4 us
    ppermute x5, starting transfers between devices, swap(): lax.ppermute(x, axis, [(i, i ^ mask) for i in range(lax.axis_size(axis))])  6.2 us
    ppermute x5, waiting for transfers between devices, swap(): lax.ppermute(x, axis, [(i, i ^ mask) for i in range(lax.axis_size(axis))])  2.64 us
    ppermute x4, waiting for transfers between devices, swap_far(): return lax.ppermute(x, axis, pairs + [(b, a) for a, b in pairs])  2.24 us
    unnamed x16, local copies, waits for them, and re-layouts  2.1 us
  transfers between devices with their start and end apart: 11, of which 6 were waited for; matrix products, arithmetic and copies ran while one was open for 2% of the time, Pallas kernels for 9%

profile of v6, /device:TPU:1, one launch (start us, length us, event | category | flops | bytes accessed | tf_op | source)
XLA Modules:
  0.0 67.0 jit_solution(2277822688847174355)
XLA Ops:
  0.6 0.0 copy-start.4
  0.6 2.2 %collective-permute-start.2 = (bf16[8,128,128]{2,1,0:T(8,128)(2,1)}, bf16[8,128,128]{2,1,0:T(8,128)(2,1)S(1)}, u32[]{:S(2)}, u32[]{:S(2)}) collective-permute-start(bf16[8,128,128]{2,1,0:T(8,128)(2,1)} %bitcast.14), channel_id=1, source_target_pairs={{0,8},{8,0},{16,24},{24,16},{32,40},{40,32},{48,56},{56,48},{64,72... | collective-permute-start | bytes 786440 | tf_op jit(solution)/shard_map/ppermute | solution.py:310
  2.9 0.7 collective-permute-start.3
  3.5 0.9 %slice_bitcast_fusion = (bf16[2,128,128]{2,1,0:T(8,128)(2,1)S(1)}, bf16[2,128,128]{2,1,0:T(8,128)(2,1)S(1)}) fusion(bf16[2,8,128,128]{3,2,1,0:T(8,128)(2,1)} %bitcast.10), kind=kLoop, calls=%fused_computation | loop fusion | bytes 262144 | tf_op jit(solution)/shard_map/squeeze | solution.py:325
  4.5 1.2 %collective-permute-start = (bf16[2,128,128]{2,1,0:T(8,128)(2,1)S(1)}, bf16[2,128,128]{2,1,0:T(8,128)(2,1)S(1)}, u32[]{:S(2)}, u32[]{:S(2)}) collective-permute-start(bf16[2,128,128]{2,1,0:T(8,128)(2,1)S(1)} %get-tuple-element.41), channel_id=1, source_target_pairs={{0,1},{1,0},{2,3},{3,2},{4,5},{5,4},{6,7},{7,6},{8,9},{9,8},{10,11... | collective-permute-start | bytes 196616 | tf_op jit(solution)/shard_map/ppermute | solution.py:310
  5.7 2.8 %collective-permute-start.1 = (bf16[2,128,128]{2,1,0:T(8,128)(2,1)S(1)}, bf16[2,128,128]{2,1,0:T(8,128)(2,1)S(1)}, u32[]{:S(2)}, u32[]{:S(2)}) collective-permute-start(bf16[2,128,128]{2,1,0:T(8,128)(2,1)S(1)} %get-tuple-element.44), channel_id=1, source_target_pairs={{1,2},{3,4},{5,6},{2,1},{4,3},{6,5},{9,10},{11,12},{13,14},{10,9},... | collective-permute-start | bytes 196616 | tf_op jit(solution)/shard_map/ppermute | solution.py:316
  8.5 0.0 copy-done.4
  8.5 0.0 copy-start
  8.5 1.0 %copy-done = bf16[1,2,8,128,128]{4,3,2,1,0:T(8,128)(2,1)S(1)} copy-done((bf16[1,2,8,128,128]{4,3,2,1,0:T(8,128)(2,1)S(1)}, bf16[1,2,8,128,128]{4,3,2,1,0:T(8,128)(2,1)}, u32[]{:S(2)}) %copy-start) | copy-done | bytes 524312
  9.6 0.4 shard_map.93
  10.0 0.0 collective-permute-done.near_ref
  10.0 1.2 %collective-permute-done.1.far_ref = bf16[2,128,128]{2,1,0:T(8,128)(2,1)S(1)} collective-permute-done((bf16[2,128,128]{2,1,0:T(8,128)(2,1)S(1)}, bf16[2,128,128]{2,1,0:T(8,128)(2,1)S(1)}, u32[]{:S(2)}, u32[]{:S(2)}) %collective-permute-start.1) | collective-permute-done | bytes 65568 | tf_op jit(solution)/shard_map/ppermute | solution.py:316
  11.3 0.0 copy-start.2
  11.3 0.0 copy-start.3
  11.3 0.0 copy-start.5
  11.3 1.4 %shard_map.94 = (f32[2,4,2,128,128]{4,3,2,1,0:T(8,128)S(1)}, bf16[2,4,2,128,128]{4,3,2,1,0:T(8,128)(2,1)S(1)}, bf16[2,128,1280]{2,1,0:T(8,128)(2,1)S(1)}, bf16[2,128,1024]{2,1,0:T(8,128)(2,1)S(1)}) custom-call(bf16[2,8,128,128]{3,2,1,0:T(8,128)(2,1)S(1)} %get-tuple-element.43.x_ref, bf16[2,128,128]{2,1,0:T(8,128)(2,1)S(1)} %collective-permute-done.near_ref, ...), custom_call_target="tpu_custom_call" | custom-call | flops 603979776 | bytes 4000000 | tf_op jit(solution)/shard_map/pallas_call | solution.py:281
  12.7 0.9 %collective-permute-done.2.near_ref = bf16[8,128,128]{2,1,0:T(8,128)(2,1)S(1)} collective-permute-done((bf16[8,128,128]{2,1,0:T(8,128)(2,1)}, bf16[8,128,128]{2,1,0:T(8,128)(2,1)S(1)}, u32[]{:S(2)}, u32[]{:S(2)}) %collective-permute-start.2) | collective-permute-done | bytes 262176 | tf_op jit(solution)/shard_map/ppermute | solution.py:310
  13.6 0.0 collective-permute-done.3.far_ref
  13.6 0.0 copy-done.2
  13.6 0.0 copy-done.3
  13.6 0.0 copy-done.5
  13.6 3.0 %shard_map.95 = (bf16[2,8,128,128]{3,2,1,0:T(8,128)(2,1)S(1)}, bf16[2,128,128]{2,1,0:T(8,128)(2,1)S(1)}, bf16[19,64,128]{2,1,0:T(8,128)(2,1)S(1)}, f32[15,64,128]{2,1,0:T(8,128)S(1)}) custom-call(f32[2,4,2,128,128]{4,3,2,1,0:T(8,128)S(1)} %get-tuple-element.47.slope_ref, bf16[2,128,1280]{2,1,0:T(8,128)(2,1)S(1)} %get-tuple-element.48.xt_ref, ...), custom_call_target="tpu_custom_call" | custom-call | flops 1409286144 | bytes 4000000 | tf_op jit(solution)/shard_map/pallas_call | solution.py:281
  16.6 0.0 copy-start.6
  16.6 1.8 %collective-permute-start.4 = (bf16[19,64,128]{2,1,0:T(8,128)(2,1)S(1)}, bf16[19,64,128]{2,1,0:T(8,128)(2,1)S(1)}, u32[]{:S(2)}, u32[]{:S(2)}) collective-permute-start(bf16[19,64,128]{2,1,0:T(8,128)(2,1)S(1)} %get-tuple-element.51), channel_id=1, source_target_pairs={{0,1},{1,0},{2,3},{3,2},{4,5},{5,4},{6,7},{7,6},{8,9},{9,8},{10,11... | collective-permute-start | bytes 933896 | tf_op jit(solution)/shard_map/ppermute | solution.py:310
  18.4 0.6 shard_map.97
  19.0 0.0 copy-done.6
  19.0 0.6 collective-permute-done.4.got_ref.sent_ref
  19.7 13.3 %all_to_all.15 = bf16[16,64,128]{2,1,0:T(8,128)(2,1)S(1)} all-to-all(bf16[16,64,128]{2,1,0:T(8,128)(2,1)S(1)} %shard_map.96), channel_id=1, replica_groups={{142,140,138,136,134,132,130,128,14,12,10,8,6,4,2,0},{143,141,139,137,1..., dimensions={0} | all-to-all | bytes 524288 | tf_op jit(solution)/shard_map/all_to_all | solution.py:306
  33.0 0.7 %broadcast_in_dim.9 = bf16[8,64,128]{2,1,0:T(8,128)(2,1)} broadcast(bf16[64,128]{1,0:T(8,128)(2,1)S(1)} %reduce_sum.24), dimensions={1,2} | broadcast | bytes 147456 | tf_op jit(solution)/shard_map/broadcast_in_dim | solution.py:359
  33.7 9.9 %all-to-all-start.1 = ((bf16[8,64,128]{2,1,0:T(8,128)(2,1)}), bf16[8,64,128]{2,1,0:T(8,128)(2,1)S(1)}, u32[]{:S(2)}, u32[]{:S(2)}) async-start(bf16[8,64,128]{2,1,0:T(8,128)(2,1)} %broadcast_in_dim.9), calls=%async_computation.1 | async-start | bytes 262144 | tf_op jit(solution)/shard_map/all_to_all | solution.py:306
  43.6 4.2 %collective-permute-start.5 = (bf16[2,128,128]{2,1,0:T(8,128)(2,1)S(1)}, bf16[2,128,128]{2,1,0:T(8,128)(2,1)S(1)}, u32[]{:S(2)}, u32[]{:S(2)}) collective-permute-start(bf16[2,128,128]{2,1,0:T(8,128)(2,1)S(1)} %get-tuple-element.61), channel_id=1, source_target_pairs={{1,2},{3,4},{5,6},{2,1},{4,3},{6,5},{9,10},{11,12},{13,14},{10,9},... | collective-permute-start | bytes 196616 | tf_op jit(solution)/shard_map/ppermute | solution.py:316
  47.8 0.5 collective-permute-start.6
  48.4 0.7 collective-permute-start.7
  49.1 1.0 %collective-permute-done.5.g_far_ref = bf16[2,128,128]{2,1,0:T(8,128)(2,1)S(1)} collective-permute-done((bf16[2,128,128]{2,1,0:T(8,128)(2,1)S(1)}, bf16[2,128,128]{2,1,0:T(8,128)(2,1)S(1)}, u32[]{:S(2)}, u32[]{:S(2)}) %collective-permute-start.5) | collective-permute-done | bytes 65568 | tf_op jit(solution)/shard_map/ppermute | solution.py:316
  50.1 0.0 all-to-all-done.1
  50.1 0.8 %broadcast_in_dim.10 = bf16[16,64,128]{2,1,0:T(8,128)(2,1)} broadcast(bf16[64,128]{1,0:T(8,128)(2,1)S(1)} %reduce_sum.25), dimensions={1,2} | broadcast | bytes 278528 | tf_op jit(solution)/shard_map/broadcast_in_dim | solution.py:363
  50.8 8.1 %all-to-all-start.2 = ((bf16[16,64,128]{2,1,0:T(8,128)(2,1)}), bf16[16,64,128]{2,1,0:T(8,128)(2,1)S(1)}, u32[]{:S(2)}, u32[]{:S(2)}) async-start(bf16[16,64,128]{2,1,0:T(8,128)(2,1)} %broadcast_in_dim.10), calls=%async_computation.2 | async-start | bytes 524288 | tf_op jit(solution)/shard_map/all_to_all | solution.py:306
  59.0 0.0 copy-start.7
  59.0 1.0 %copy-done.7 = bf16[2,8,128,128]{3,2,1,0:T(8,128)(2,1)S(1)} copy-done((bf16[2,8,128,128]{3,2,1,0:T(8,128)(2,1)S(1)}, bf16[2,8,128,128]{3,2,1,0:T(8,128)(2,1)}, u32[]{:S(2)}) %copy-start.7) | copy-done | bytes 524312
  60.0 0.0 copy-start.1
  60.0 2.1 %shard_map.99 = bf16[2,4,2,128,128]{4,3,2,1,0:T(8,128)(2,1)} custom-call(bf16[2,8,128,128]{3,2,1,0:T(8,128)(2,1)S(1)} %copy-done.7, bf16[19,64,128]{2,1,0:T(8,128)(2,1)S(1)} %collective-permute-done.4.got_ref.sent_ref, bf16[2,128,128]{2,1,0:T(8,128)(2,1)S(1)} %collective-permute-done.5.g_far_ref, bf16[8,128,128]{2,1,0:T(8,128)(2,1)S(1)} %bitcast.17, ...), custom_call_target="tpu_custom_call" | custom-call | flops 738197504 | bytes 4000000 | tf_op jit(solution)/shard_map/pallas_call | solution.py:281
  62.1 0.0 collective-permute-done.6.near_ref
  62.1 0.0 collective-permute-done.7.far_ref
  62.1 0.0 copy-done.1
  62.1 1.6 %shard_map.98 = bf16[8,128,128]{2,1,0:T(8,128)(2,1)} custom-call(bf16[2,8,128,128]{3,2,1,0:T(8,128)(2,1)S(1)} %bitcast.12, bf16[2,8,128,128]{3,2,1,0:T(8,128)(2,1)S(1)} %bitcast.13, bf16[8,128,128]{2,1,0:T(8,128)(2,1)S(1)} %collective-permute-done.6.near_ref, bf16[8,128,128]{2,1,0:T(8,128)(2,1)S(1)} %collective-permute-done.7.far_ref, ...), custom_call_target="tpu_custom_call" | custom-call | flops 335544320 | bytes 4000000 | tf_op jit(solution)/shard_map/pallas_call | solution.py:281
  63.7 0.7 %all-to-all-done.2.mine_ref = bf16[16,64,128]{2,1,0:T(8,128)(2,1)S(1)} async-done(((bf16[16,64,128]{2,1,0:T(8,128)(2,1)}), bf16[16,64,128]{2,1,0:T(8,128)(2,1)S(1)}, u32[]{:S(2)}, u32[]{:S(2)}) %all-to-all-start.2) | async-done | bytes 262176 | tf_op jit(solution)/shard_map/all_to_all | solution.py:306
  64.5 0.4 collective-permute-start.8
  64.8 1.2 %collective-permute-done.8.other_ref = bf16[16,64,128]{2,1,0:T(8,128)(2,1)S(1)} collective-permute-done((bf16[16,64,128]{2,1,0:T(8,128)(2,1)S(1)}, bf16[16,64,128]{2,1,0:T(8,128)(2,1)S(1)}, u32[]{:S(2)}, u32[]{:S(2)}) %collective-permute-start.8) | collective-permute-done | bytes 262176 | tf_op jit(solution)/shard_map/ppermute | solution.py:310
  66.0 1.0 %shard_map.100 = (f32[9,128,128]{2,1,0:T(8,128)}, f32[3,128,128]{2,1,0:T(8,128)}, f32[3,128,128]{2,1,0:T(8,128)}) custom-call(bf16[16,64,128]{2,1,0:T(8,128)(2,1)S(1)} %all-to-all-done.2.mine_ref, bf16[16,64,128]{2,1,0:T(8,128)(2,1)S(1)} %collective-permute-done.8.other_ref), custom_call_target="tpu_custom_call" | custom-call | bytes 4000000 | tf_op jit(solution)/shard_map/pallas_call | solution.py:281
  (4 shorter events, 0.1 us)
Async XLA Ops:
  0.6 7.9 %copy-start.4 = (bf16[3,3,128,128]{3,2,1,0:T(8,128)(2,1)S(1)}, bf16[3,3,128,128]{3,2,1,0:T(8,128)(2,1)}, u32[]{:S(2)}) copy-start(bf16[3,3,128,128]{3,2,1,0:T(8,128)(2,1)} %w_ref.1) | copy-start | bytes 884740
  0.6 12.9 %collective-permute-start.2 = (bf16[8,128,128]{2,1,0:T(8,128)(2,1)}, bf16[8,128,128]{2,1,0:T(8,128)(2,1)S(1)}, u32[]{:S(2)}, u32[]{:S(2)}) collective-permute-start(bf16[8,128,128]{2,1,0:T(8,128)(2,1)} %bitcast.14), channel_id=1, source_target_pairs={{0,8},{8,0},{16,24},{24,16},{32,40},{40,32},{48,56},{56,48},{64,72... | collective-permute-start | bytes 786440 | tf_op jit(solution)/shard_map/ppermute | solution.py:310
  2.9 10.7 %collective-permute-start.3 = (bf16[8,128,128]{2,1,0:T(8,128)(2,1)}, bf16[8,128,128]{2,1,0:T(8,128)(2,1)S(1)}, u32[]{:S(2)}, u32[]{:S(2)}) collective-permute-start(bf16[8,128,128]{2,1,0:T(8,128)(2,1)} %bitcast.15), channel_id=1, source_target_pairs={{8,16},{24,32},{40,48},{56,64},{72,80},{88,96},{104,112},{16,8},{3... | collective-permute-start | bytes 786440 | tf_op jit(solution)/shard_map/ppermute | solution.py:316
  4.5 5.6 %collective-permute-start = (bf16[2,128,128]{2,1,0:T(8,128)(2,1)S(1)}, bf16[2,128,128]{2,1,0:T(8,128)(2,1)S(1)}, u32[]{:S(2)}, u32[]{:S(2)}) collective-permute-start(bf16[2,128,128]{2,1,0:T(8,128)(2,1)S(1)} %get-tuple-element.41), channel_id=1, source_target_pairs={{0,1},{1,0},{2,3},{3,2},{4,5},{5,4},{6,7},{7,6},{8,9},{9,8},{10,11... | collective-permute-start | bytes 196616 | tf_op jit(solution)/shard_map/ppermute | solution.py:310
  5.7 5.6 %collective-permute-start.1 = (bf16[2,128,128]{2,1,0:T(8,128)(2,1)S(1)}, bf16[2,128,128]{2,1,0:T(8,128)(2,1)S(1)}, u32[]{:S(2)}, u32[]{:S(2)}) collective-permute-start(bf16[2,128,128]{2,1,0:T(8,128)(2,1)S(1)} %get-tuple-element.44), channel_id=1, source_target_pairs={{1,2},{3,4},{5,6},{2,1},{4,3},{6,5},{9,10},{11,12},{13,14},{10,9},... | collective-permute-start | bytes 196616 | tf_op jit(solution)/shard_map/ppermute | solution.py:316
  8.5 1.0 %copy-start = (bf16[1,2,8,128,128]{4,3,2,1,0:T(8,128)(2,1)S(1)}, bf16[1,2,8,128,128]{4,3,2,1,0:T(8,128)(2,1)}, u32[]{:S(2)}) copy-start(bf16[1,2,8,128,128]{4,3,2,1,0:T(8,128)(2,1)} %param.5) | copy-start | bytes 1572868
  11.3 2.3 %copy-start.2 = (bf16[3,128,128]{2,1,0:T(8,128)(2,1)S(1)}, bf16[3,128,128]{2,1,0:T(8,128)(2,1)}, u32[]{:S(2)}) copy-start(bf16[3,128,128]{2,1,0:T(8,128)(2,1)} %wt_ref.5) | copy-start | bytes 294916
  11.3 2.3 %copy-start.3 = (bf16[3,128,128]{2,1,0:T(8,128)(2,1)S(1)}, bf16[3,128,128]{2,1,0:T(8,128)(2,1)}, u32[]{:S(2)}) copy-start(bf16[3,128,128]{2,1,0:T(8,128)(2,1)} %wd_ref.7) | copy-start | bytes 294916
  11.3 2.3 %copy-start.5 = (bf16[1,1,8,128,128]{4,3,2,1,0:T(8,128)(2,1)S(1)}, bf16[1,1,8,128,128]{4,3,2,1,0:T(8,128)(2,1)}, u32[]{:S(2)}) copy-start(bf16[1,1,8,128,128]{4,3,2,1,0:T(8,128)(2,1)} %param.9) | copy-start | bytes 786436
  16.6 2.4 %copy-start.6 = (bf16[2,8,128,128]{3,2,1,0:T(8,128)(2,1)}, bf16[2,8,128,128]{3,2,1,0:T(8,128)(2,1)S(1)}, u32[]{:S(2)}) copy-start(bf16[2,8,128,128]{3,2,1,0:T(8,128)(2,1)S(1)} %get-tuple-element.65.gpre_ref) | copy-start | bytes 1572868
  16.6 3.1 %collective-permute-start.4 = (bf16[19,64,128]{2,1,0:T(8,128)(2,1)S(1)}, bf16[19,64,128]{2,1,0:T(8,128)(2,1)S(1)}, u32[]{:S(2)}, u32[]{:S(2)}) collective-permute-start(bf16[19,64,128]{2,1,0:T(8,128)(2,1)S(1)} %get-tuple-element.51), channel_id=1, source_target_pairs={{0,1},{1,0},{2,3},{3,2},{4,5},{5,4},{6,7},{7,6},{8,9},{9,8},{10,11... | collective-permute-start | bytes 933896 | tf_op jit(solution)/shard_map/ppermute | solution.py:310
  33.7 16.4 %all-to-all-start.1 = ((bf16[8,64,128]{2,1,0:T(8,128)(2,1)}), bf16[8,64,128]{2,1,0:T(8,128)(2,1)S(1)}, u32[]{:S(2)}, u32[]{:S(2)}) async-start(bf16[8,64,128]{2,1,0:T(8,128)(2,1)} %broadcast_in_dim.9), calls=%async_computation.1 | async-start | bytes 262144 | tf_op jit(solution)/shard_map/all_to_all | solution.py:306
  43.6 6.5 %collective-permute-start.5 = (bf16[2,128,128]{2,1,0:T(8,128)(2,1)S(1)}, bf16[2,128,128]{2,1,0:T(8,128)(2,1)S(1)}, u32[]{:S(2)}, u32[]{:S(2)}) collective-permute-start(bf16[2,128,128]{2,1,0:T(8,128)(2,1)S(1)} %get-tuple-element.61), channel_id=1, source_target_pairs={{1,2},{3,4},{5,6},{2,1},{4,3},{6,5},{9,10},{11,12},{13,14},{10,9},... | collective-permute-start | bytes 196616 | tf_op jit(solution)/shard_map/ppermute | solution.py:316
  47.8 14.3 %collective-permute-start.6 = (bf16[8,128,128]{2,1,0:T(8,128)(2,1)S(1)}, bf16[8,128,128]{2,1,0:T(8,128)(2,1)S(1)}, u32[]{:S(2)}, u32[]{:S(2)}) collective-permute-start(bf16[8,128,128]{2,1,0:T(8,128)(2,1)S(1)} %get-tuple-element.63), channel_id=1, source_target_pairs={{0,8},{8,0},{16,24},{24,16},{32,40},{40,32},{48,56},{56,48},{64,72... | collective-permute-start | bytes 786440 | tf_op jit(solution)/shard_map/ppermute | solution.py:310
  48.4 13.8 %collective-permute-start.7 = (bf16[8,128,128]{2,1,0:T(8,128)(2,1)S(1)}, bf16[8,128,128]{2,1,0:T(8,128)(2,1)S(1)}, u32[]{:S(2)}, u32[]{:S(2)}) collective-permute-start(bf16[8,128,128]{2,1,0:T(8,128)(2,1)S(1)} %get-tuple-element.64), channel_id=1, source_target_pairs={{8,16},{24,32},{40,48},{56,64},{72,80},{88,96},{104,112},{16,8},{3... | collective-permute-start | bytes 786440 | tf_op jit(solution)/shard_map/ppermute | solution.py:316
  50.8 13.6 %all-to-all-start.2 = ((bf16[16,64,128]{2,1,0:T(8,128)(2,1)}), bf16[16,64,128]{2,1,0:T(8,128)(2,1)S(1)}, u32[]{:S(2)}, u32[]{:S(2)}) async-start(bf16[16,64,128]{2,1,0:T(8,128)(2,1)} %broadcast_in_dim.10), calls=%async_computation.2 | async-start | bytes 524288 | tf_op jit(solution)/shard_map/all_to_all | solution.py:306
  59.0 1.0 %copy-start.7 = (bf16[2,8,128,128]{3,2,1,0:T(8,128)(2,1)S(1)}, bf16[2,8,128,128]{3,2,1,0:T(8,128)(2,1)}, u32[]{:S(2)}) copy-start(bf16[2,8,128,128]{3,2,1,0:T(8,128)(2,1)} %copy-done.6) | copy-start | bytes 1572868
  60.0 2.1 %copy-start.1 = (bf16[1,2,8,128,128]{4,3,2,1,0:T(8,128)(2,1)S(1)}, bf16[1,2,8,128,128]{4,3,2,1,0:T(8,128)(2,1)}, u32[]{:S(2)}) copy-start(bf16[1,2,8,128,128]{4,3,2,1,0:T(8,128)(2,1)} %param.5) | copy-start | bytes 1572868
  64.5 1.6 %collective-permute-start.8 = (bf16[16,64,128]{2,1,0:T(8,128)(2,1)S(1)}, bf16[16,64,128]{2,1,0:T(8,128)(2,1)S(1)}, u32[]{:S(2)}, u32[]{:S(2)}) collective-permute-start(bf16[16,64,128]{2,1,0:T(8,128)(2,1)S(1)} %all-to-all-done.2.mine_ref), channel_id=1, source_target_pairs={{0,1},{1,0},{2,3},{3,2},{4,5},{5,4},{6,7},{7,6},{8,9},{9,8},{10,11... | collective-permute-start | bytes 786440 | tf_op jit(solution)/shard_map/ppermute | solution.py:310

commit v7 on v6

--- a/solution.py
+++ b/solution.py
@@ -291,14 +291,29 @@
     )(*args)
 
 
-def gather_kernel(mine_ref, other_ref, spatial_ref, time_ref, down_ref):
-    mine = lax.axis_index("core") == 0
-    low = jnp.where(mine, mine_ref[...], other_ref[...]).astype(F32)
-    high = jnp.where(mine, other_ref[...], mine_ref[...]).astype(F32)
-    for first, ref in ((0, spatial_ref), (9, time_ref), (12, down_ref)):
-        count = ref.shape[0]
-        ref[:, :64] = low[first : first + count]
-        ref[:, 64:] = high[first : first + count]
+def write_half(side, half_ref, outs, wide_ref, sem):
+    wide_ref[...] = half_ref[:15].astype(F32)
+    rows = pl.ds(pl.multiple_of(side * 64, 64), 64)
+    copies = []
+    for i, (first, out) in enumerate(zip((0, 9, 12), outs)):
+        count = out.shape[0]
+        copies.append(
+            pltpu.make_async_copy(wide_ref.at[first : first + count], out.at[:, rows], sem.at[i])
+        )
+    for copy in copies:
+        copy.start()
+    for copy in copies:
+        copy.wait()
+
+
+def own_half_kernel(half_ref, spatial_hbm, time_hbm, down_hbm, wide_ref, sem):
+    outs = (spatial_hbm, time_hbm, down_hbm)
+    write_half(lax.axis_index("core"), half_ref, outs, wide_ref, sem)
+
+
+def other_half_kernel(half_ref, a, b, c, spatial_hbm, time_hbm, down_hbm, wide_ref, sem):
+    outs = (spatial_hbm, time_hbm, down_hbm)
+    write_half(1 - lax.axis_index("core"), half_ref, outs, wide_ref, sem)
 
 
 def exchange(x, axis, order):
@@ -357,7 +372,7 @@
     t_near, t_far = swap(to_t_near, time, 1), swap_far(to_t_far, time)
     g_far = swap_far(to_far, rows)
     column = jnp.broadcast_to(total.astype(BF16), (8, 64, C))
-    column = exchange(column, "z", [4, 3, 5, 2, 6, 1, 7, 0])
+    column = exchange(column, "z", [4, 3, 5, 2, 6, 1, 0, 7])
     column, g_far = lax.optimization_barrier((column, g_far))
     total = jnp.sum(column.astype(F32), axis=0)
     out = jnp.broadcast_to(total.astype(BF16), (16, 64, C))
@@ -372,9 +387,19 @@
         scratch=[pltpu.VMEM((2 * C, 12 * C), BF16), rows_scratch, frame_scratch, frame_scratch],
     )
     out, down, grad_features = lax.optimization_barrier((out, down, grad_features))
-    grads = call(
-        gather_kernel, [((n, C, C), F32) for n in (9, 3, 3)], (out, swap(out, "core", 1)), 0,
-    )
+    anywhere = pl.BlockSpec(memory_space=pl.ANY)
+    shared = dict(
+        out_shape=[jax.ShapeDtypeStruct((n, C, C), F32) for n in (9, 3, 3)],
+        out_specs=[anywhere] * 3,
+        scratch_shapes=[pltpu.VMEM((15, 64, C), F32), pltpu.SemaphoreType.DMA((3,))],
+        compiler_params=pltpu.CompilerParams(vmem_limit_bytes=24 * 1024 * 1024),
+    )
+    other = swap(out, "core", 1)
+    grads = pl.pallas_call(own_half_kernel, in_specs=[VMEM], **shared)(out)
+    grads = pl.pallas_call(
+        other_half_kernel, in_specs=[VMEM] + [anywhere] * 3,
+        input_output_aliases={1: 0, 2: 1, 3: 2}, **shared,
+    )(other, *grads)
     return (
         down[None, None],
         grad_features.reshape(1, 2, 8, 128, C),

time: 67.6 us -> 67.4 us (level)
  waiting for transfers between devices: 5.62 us -> 4.77 us
  Pallas kernels: 10.2 us -> 10.9 us
    pallas_call x0 -> x2, Pallas kernels: none -> 1.65 us  [the longest x1 0.83 us: per_device(): pl.pallas_call(other_half_kernel, in_specs=[VMEM] + [anywhere] * 3, input...]
    pallas_call x8 -> x7, Pallas kernels: 9.81 us -> 8.8 us  [call(): pl.pallas_call(kernel, out_shape=[jax.ShapeDtypeStruct(s, d) for s, d in...]
    ppermute x5, waiting for transfers between devices: 2.64 us -> 1.81 us  [swap(): lax.ppermute(x, axis, [(i, i ^ mask) for i in range(lax.axis_size(axis))])]
  transfers between devices with their start and end apart: 11 -> 11, of which waited for: 6 -> 6; matrix products, arithmetic and copies ran while one was open for 2% -> 2% of each run, Pallas kernels for 9% -> 10%
where the time goes in v7:
time: 67.4 us; the launch traced here: 66.8 us
  starting transfers between devices  32.6 us (48%)
  blocking collectives  13.3 us (20%)
  Pallas kernels  10.9 us (16%)
  waiting for transfers between devices  4.77 us (7%)
  local copies, waits for them, and re-layouts  4.42 us (7%)
  between operations  0.79 us (1%)
    all_to_all x2, starting transfers between devices, exchange(): return lax.all_to_all(x, axis, 0, 0, axis_index_groups=groups, tiled=True)  18 us
    all_to_all x1, blocking collectives, exchange(): return lax.all_to_all(x, axis, 0, 0, axis_index_groups=groups, tiled=True)  13.3 us
    pallas_call x7, Pallas kernels, call(): pl.pallas_call(kernel, out_shape=[jax.ShapeDtypeStruct(s, d) for s, d in...  8.8 us
    ppermute x4, starting transfers between devices, swap_far(): return lax.ppermute(x, axis, pairs + [(b, a) for a, b in pairs])  8.4 us
    ppermute x5, starting transfers between devices, swap(): lax.ppermute(x, axis, [(i, i ^ mask) for i in range(lax.axis_size(axis))])  6.22 us
    ppermute x4, waiting for transfers between devices, swap_far(): return lax.ppermute(x, axis, pairs + [(b, a) for a, b in pairs])  2.24 us
    unnamed x16, local copies, waits for them, and re-layouts  2.1 us
    ppermute x5, waiting for transfers between devices, swap(): lax.ppermute(x, axis, [(i, i ^ mask) for i in range(lax.axis_size(axis))])  1.81 us
  transfers between devices with their start and end apart: 11, of which 6 were waited for; matrix products, arithmetic and copies ran while one was open for 2% of the time, Pallas kernels for 10%

profile of v7, /device:TPU:1, one launch (start us, length us, event | category | flops | bytes accessed | tf_op | source)
XLA Modules:
  0.0 66.8 jit_solution(234659930492534590)
XLA Ops:
  0.6 0.0 copy-start.4
  0.6 2.2 %collective-permute-start.2 = (bf16[8,128,128]{2,1,0:T(8,128)(2,1)}, bf16[8,128,128]{2,1,0:T(8,128)(2,1)S(1)}, u32[]{:S(2)}, u32[]{:S(2)}) collective-permute-start(bf16[8,128,128]{2,1,0:T(8,128)(2,1)} %bitcast.14), channel_id=1, source_target_pairs={{0,8},{8,0},{16,24},{24,16},{32,40},{40,32},{48,56},{56,48},{64,72... | collective-permute-start | bytes 786440 | tf_op jit(solution)/shard_map/ppermute | solution.py:325
  2.9 0.7 collective-permute-start.3
  3.5 0.9 %slice_bitcast_fusion = (bf16[2,128,128]{2,1,0:T(8,128)(2,1)S(1)}, bf16[2,128,128]{2,1,0:T(8,128)(2,1)S(1)}) fusion(bf16[2,8,128,128]{3,2,1,0:T(8,128)(2,1)} %bitcast.10), kind=kLoop, calls=%fused_computation | loop fusion | bytes 262144 | tf_op jit(solution)/shard_map/squeeze | solution.py:340
  4.5 1.2 %collective-permute-start = (bf16[2,128,128]{2,1,0:T(8,128)(2,1)S(1)}, bf16[2,128,128]{2,1,0:T(8,128)(2,1)S(1)}, u32[]{:S(2)}, u32[]{:S(2)}) collective-permute-start(bf16[2,128,128]{2,1,0:T(8,128)(2,1)S(1)} %get-tuple-element.44), channel_id=1, source_target_pairs={{0,1},{1,0},{2,3},{3,2},{4,5},{5,4},{6,7},{7,6},{8,9},{9,8},{10,11... | collective-permute-start | bytes 196616 | tf_op jit(solution)/shard_map/ppermute | solution.py:325
  5.7 2.8 %collective-permute-start.1 = (bf16[2,128,128]{2,1,0:T(8,128)(2,1)S(1)}, bf16[2,128,128]{2,1,0:T(8,128)(2,1)S(1)}, u32[]{:S(2)}, u32[]{:S(2)}) collective-permute-start(bf16[2,128,128]{2,1,0:T(8,128)(2,1)S(1)} %get-tuple-element.47), channel_id=1, source_target_pairs={{1,2},{3,4},{5,6},{2,1},{4,3},{6,5},{9,10},{11,12},{13,14},{10,9},... | collective-permute-start | bytes 196616 | tf_op jit(solution)/shard_map/ppermute | solution.py:331
  8.5 0.0 copy-done.4
  8.5 0.0 copy-start
  8.5 1.0 %copy-done = bf16[1,2,8,128,128]{4,3,2,1,0:T(8,128)(2,1)S(1)} copy-done((bf16[1,2,8,128,128]{4,3,2,1,0:T(8,128)(2,1)S(1)}, bf16[1,2,8,128,128]{4,3,2,1,0:T(8,128)(2,1)}, u32[]{:S(2)}) %copy-start) | copy-done | bytes 524312
  9.6 0.4 shard_map.93
  10.0 0.0 collective-permute-done.near_ref
  10.0 1.2 %collective-permute-done.1.far_ref = bf16[2,128,128]{2,1,0:T(8,128)(2,1)S(1)} collective-permute-done((bf16[2,128,128]{2,1,0:T(8,128)(2,1)S(1)}, bf16[2,128,128]{2,1,0:T(8,128)(2,1)S(1)}, u32[]{:S(2)}, u32[]{:S(2)}) %collective-permute-start.1) | collective-permute-done | bytes 65568 | tf_op jit(solution)/shard_map/ppermute | solution.py:331
  11.3 0.0 copy-start.2
  11.3 0.0 copy-start.3
  11.3 0.0 copy-start.5
  11.3 1.4 %shard_map.94 = (f32[2,4,2,128,128]{4,3,2,1,0:T(8,128)S(1)}, bf16[2,4,2,128,128]{4,3,2,1,0:T(8,128)(2,1)S(1)}, bf16[2,128,1280]{2,1,0:T(8,128)(2,1)S(1)}, bf16[2,128,1024]{2,1,0:T(8,128)(2,1)S(1)}) custom-call(bf16[2,8,128,128]{3,2,1,0:T(8,128)(2,1)S(1)} %get-tuple-element.46.x_ref, bf16[2,128,128]{2,1,0:T(8,128)(2,1)S(1)} %collective-permute-done.near_ref, ...), custom_call_target="tpu_custom_call" | custom-call | flops 603979776 | bytes 4000000 | tf_op jit(solution)/shard_map/pallas_call | solution.py:281
  12.7 0.9 %collective-permute-done.2.near_ref = bf16[8,128,128]{2,1,0:T(8,128)(2,1)S(1)} collective-permute-done((bf16[8,128,128]{2,1,0:T(8,128)(2,1)}, bf16[8,128,128]{2,1,0:T(8,128)(2,1)S(1)}, u32[]{:S(2)}, u32[]{:S(2)}) %collective-permute-start.2) | collective-permute-done | bytes 262176 | tf_op jit(solution)/shard_map/ppermute | solution.py:325
  13.6 0.0 collective-permute-done.3.far_ref
  13.6 0.0 copy-done.2
  13.6 0.0 copy-done.3
  13.6 0.0 copy-done.5
  13.6 3.0 %shard_map.95 = (bf16[2,8,128,128]{3,2,1,0:T(8,128)(2,1)S(1)}, bf16[2,128,128]{2,1,0:T(8,128)(2,1)S(1)}, bf16[19,64,128]{2,1,0:T(8,128)(2,1)S(1)}, f32[15,64,128]{2,1,0:T(8,128)S(1)}) custom-call(f32[2,4,2,128,128]{4,3,2,1,0:T(8,128)S(1)} %get-tuple-element.50.slope_ref, bf16[2,128,1280]{2,1,0:T(8,128)(2,1)S(1)} %get-tuple-element.51.xt_ref, ...), custom_call_target="tpu_custom_call" | custom-call | flops 1409286144 | bytes 4000000 | tf_op jit(solution)/shard_map/pallas_call | solution.py:281
  16.6 0.0 copy-start.6
  16.6 1.8 %collective-permute-start.4 = (bf16[19,64,128]{2,1,0:T(8,128)(2,1)S(1)}, bf16[19,64,128]{2,1,0:T(8,128)(2,1)S(1)}, u32[]{:S(2)}, u32[]{:S(2)}) collective-permute-start(bf16[19,64,128]{2,1,0:T(8,128)(2,1)S(1)} %get-tuple-element.54), channel_id=1, source_target_pairs={{0,1},{1,0},{2,3},{3,2},{4,5},{5,4},{6,7},{7,6},{8,9},{9,8},{10,11... | collective-permute-start | bytes 933896 | tf_op jit(solution)/shard_map/ppermute | solution.py:325
  18.4 0.6 shard_map.97
  19.0 0.0 copy-done.6
  19.0 0.6 collective-permute-done.4.got_ref.sent_ref
  19.7 13.3 %all_to_all.15 = bf16[16,64,128]{2,1,0:T(8,128)(2,1)S(1)} all-to-all(bf16[16,64,128]{2,1,0:T(8,128)(2,1)S(1)} %shard_map.96), channel_id=1, replica_groups={{142,140,138,136,134,132,130,128,14,12,10,8,6,4,2,0},{143,141,139,137,1..., dimensions={0} | all-to-all | bytes 524288 | tf_op jit(solution)/shard_map/all_to_all | solution.py:321
  33.0 0.7 %broadcast_in_dim.9 = bf16[8,64,128]{2,1,0:T(8,128)(2,1)} broadcast(bf16[64,128]{1,0:T(8,128)(2,1)S(1)} %reduce_sum.24), dimensions={1,2} | broadcast | bytes 147456 | tf_op jit(solution)/shard_map/broadcast_in_dim | solution.py:374
  33.7 9.9 %all-to-all-start.1 = ((bf16[8,64,128]{2,1,0:T(8,128)(2,1)}), bf16[8,64,128]{2,1,0:T(8,128)(2,1)S(1)}, u32[]{:S(2)}, u32[]{:S(2)}) async-start(bf16[8,64,128]{2,1,0:T(8,128)(2,1)} %broadcast_in_dim.9), calls=%async_computation.1 | async-start | bytes 262144 | tf_op jit(solution)/shard_map/all_to_all | solution.py:321
  43.6 4.2 %collective-permute-start.5 = (bf16[2,128,128]{2,1,0:T(8,128)(2,1)S(1)}, bf16[2,128,128]{2,1,0:T(8,128)(2,1)S(1)}, u32[]{:S(2)}, u32[]{:S(2)}) collective-permute-start(bf16[2,128,128]{2,1,0:T(8,128)(2,1)S(1)} %get-tuple-element.64), channel_id=1, source_target_pairs={{1,2},{3,4},{5,6},{2,1},{4,3},{6,5},{9,10},{11,12},{13,14},{10,9},... | collective-permute-start | bytes 196616 | tf_op jit(solution)/shard_map/ppermute | solution.py:331
  47.8 0.5 collective-permute-start.6
  48.4 0.7 collective-permute-start.7
  49.0 1.0 %collective-permute-done.5.g_far_ref = bf16[2,128,128]{2,1,0:T(8,128)(2,1)S(1)} collective-permute-done((bf16[2,128,128]{2,1,0:T(8,128)(2,1)S(1)}, bf16[2,128,128]{2,1,0:T(8,128)(2,1)S(1)}, u32[]{:S(2)}, u32[]{:S(2)}) %collective-permute-start.5) | collective-permute-done | bytes 65568 | tf_op jit(solution)/shard_map/ppermute | solution.py:331
  50.1 0.0 all-to-all-done.1
  50.1 0.8 %broadcast_in_dim.10 = bf16[16,64,128]{2,1,0:T(8,128)(2,1)} broadcast(bf16[64,128]{1,0:T(8,128)(2,1)S(1)} %reduce_sum.25), dimensions={1,2} | broadcast | bytes 278528 | tf_op jit(solution)/shard_map/broadcast_in_dim | solution.py:378
  50.8 8.1 %all-to-all-start.2 = ((bf16[16,64,128]{2,1,0:T(8,128)(2,1)}), bf16[16,64,128]{2,1,0:T(8,128)(2,1)S(1)}, u32[]{:S(2)}, u32[]{:S(2)}) async-start(bf16[16,64,128]{2,1,0:T(8,128)(2,1)} %broadcast_in_dim.10), calls=%async_computation.2 | async-start | bytes 524288 | tf_op jit(solution)/shard_map/all_to_all | solution.py:321
  59.0 0.0 copy-start.7
  59.0 1.0 %copy-done.7 = bf16[2,8,128,128]{3,2,1,0:T(8,128)(2,1)S(1)} copy-done((bf16[2,8,128,128]{3,2,1,0:T(8,128)(2,1)S(1)}, bf16[2,8,128,128]{3,2,1,0:T(8,128)(2,1)}, u32[]{:S(2)}) %copy-start.7) | copy-done | bytes 524312
  60.0 0.0 copy-start.1
  60.0 2.1 %shard_map.99 = bf16[2,4,2,128,128]{4,3,2,1,0:T(8,128)(2,1)} custom-call(bf16[2,8,128,128]{3,2,1,0:T(8,128)(2,1)S(1)} %copy-done.7, bf16[19,64,128]{2,1,0:T(8,128)(2,1)S(1)} %collective-permute-done.4.got_ref.sent_ref, bf16[2,128,128]{2,1,0:T(8,128)(2,1)S(1)} %collective-permute-done.5.g_far_ref, bf16[8,128,128]{2,1,0:T(8,128)(2,1)S(1)} %bitcast.17, ...), custom_call_target="tpu_custom_call" | custom-call | flops 738197504 | bytes 4000000 | tf_op jit(solution)/shard_map/pallas_call | solution.py:281
  62.1 0.0 collective-permute-done.6.near_ref
  62.1 0.0 collective-permute-done.7.far_ref
  62.1 0.0 copy-done.1
  62.1 1.6 %shard_map.98 = bf16[8,128,128]{2,1,0:T(8,128)(2,1)} custom-call(bf16[2,8,128,128]{3,2,1,0:T(8,128)(2,1)S(1)} %bitcast.12, bf16[2,8,128,128]{3,2,1,0:T(8,128)(2,1)S(1)} %bitcast.13, bf16[8,128,128]{2,1,0:T(8,128)(2,1)S(1)} %collective-permute-done.6.near_ref, bf16[8,128,128]{2,1,0:T(8,128)(2,1)S(1)} %collective-permute-done.7.far_ref, ...), custom_call_target="tpu_custom_call" | custom-call | flops 335544320 | bytes 4000000 | tf_op jit(solution)/shard_map/pallas_call | solution.py:281
  63.7 0.7 %all-to-all-done.2.half_ref = bf16[16,64,128]{2,1,0:T(8,128)(2,1)S(1)} async-done(((bf16[16,64,128]{2,1,0:T(8,128)(2,1)}), bf16[16,64,128]{2,1,0:T(8,128)(2,1)S(1)}, u32[]{:S(2)}, u32[]{:S(2)}) %all-to-all-start.2) | async-done | bytes 262176 | tf_op jit(solution)/shard_map/all_to_all | solution.py:321
  64.4 0.4 collective-permute-start.8
  64.8 0.8 %shard_map.100 = (f32[9,128,128]{2,1,0:T(8,128)}, f32[3,128,128]{2,1,0:T(8,128)}, f32[3,128,128]{2,1,0:T(8,128)}) custom-call(bf16[16,64,128]{2,1,0:T(8,128)(2,1)S(1)} %all-to-all-done.2.half_ref), custom_call_target="tpu_custom_call" | custom-call | tf_op jit(solution)/shard_map/pallas_call | solution.py:398
  65.7 0.3 collective-permute-done.8.half_ref
  66.0 0.8 %shard_map.101 = (f32[9,128,128]{2,1,0:T(8,128)}, f32[3,128,128]{2,1,0:T(8,128)}, f32[3,128,128]{2,1,0:T(8,128)}) custom-call(bf16[16,64,128]{2,1,0:T(8,128)(2,1)S(1)} %collective-permute-done.8.half_ref, f32[9,128,128]{2,1,0:T(8,128)} %get-tuple-element.73.a, ...), custom_call_target="tpu_custom_call", output_to_operand_aliasing={{0}: (1, {}), {1}: (2, {}), {2}: (3, {})} | custom-call | tf_op jit(solution)/shard_map/pallas_call | solution.py:399
  (4 shorter events, 0.1 us)
Async XLA Ops:
  0.6 7.9 %copy-start.4 = (bf16[3,3,128,128]{3,2,1,0:T(8,128)(2,1)S(1)}, bf16[3,3,128,128]{3,2,1,0:T(8,128)(2,1)}, u32[]{:S(2)}) copy-start(bf16[3,3,128,128]{3,2,1,0:T(8,128)(2,1)} %w_ref.1) | copy-start | bytes 884740
  0.6 12.9 %collective-permute-start.2 = (bf16[8,128,128]{2,1,0:T(8,128)(2,1)}, bf16[8,128,128]{2,1,0:T(8,128)(2,1)S(1)}, u32[]{:S(2)}, u32[]{:S(2)}) collective-permute-start(bf16[8,128,128]{2,1,0:T(8,128)(2,1)} %bitcast.14), channel_id=1, source_target_pairs={{0,8},{8,0},{16,24},{24,16},{32,40},{40,32},{48,56},{56,48},{64,72... | collective-permute-start | bytes 786440 | tf_op jit(solution)/shard_map/ppermute | solution.py:325
  2.9 10.7 %collective-permute-start.3 = (bf16[8,128,128]{2,1,0:T(8,128)(2,1)}, bf16[8,128,128]{2,1,0:T(8,128)(2,1)S(1)}, u32[]{:S(2)}, u32[]{:S(2)}) collective-permute-start(bf16[8,128,128]{2,1,0:T(8,128)(2,1)} %bitcast.15), channel_id=1, source_target_pairs={{8,16},{24,32},{40,48},{56,64},{72,80},{88,96},{104,112},{16,8},{3... | collective-permute-start | bytes 786440 | tf_op jit(solution)/shard_map/ppermute | solution.py:331
  4.5 5.6 %collective-permute-start = (bf16[2,128,128]{2,1,0:T(8,128)(2,1)S(1)}, bf16[2,128,128]{2,1,0:T(8,128)(2,1)S(1)}, u32[]{:S(2)}, u32[]{:S(2)}) collective-permute-start(bf16[2,128,128]{2,1,0:T(8,128)(2,1)S(1)} %get-tuple-element.44), channel_id=1, source_target_pairs={{0,1},{1,0},{2,3},{3,2},{4,5},{5,4},{6,7},{7,6},{8,9},{9,8},{10,11... | collective-permute-start | bytes 196616 | tf_op jit(solution)/shard_map/ppermute | solution.py:325
  5.7 5.6 %collective-permute-start.1 = (bf16[2,128,128]{2,1,0:T(8,128)(2,1)S(1)}, bf16[2,128,128]{2,1,0:T(8,128)(2,1)S(1)}, u32[]{:S(2)}, u32[]{:S(2)}) collective-permute-start(bf16[2,128,128]{2,1,0:T(8,128)(2,1)S(1)} %get-tuple-element.47), channel_id=1, source_target_pairs={{1,2},{3,4},{5,6},{2,1},{4,3},{6,5},{9,10},{11,12},{13,14},{10,9},... | collective-permute-start | bytes 196616 | tf_op jit(solution)/shard_map/ppermute | solution.py:331
  8.5 1.0 %copy-start = (bf16[1,2,8,128,128]{4,3,2,1,0:T(8,128)(2,1)S(1)}, bf16[1,2,8,128,128]{4,3,2,1,0:T(8,128)(2,1)}, u32[]{:S(2)}) copy-start(bf16[1,2,8,128,128]{4,3,2,1,0:T(8,128)(2,1)} %param.5) | copy-start | bytes 1572868
  11.3 2.3 %copy-start.2 = (bf16[3,128,128]{2,1,0:T(8,128)(2,1)S(1)}, bf16[3,128,128]{2,1,0:T(8,128)(2,1)}, u32[]{:S(2)}) copy-start(bf16[3,128,128]{2,1,0:T(8,128)(2,1)} %wt_ref.5) | copy-start | bytes 294916
  11.3 2.3 %copy-start.3 = (bf16[3,128,128]{2,1,0:T(8,128)(2,1)S(1)}, bf16[3,128,128]{2,1,0:T(8,128)(2,1)}, u32[]{:S(2)}) copy-start(bf16[3,128,128]{2,1,0:T(8,128)(2,1)} %wd_ref.7) | copy-start | bytes 294916
  11.3 2.3 %copy-start.5 = (bf16[1,1,8,128,128]{4,3,2,1,0:T(8,128)(2,1)S(1)}, bf16[1,1,8,128,128]{4,3,2,1,0:T(8,128)(2,1)}, u32[]{:S(2)}) copy-start(bf16[1,1,8,128,128]{4,3,2,1,0:T(8,128)(2,1)} %param.9) | copy-start | bytes 786436
  16.6 2.4 %copy-start.6 = (bf16[2,8,128,128]{3,2,1,0:T(8,128)(2,1)}, bf16[2,8,128,128]{3,2,1,0:T(8,128)(2,1)S(1)}, u32[]{:S(2)}) copy-start(bf16[2,8,128,128]{3,2,1,0:T(8,128)(2,1)S(1)} %get-tuple-element.68.gpre_ref) | copy-start | bytes 1572868
  16.6 3.1 %collective-permute-start.4 = (bf16[19,64,128]{2,1,0:T(8,128)(2,1)S(1)}, bf16[19,64,128]{2,1,0:T(8,128)(2,1)S(1)}, u32[]{:S(2)}, u32[]{:S(2)}) collective-permute-start(bf16[19,64,128]{2,1,0:T(8,128)(2,1)S(1)} %get-tuple-element.54), channel_id=1, source_target_pairs={{0,1},{1,0},{2,3},{3,2},{4,5},{5,4},{6,7},{7,6},{8,9},{9,8},{10,11... | collective-permute-start | bytes 933896 | tf_op jit(solution)/shard_map/ppermute | solution.py:325
  33.7 16.4 %all-to-all-start.1 = ((bf16[8,64,128]{2,1,0:T(8,128)(2,1)}), bf16[8,64,128]{2,1,0:T(8,128)(2,1)S(1)}, u32[]{:S(2)}, u32[]{:S(2)}) async-start(bf16[8,64,128]{2,1,0:T(8,128)(2,1)} %broadcast_in_dim.9), calls=%async_computation.1 | async-start | bytes 262144 | tf_op jit(solution)/shard_map/all_to_all | solution.py:321
  43.6 6.5 %collective-permute-start.5 = (bf16[2,128,128]{2,1,0:T(8,128)(2,1)S(1)}, bf16[2,128,128]{2,1,0:T(8,128)(2,1)S(1)}, u32[]{:S(2)}, u32[]{:S(2)}) collective-permute-start(bf16[2,128,128]{2,1,0:T(8,128)(2,1)S(1)} %get-tuple-element.64), channel_id=1, source_target_pairs={{1,2},{3,4},{5,6},{2,1},{4,3},{6,5},{9,10},{11,12},{13,14},{10,9},... | collective-permute-start | bytes 196616 | tf_op jit(solution)/shard_map/ppermute | solution.py:331
  47.8 14.3 %collective-permute-start.6 = (bf16[8,128,128]{2,1,0:T(8,128)(2,1)S(1)}, bf16[8,128,128]{2,1,0:T(8,128)(2,1)S(1)}, u32[]{:S(2)}, u32[]{:S(2)}) collective-permute-start(bf16[8,128,128]{2,1,0:T(8,128)(2,1)S(1)} %get-tuple-element.66), channel_id=1, source_target_pairs={{0,8},{8,0},{16,24},{24,16},{32,40},{40,32},{48,56},{56,48},{64,72... | collective-permute-start | bytes 786440 | tf_op jit(solution)/shard_map/ppermute | solution.py:325
  48.4 13.8 %collective-permute-start.7 = (bf16[8,128,128]{2,1,0:T(8,128)(2,1)S(1)}, bf16[8,128,128]{2,1,0:T(8,128)(2,1)S(1)}, u32[]{:S(2)}, u32[]{:S(2)}) collective-permute-start(bf16[8,128,128]{2,1,0:T(8,128)(2,1)S(1)} %get-tuple-element.67), channel_id=1, source_target_pairs={{8,16},{24,32},{40,48},{56,64},{72,80},{88,96},{104,112},{16,8},{3... | collective-permute-start | bytes 786440 | tf_op jit(solution)/shard_map/ppermute | solution.py:331
  50.8 13.6 %all-to-all-start.2 = ((bf16[16,64,128]{2,1,0:T(8,128)(2,1)}), bf16[16,64,128]{2,1,0:T(8,128)(2,1)S(1)}, u32[]{:S(2)}, u32[]{:S(2)}) async-start(bf16[16,64,128]{2,1,0:T(8,128)(2,1)} %broadcast_in_dim.10), calls=%async_computation.2 | async-start | bytes 524288 | tf_op jit(solution)/shard_map/all_to_all | solution.py:321
  59.0 1.0 %copy-start.7 = (bf16[2,8,128,128]{3,2,1,0:T(8,128)(2,1)S(1)}, bf16[2,8,128,128]{3,2,1,0:T(8,128)(2,1)}, u32[]{:S(2)}) copy-start(bf16[2,8,128,128]{3,2,1,0:T(8,128)(2,1)} %copy-done.6) | copy-start | bytes 1572868
  60.0 2.1 %copy-start.1 = (bf16[1,2,8,128,128]{4,3,2,1,0:T(8,128)(2,1)S(1)}, bf16[1,2,8,128,128]{4,3,2,1,0:T(8,128)(2,1)}, u32[]{:S(2)}) copy-start(bf16[1,2,8,128,128]{4,3,2,1,0:T(8,128)(2,1)} %param.5) | copy-start | bytes 1572868
  64.4 1.6 %collective-permute-start.8 = (bf16[16,64,128]{2,1,0:T(8,128)(2,1)S(1)}, bf16[16,64,128]{2,1,0:T(8,128)(2,1)S(1)}, u32[]{:S(2)}, u32[]{:S(2)}) collective-permute-start(bf16[16,64,128]{2,1,0:T(8,128)(2,1)S(1)} %all-to-all-done.2.half_ref), channel_id=1, source_target_pairs={{0,1},{1,0},{2,3},{3,2},{4,5},{5,4},{6,7},{7,6},{8,9},{9,8},{10,11... | collective-permute-start | bytes 786440 | tf_op jit(solution)/shard_map/ppermute | solution.py:325
